TPU v7x, 32 devices: a whole 2x2x4 slice. The times are simulated.
32 devices in a mesh: groups: 2 (over y), row: 4 (over z), col: 4 (over x, core).
Axes of the slice: x: 2, y: 2, z: 4, core: 2. Of those that a mesh axis runs over, the one named last changes fastest.
Arguments:
- positions: float32 [4096, 3, 128], P(('groups', 'row', 'col')), parts along dimension 0, may hold values from -6 to 6
- normals: float32 [4096, 3, 128], P(('groups', 'row', 'col')), parts along dimension 0, may hold values from -6 to 6
- curvature: float32 [4096, 128], P(('groups', 'row', 'col')), parts along dimension 0, may hold values from 0.5 to 3
- pair_targets: int32 [32, 512], P(('groups', 'row', 'col')), parts along dimension 0, may hold values from 0 to 511, as said below
- pair_sources: int32 [32, 512], P(('groups', 'row', 'col')), parts along dimension 0, may hold values from 0 to 511
- pair_count: int32 [32], P(('groups', 'row', 'col')), parts along dimension 0, may hold values from 64 to 512, as said below
- node_counts: int32 [512, 8], P('groups'), parts along dimension 0, may hold values from 1 to 128, 642 in all within a row
- drop_clusters: int32 [512, 8], P('groups'), parts along dimension 0, may hold values from 0 to 2047, as said below
- drop_owner: int32 [512], P('groups'), parts along dimension 0, may hold values from 0 to 15, as said below
Outputs:
- drop_velocity: float32 [4096, 3, 128], P(('groups', 'row', 'col')), parts along dimension 0
There are 2 independent parts, one for each index of `groups`. A program takes and returns all parts, laid end to end along the dimension named above; each array names one. Nothing has to cross between parts.
Inputs may be any that keep to these rules, and one draw needn't show every extreme that they name: `drop_clusters`: every cluster of 0 to 2047 appears exactly once. Of the 128 clusters of one device, at most 16 belong to drops of any one owner, and this many is reached. `drop_owner`: every device owns exactly 16 drops. `pair_count`: the largest count is reached on some device; list entries past a device's count are not pairs. In each device's list, at most 256 entries have the same value of pair_targets // 128, and every device's list reaches this many for some value. `node_counts`: each drop's counts sum to 642.
All inputs are finite; a program needn't handle non-finite values.
Results may differ from a plain program's by a relative error of at most 0.0003.
Values sent between devices are 32-bit elements; how exact they have to be, the bound alone decides.
No kernel may reach another device: no remote copies, remote signals or barrier semaphores. Data moves between devices by JAX's collectives and lax.ppermute only.
A program may use at most 64 MiB of HBM per device.

v0:
```python
import math

import jax
import jax.numpy as jnp
from jax import lax
from jax.sharding import PartitionSpec as P

pair_block = 32
regular_sq = 0.0025
stokes_scale = 1.0 / (8.0 * math.pi)


def stokeslet(target_pos, source_pos, source_force):
    delta_x = target_pos[:, 0, :, None] - source_pos[:, 0, None, :]
    delta_y = target_pos[:, 1, :, None] - source_pos[:, 1, None, :]
    delta_z = target_pos[:, 2, :, None] - source_pos[:, 2, None, :]
    dist_sq = delta_x * delta_x + delta_y * delta_y + delta_z * delta_z
    inverse = lax.rsqrt(dist_sq + regular_sq)
    weight = inverse * inverse * inverse
    isotropic = (dist_sq + 2.0 * regular_sq) * weight
    force_x = source_force[:, 0, None, :]
    force_y = source_force[:, 1, None, :]
    force_z = source_force[:, 2, None, :]
    project = (delta_x * force_x + delta_y * force_y + delta_z * force_z) * weight
    speed_x = jnp.sum(isotropic * force_x + project * delta_x, axis=2)
    speed_y = jnp.sum(isotropic * force_y + project * delta_y, axis=2)
    speed_z = jnp.sum(isotropic * force_z + project * delta_z, axis=2)
    return stokes_scale * jnp.stack([speed_x, speed_y, speed_z], axis=1)


def per_device(
    positions,
    normals,
    curvature,
    pair_targets,
    pair_sources,
    pair_count,
    node_counts,
    drop_clusters,
    drop_owner,
):
    local_count = positions.shape[0]
    node_slots = positions.shape[2]
    row_size = lax.axis_size("row")
    col_size = lax.axis_size("col")
    device_total = row_size * col_size
    device = lax.axis_index("row") * col_size + lax.axis_index("col")
    capacity = max(2, 2 * local_count // device_total)
    per_drop = drop_clusters.shape[1]
    drops_here = local_count // per_drop
    flat_clusters = drop_clusters.reshape(-1)
    flat_counts = node_counts.reshape(-1)
    entries = flat_clusters.shape[0]
    inverse_map = (
        jnp.zeros((entries,), jnp.int32).at[flat_clusters].set(jnp.arange(entries, dtype=jnp.int32))
    )
    home_entry = lax.dynamic_slice_in_dim(inverse_map, device * local_count, local_count)
    home_counts = flat_counts[home_entry]
    slot_index = jnp.arange(node_slots, dtype=jnp.int32)
    home_live = (slot_index[None, :] < home_counts[:, None]).astype(jnp.float32)
    forces = (curvature * home_live)[:, None, :] * normals
    targets = lax.all_gather(positions, "col", axis=0, tiled=True)
    source_pos, source_force = (
        lax.all_gather(positions, "row", axis=0, tiled=True),
        lax.all_gather(forces, "row", axis=0, tiled=True),
    )
    target_rows = targets.shape[0]
    pair_slots = pair_targets.shape[1]
    valid = jnp.arange(pair_slots, dtype=jnp.int32) < pair_count[0]
    sort_keys = jnp.where(valid, pair_targets[0], target_rows)
    ordering = jnp.argsort(sort_keys, stable=True)
    sorted_targets = sort_keys[ordering]
    sorted_sources = pair_sources[0][ordering]
    first = jnp.sum(sorted_targets < 0)
    beyond = jnp.sum(sorted_targets < 0 + target_rows)
    blocks = (beyond - first + pair_block - 1) // pair_block

    def accumulate(block_number, totals):
        picked = first + block_number * pair_block + jnp.arange(pair_block, dtype=jnp.int32)
        active = picked < beyond
        picked = jnp.minimum(picked, pair_slots - 1)
        target_ids = jnp.minimum(sorted_targets[picked], target_rows - 1)
        source_ids = sorted_sources[picked]
        speeds = stokeslet(targets[target_ids], source_pos[source_ids], source_force[source_ids])
        speeds = speeds * active.astype(jnp.float32)[:, None, None]
        offsets = jnp.clip(target_ids - 0, 0, target_rows - 1)
        return totals.at[offsets].add(speeds)

    home_speed = lax.psum_scatter(
        lax.fori_loop(0, blocks, accumulate, jnp.zeros((target_rows, 3, node_slots), jnp.float32)),
        "col",
        scatter_dimension=0,
        tiled=True,
    )
    home_owner = drop_owner[home_entry // per_drop]
    local_order = jnp.arange(local_count, dtype=jnp.int32)
    earlier = (home_owner[None, :] == home_owner[:, None]) & (
        local_order[None, :] < local_order[:, None]
    )
    send_rank = jnp.sum(earlier, axis=1)
    outgoing = jnp.zeros((device_total * capacity, 3, node_slots), jnp.float32)
    outgoing = outgoing.at[home_owner * capacity + send_rank].set(home_speed)
    arrived = lax.all_to_all(outgoing, ("row", "col"), split_axis=0, concat_axis=0, tiled=True)
    owner_order = jnp.argsort(drop_owner, stable=True)
    owned = lax.dynamic_slice_in_dim(owner_order, device * drops_here, drops_here)
    owned_clusters = drop_clusters[owned].reshape(-1)
    owned_counts = node_counts[owned].reshape(-1)
    anchor = owned_clusters // local_count
    before = (anchor[None, :] == anchor[:, None]) & (
        owned_clusters[None, :] < owned_clusters[:, None]
    )
    arrive_rank = jnp.sum(before, axis=1)
    owned_live = (slot_index[None, :] < owned_counts[:, None]).astype(jnp.float32)
    return arrived[anchor * capacity + arrive_rank] * owned_live[:, None, :]


def solution(mesh):
    in_specs = (
        P(("groups", "row", "col"), None, None),
        P(("groups", "row", "col"), None, None),
        P(("groups", "row", "col"), None),
        P(("groups", "row", "col"), None),
        P(("groups", "row", "col"), None),
        P(("groups", "row", "col")),
        P("groups", None),
        P("groups", None),
        P("groups"),
    )
    out_specs = P(("groups", "row", "col"), None, None)
    return jax.shard_map(
        per_device, mesh=mesh, in_specs=in_specs, out_specs=out_specs, check_vma=False
    )
```

profile of v0, /device:TPU:0, one launch (start us, length us, event | category | flops | bytes accessed | tf_op | source)
XLA Modules:
  0.0 374.9 jit_solution(6808647549697550242)
XLA Ops:
  7.2 0.7 fusion.24
  7.9 3.8 %sort.34 = (s32[512]{0:T(512)}, s32[512]{0:T(512)S(1)}) sort(s32[512]{0:T(512)S(1)} %fusion.24, s32[512]{0:T(512)S(1)} %iota.36), dimensions={0}, to_apply=%region_2.3 | sort | flops 4608 | bytes 8192 | tf_op jit(solution)/shard_map/jit(argsort)/sort | solution.py:71
  11.7 3.5 gather_fusion.6
  15.2 0.7 convert_reduce_fusion.2
  17.1 10.0 %all_gather.9 = f32[512,3,128]{2,0,1:T(8,128)S(1)} all-gather(f32[128,3,128]{2,0,1:T(8,128)S(1)} %copy-done.3), channel_id=1, replica_groups=mesh['groups'=2,'row'=4,'col'=4] {'col'}, dimensions={0}, use_global_device_ids=true | all-gather | bytes 983040 | tf_op jit(solution)/shard_map/all_gather | solution.py:62
  27.1 19.9 %all_gather.10 = f32[512,3,128]{2,0,1:T(8,128)S(1)} all-gather(f32[128,3,128]{2,0,1:T(8,128)S(1)} %copy-done.3), channel_id=1, replica_groups=mesh['groups'=2,'row'=4,'col'=4] {'row'}, dimensions={0}, use_global_device_ids=true | all-gather | bytes 983040 | tf_op jit(solution)/shard_map/all_gather | solution.py:64
  47.6 8.0 %scatter_custom_fusion.1 = s32[2048]{0:T(1024)S(1)} fusion(s32[2048]{0:T(1024)S(1)} %bitcast.89, s32[2048]{0:T(1024)S(1)} %iota.34, s32[]{:T(128)} %constant.80.clone.1), kind=kCustom, calls=%fused_computation.70 | custom fusion | bytes 8196 | tf_op jit(solution)/shard_map/scatter | solution.py:55
  56.3 1.1 gather_fusion.8
  57.6 18.2 %all_gather.11 = f32[512,3,128]{2,0,1:T(8,128)S(1)} all-gather(f32[128,3,128]{2,0,1:T(8,128)S(1)} %broadcast_multiply_fusion.1), channel_id=1, replica_groups=mesh['groups'=2,'row'=4,'col'=4] {'row'}, dimensions={0}, use_global_device_ids=true | all-gather | bytes 983040 | tf_op jit(solution)/shard_map/all_gather | solution.py:65
  76.4 3.5 gather_fusion.7
  79.9 1.5 copy.42
  82.1 82.1 %while.10 = (s32[]{:T(128)}, f32[512,3,128]{2,1,0:T(4,128)S(1)}, s32[]{:T(128)}, s32[]{:T(128)}, s32[512]{0:T(512)S(1)}, /*index=5*/f32[512,3,128]{2,1,0:T(4,128...) while((s32[]{:T(128)}, f32[512,3,128]{2,1,0:T(4,128)S(1)}, ...), condition=%wide.region_10.11_spmd, body=%wide.region_5.10_spmd.sunk | while | flops 16293508 | bytes 1145625 | solution.py:90
  82.7 0.7 gather_fusion
  84.0 1.8 gather_fusion.4
  85.9 0.7 gather_fusion.1
  87.2 0.6 fusion.40
  88.5 4.7 %fusion.43 = (f32[32,128]{1,0:T(8,128)S(1)}, f32[32,128]{1,0:T(8,128)S(1)}, f32[32,128]{1,0:T(8,128)S(1)}) fusion(f32[32,128]{1,0:T(8,128)} %bitcast.81, f32[32,128]{1,0:T(8,128)S(1)} %bitcast.84, f32[32,128]{1,0:T(8,128)S(1)} %bitcast.78, f32[32,128]{1,0:T(8,128)S(1)} %bitcast.85, f32[32,128]{1,0:T(8,128)S(1)} %bitcast.79, ...), kind=kLoop, calls=%fused_computation.31.clone.1 | loop fusion | flops 16240640 | bytes 196608 | tf_op jit(solution)/shard_map/while/body/reduce_sum | solution.py:25
  93.2 0.6 compare_select_fusion.22
  94.0 1.8 scatter_fusion
  96.4 0.7 gather_fusion
  97.7 1.8 gather_fusion.4
  99.6 0.7 gather_fusion.1
  100.9 0.6 fusion.40
  102.2 4.7 %fusion.43 = (f32[32,128]{1,0:T(8,128)S(1)}, f32[32,128]{1,0:T(8,128)S(1)}, f32[32,128]{1,0:T(8,128)S(1)}) fusion(f32[32,128]{1,0:T(8,128)} %bitcast.81, f32[32,128]{1,0:T(8,128)S(1)} %bitcast.84, f32[32,128]{1,0:T(8,128)S(1)} %bitcast.78, f32[32,128]{1,0:T(8,128)S(1)} %bitcast.85, f32[32,128]{1,0:T(8,128)S(1)} %bitcast.79, ...), kind=kLoop, calls=%fused_computation.31.clone.1 | loop fusion | flops 16240640 | bytes 196608 | tf_op jit(solution)/shard_map/while/body/reduce_sum | solution.py:25
  106.9 0.6 compare_select_fusion.22
  107.7 1.8 scatter_fusion
  110.1 0.7 gather_fusion
  111.4 1.8 gather_fusion.4
  113.2 0.7 gather_fusion.1
  114.6 0.6 fusion.40
  115.9 4.7 %fusion.43 = (f32[32,128]{1,0:T(8,128)S(1)}, f32[32,128]{1,0:T(8,128)S(1)}, f32[32,128]{1,0:T(8,128)S(1)}) fusion(f32[32,128]{1,0:T(8,128)} %bitcast.81, f32[32,128]{1,0:T(8,128)S(1)} %bitcast.84, f32[32,128]{1,0:T(8,128)S(1)} %bitcast.78, f32[32,128]{1,0:T(8,128)S(1)} %bitcast.85, f32[32,128]{1,0:T(8,128)S(1)} %bitcast.79, ...), kind=kLoop, calls=%fused_computation.31.clone.1 | loop fusion | flops 16240640 | bytes 196608 | tf_op jit(solution)/shard_map/while/body/reduce_sum | solution.py:25
  120.6 0.6 compare_select_fusion.22
  121.3 1.8 scatter_fusion
  123.7 0.7 gather_fusion
  125.1 1.8 gather_fusion.4
  126.9 0.7 gather_fusion.1
  128.3 0.6 fusion.40
  129.6 4.7 %fusion.43 = (f32[32,128]{1,0:T(8,128)S(1)}, f32[32,128]{1,0:T(8,128)S(1)}, f32[32,128]{1,0:T(8,128)S(1)}) fusion(f32[32,128]{1,0:T(8,128)} %bitcast.81, f32[32,128]{1,0:T(8,128)S(1)} %bitcast.84, f32[32,128]{1,0:T(8,128)S(1)} %bitcast.78, f32[32,128]{1,0:T(8,128)S(1)} %bitcast.85, f32[32,128]{1,0:T(8,128)S(1)} %bitcast.79, ...), kind=kLoop, calls=%fused_computation.31.clone.1 | loop fusion | flops 16240640 | bytes 196608 | tf_op jit(solution)/shard_map/while/body/reduce_sum | solution.py:25
  135.0 1.8 scatter_fusion
  137.4 0.7 gather_fusion
  138.7 1.8 gather_fusion.4
  140.6 0.7 gather_fusion.1
  142.0 0.6 fusion.40
  143.3 4.7 %fusion.43 = (f32[32,128]{1,0:T(8,128)S(1)}, f32[32,128]{1,0:T(8,128)S(1)}, f32[32,128]{1,0:T(8,128)S(1)}) fusion(f32[32,128]{1,0:T(8,128)} %bitcast.81, f32[32,128]{1,0:T(8,128)S(1)} %bitcast.84, f32[32,128]{1,0:T(8,128)S(1)} %bitcast.78, f32[32,128]{1,0:T(8,128)S(1)} %bitcast.85, f32[32,128]{1,0:T(8,128)S(1)} %bitcast.79, ...), kind=kLoop, calls=%fused_computation.31.clone.1 | loop fusion | flops 16240640 | bytes 196608 | tf_op jit(solution)/shard_map/while/body/reduce_sum | solution.py:25
  148.0 0.6 compare_select_fusion.22
  148.7 1.8 scatter_fusion
  151.1 0.7 gather_fusion
  152.4 1.8 gather_fusion.4
  154.3 0.7 gather_fusion.1
  155.6 0.6 fusion.40
  156.9 4.7 %fusion.43 = (f32[32,128]{1,0:T(8,128)S(1)}, f32[32,128]{1,0:T(8,128)S(1)}, f32[32,128]{1,0:T(8,128)S(1)}) fusion(f32[32,128]{1,0:T(8,128)} %bitcast.81, f32[32,128]{1,0:T(8,128)S(1)} %bitcast.84, f32[32,128]{1,0:T(8,128)S(1)} %bitcast.78, f32[32,128]{1,0:T(8,128)S(1)} %bitcast.85, f32[32,128]{1,0:T(8,128)S(1)} %bitcast.79, ...), kind=kLoop, calls=%fused_computation.31.clone.1 | loop fusion | flops 16240640 | bytes 196608 | tf_op jit(solution)/shard_map/while/body/reduce_sum | solution.py:25
  161.6 0.6 compare_select_fusion.22
  162.4 1.8 scatter_fusion
  164.2 1.0 copy-done.2
  165.3 3.2 sort.35
  168.5 1.4 gather_fusion.5
  172.0 160.5 %all-reduce.3.cloned.1.call-done = f32[512,3,128]{2,1,0:T(4,128)} async-done(((f32[512,3,128]{2,1,0:T(4,128)}), f32[512,3,128]{2,1,0:T(4,128)}) %all-reduce.3.cloned.1.call-update) | async-done | bytes 786448
  332.5 1.0 constant_dynamic-slice_fusion
  333.5 0.9 broadcast_in_dim.16
  334.4 12.5 %scatter_fusion.1 = f32[256,3,128]{2,1,0:T(4,128)} fusion(f32[256,3,128]{2,1,0:T(4,128)} %broadcast_in_dim.16, s32[128]{0:T(128)S(1)} %fusion.25, f32[128,3,128]{2,1,0:T(4,128)S(1)} %constant_dynamic-slice_fusion), kind=kCustom, calls=%fused_computation.14 | custom fusion | bytes 590336 | tf_op jit(solution)/shard_map/scatter | solution.py:102
  346.9 5.1 %all-to-all-start = ((f32[256,3,128]{2,1,0:T(4,128)}), f32[256,3,128]{2,1,0:T(4,128)S(1)}, u32[]{:S(2)}, u32[]{:S(2)}) async-start(f32[256,3,128]{2,1,0:T(4,128)} %scatter_fusion.1), calls=%async_computation | async-start | bytes 1048576 | tf_op jit(solution)/shard_map/all_to_all | solution.py:103
  353.1 13.4 %all-to-all-done = f32[256,3,128]{2,1,0:T(4,128)S(1)} async-done(((f32[256,3,128]{2,1,0:T(4,128)}), f32[256,3,128]{2,1,0:T(4,128)S(1)}, u32[]{:S(2)}, u32[]{:S(2)}) %all-to-all-start) | async-done | bytes 393248 | tf_op jit(solution)/shard_map/all_to_all | solution.py:103
  366.5 0.8 gather_fusion.10
  367.3 0.7 copy.47
  (125 shorter events, 18.0 us)
Async XLA Ops:
  6.5 69.8 %copy-start = (s32[1,512]{1,0:T(1,128)S(1)}, s32[1,512]{1,0:T(1,128)}, u32[]{:S(2)}) copy-start(s32[1,512]{1,0:T(1,128)} %param.15) | copy-start | bytes 6148
  6.5 326.0 %all-reduce.3.cloned.1.call-start = ((), (), s32[]{:S(2)}) async-start(), calls=%async_computation.1 | async-start | bytes 2097152
  11.7 5.4 %copy-start.3 = (f32[128,3,128]{2,0,1:T(8,128)S(1)}, f32[128,3,128]{2,0,1:T(8,128)}, u32[]{:S(2)}) copy-start(f32[128,3,128]{2,0,1:T(8,128)} %param.11) | copy-start | bytes 589828
  15.2 31.9 %copy-start.6 = (s32[256,8]{0,1:T(8,128)S(1)}, s32[256,8]{0,1:T(8,128)}, u32[]{:S(2)}) copy-start(s32[256,8]{0,1:T(8,128)} %param.18) | copy-start | bytes 24580
  17.1 30.3 %copy-start.7 = (s32[256,8]{0,1:T(8,128)S(1)}, s32[256,8]{0,1:T(8,128)}, u32[]{:S(2)}) copy-start(s32[256,8]{0,1:T(8,128)} %param.17) | copy-start | bytes 24580
  27.1 30.4 %copy-start.5 = (f32[128,128]{1,0:T(8,128)S(1)}, f32[128,128]{1,0:T(8,128)}, u32[]{:S(2)}) copy-start(f32[128,128]{1,0:T(8,128)} %param.13) | copy-start | bytes 196612
  27.1 30.5 %copy-start.4 = (f32[128,3,128]{2,0,1:T(8,128)S(1)}, f32[128,3,128]{2,0,1:T(8,128)}, u32[]{:S(2)}) copy-start(f32[128,3,128]{2,0,1:T(8,128)} %param.12) | copy-start | bytes 589828
  164.2 1.0 copy-start.2
  164.2 1.1 copy-start.1
  164.2 6.4 %copy-start.8 = (u32[32]{0:T(128)S(1)}, u32[32]{0:T(128)}, u32[]{:S(2)}) copy-start(u32[32]{0:T(128)} %constant.101) | copy-start | bytes 388
  346.9 19.6 %all-to-all-start = ((f32[256,3,128]{2,1,0:T(4,128)}), f32[256,3,128]{2,1,0:T(4,128)S(1)}, u32[]{:S(2)}, u32[]{:S(2)}) async-start(f32[256,3,128]{2,1,0:T(4,128)} %scatter_fusion.1), calls=%async_computation | async-start | bytes 1048576 | tf_op jit(solution)/shard_map/all_to_all | solution.py:103
Sparse Core Ops, SparseCore 0:
  165.4 167.1 all-reduce.2
where the time goes:
time: 378 us; the launch traced here: 375 us
  waiting for transfers between devices  174 us (46%)
  local copies, waits for them, and re-layouts  70.9 us (19%)
  other arithmetic  56.6 us (15%)
  blocking collectives  48.1 us (13%)
  between operations  16.2 us (4%)
  starting transfers between devices  5.14 us (1%)
  loops' own time  3.85 us (1%)
    unnamed x2, waiting for transfers between devices  161 us
    reduce_sum x6, other arithmetic, stokeslet(): speed_x = jnp.sum(isotropic * force_x + project * delta_x, axis=2)  28.2 us
    all_gather x1, blocking collectives, per_device(): lax.all_gather(positions, 'row', axis=0, tiled=True)  19.9 us
    all_gather x1, blocking collectives, per_device(): lax.all_gather(forces, 'row', axis=0, tiled=True)  18.2 us
    all_to_all x1, waiting for transfers between devices, per_device(): lax.all_to_all(outgoing, ('row', 'col'), split_axis=0, concat_axis=0, til...  13.4 us
    scatter x1, local copies, waits for them, and re-layouts, per_device(): outgoing = outgoing.at[home_owner * capacity + send_rank].set(home_speed)  12.5 us
    gather x6, local copies, waits for them, and re-layouts, accumulate(): targets[target_ids]  11 us
    scatter-add x6, other arithmetic, accumulate(): return totals.at[offsets].add(speeds)  10.7 us
  transfers between devices with their start and end apart: 2, of which 2 were waited for; matrix products, arithmetic and copies ran while one was open for 2% of the time, Pallas kernels for 0%

commit v1 on v0

v1 whole, which is shorter than its diff:
```python
import functools
import math

import jax
import jax.numpy as jnp
from jax import lax
from jax.experimental import pallas as pl
from jax.experimental.pallas import tpu as pltpu
from jax.sharding import PartitionSpec as P

f32 = jnp.float32
bf16 = jnp.bfloat16
i32 = jnp.int32
regular_sq = 0.0025
length_scale = 1.0 / math.sqrt(regular_sq)
force_scale = length_scale / (8.0 * math.pi)
unroll = 8
vmem_limit = 48 * 2**20
vmem = pl.BlockSpec(memory_space=pltpu.VMEM)
smem = pl.BlockSpec(memory_space=pltpu.SMEM)


def split3(value):
    high = value.astype(bf16)
    rest = value - high.astype(f32)
    mid = rest.astype(bf16)
    low = (rest - mid.astype(f32)).astype(bf16)
    return high.astype(f32), mid.astype(f32), low.astype(f32)


def rows16(upper, lower):
    return jnp.concatenate([upper, lower], axis=0).astype(bf16)


def pair_velocity(slots, target_ref, source_ref, force_ref, target, source):
    row = lax.broadcasted_iota(i32, (8, slots), 0)
    zero = jnp.zeros((8, slots), f32)
    tile = source_ref[pl.ds(pl.multiple_of(source * 8, 8), 8), :]
    high, mid, low = split3(tile)
    left = jnp.concatenate([rows16(high, mid), rows16(low, zero)], axis=0)
    base = (target // slots) * (3 * slots) + target % slots
    columns = []
    for k in range(3):
        coord = jnp.broadcast_to(target_ref[pl.ds(base + slots * k, 1), :], (8, slots))
        x_high, x_mid, x_low = split3(coord)
        minus = jnp.where(row == k, -1.0, 0.0).astype(f32)
        top = jnp.where(row == 3, x_high, jnp.where(row == 4, x_mid, jnp.where(row == 5, x_low, minus)))
        columns.append(jnp.concatenate([rows16(top, minus), rows16(minus, zero)], axis=0))
    right = jnp.concatenate(columns, axis=1)
    delta = lax.dot_general(left, right, (((0,), (0,)), ((), ())), preferred_element_type=f32)
    block = (source // slots) * (3 * slots) + source % slots
    force = [
        jnp.broadcast_to(force_ref[pl.ds(block + slots * k, 1), :], (slots, slots)).T for k in range(3)
    ]
    total = None
    for g in range(slots // 8):
        w = delta[8 * g : 8 * g + 8]
        wx, wy, wz = w[:, :slots], w[:, slots : 2 * slots], w[:, 2 * slots :]
        fx, fy, fz = [part[8 * g : 8 * g + 8] for part in force]
        inverse = lax.rsqrt(wx * wx + wy * wy + (wz * wz + 1.0))
        cube = inverse * inverse * inverse
        isotropic = inverse + cube
        project = (wx * fx + wy * fy + wz * fz) * cube
        terms = (isotropic * fx + project * wx, isotropic * fy + project * wy, isotropic * fz + project * wz)
        total = terms if total is None else tuple(a + b for a, b in zip(total, terms))
    sums = [jnp.broadcast_to(jnp.sum(part, axis=0, keepdims=True), (8, slots)) for part in total]
    return jnp.where(row == 0, sums[0], jnp.where(row == 1, sums[1], jnp.where(row == 2, sums[2], zero)))


def hop_kernel(slots, hop, blocks, homes, has_input, pairs_ref, bounds_ref, *refs):
    refs = list(refs)
    target_refs = [refs.pop(0) for _ in range(homes)]
    source_refs = [(refs.pop(0), refs.pop(0)) for _ in range(blocks)]
    before_ref = refs.pop(0) if has_input else None
    out_ref, target_ref, source_ref, force_ref, total_ref = refs
    clusters = homes * slots
    for h in range(homes):
        target_ref[3 * slots * h : 3 * slots * (h + 1), :] = target_refs[h][...]
    tiles = source_ref.reshape(blocks * slots, 8, slots)
    for b, (position, force) in enumerate(source_refs):
        for k in range(8):
            if k < 3:
                value = position[slots * k : slots * (k + 1), :]
            else:
                value = jnp.full((slots, slots), 1.0 if k < 6 else 0.0, f32)
            tiles[slots * b : slots * (b + 1), k, :] = value
        force_ref[3 * slots * b : 3 * slots * (b + 1), :] = force[...]
    total_ref[...] = jnp.zeros_like(total_ref)
    start = bounds_ref[hop]
    stop = bounds_ref[hop + 1]
    last = pairs_ref.shape[0] - 1

    def step(i, carry):
        results = []
        for u in range(unroll):
            index = start + i * unroll + u
            packed = pairs_ref[jnp.minimum(index, last)]
            live = index < stop
            target = jnp.where(live, packed & 0xFFFF, 0)
            source = jnp.where(live, packed >> 16, 0)
            result = pair_velocity(slots, target_ref, source_ref, force_ref, target, source)
            results.append((jnp.where(live, target, clusters), result))
        for target, result in results:
            total_ref[pl.ds(pl.multiple_of(target * 8, 8), 8), :] += result
        return carry

    lax.fori_loop(0, (stop - start + unroll - 1) // unroll, step, 0)
    totals = total_ref.reshape(total_ref.shape[0] // 8, 8, slots)
    for h in range(homes):
        for k in range(3):
            rows = slice(slots * (3 * h + k), slots * (3 * h + k + 1))
            value = totals[slots * h : slots * (h + 1), k, :]
            out_ref[rows, :] = value if before_ref is None else value + before_ref[rows, :]


def hop_call(hop, pairs, bounds, targets, sources, before):
    slots = targets[0].shape[1]
    homes, blocks = len(targets), len(sources)
    operands = [pairs, bounds, *targets]
    for position, force in sources:
        operands += [position, force]
    if before is not None:
        operands.append(before)
    return pl.pallas_call(
        functools.partial(hop_kernel, slots, hop, blocks, homes, before is not None),
        out_shape=jax.ShapeDtypeStruct((homes * 3 * slots, slots), f32),
        in_specs=[smem, smem] + [vmem] * (len(operands) - 2),
        out_specs=vmem,
        scratch_shapes=[
            pltpu.VMEM((homes * 3 * slots, slots), f32),
            pltpu.VMEM((blocks * slots * 8, slots), f32),
            pltpu.VMEM((blocks * 3 * slots, slots), f32),
            pltpu.VMEM((homes * slots * 8 + 8, slots), f32),
        ],
        compiler_params=pltpu.CompilerParams(vmem_limit_bytes=vmem_limit),
        cost_estimate=pl.CostEstimate(flops=10**8, bytes_accessed=4 * 10**6, transcendentals=10**6),
        name=f"pairs_hop{hop}",
    )(*operands)


def pack_kernel(slots, capacity, place_ref, *refs):
    *speed_refs, out_ref, speed_ref = refs
    total = speed_refs[0][...]
    for part in speed_refs[1:]:
        total = total + part[...]
    speed_ref[...] = total
    out_ref[...] = jnp.zeros_like(out_ref)

    def step(i, carry):
        for u in range(8):
            cluster = i * 8 + u
            place = place_ref[cluster]
            for k in range(3):
                out_ref[pl.ds(place + capacity * k, 1), :] = speed_ref[pl.ds(cluster + slots * k, 1), :]
        return carry

    lax.fori_loop(0, place_ref.shape[0] // 8, step, 0)


def pack_call(places, speeds, capacity, devices):
    slots = speeds[0].shape[1]
    return pl.pallas_call(
        functools.partial(pack_kernel, places.shape[0], capacity),
        out_shape=jax.ShapeDtypeStruct((devices * capacity * 3, slots), f32),
        in_specs=[smem] + [vmem] * len(speeds),
        out_specs=vmem,
        scratch_shapes=[pltpu.VMEM(speeds[0].shape, f32)],
        compiler_params=pltpu.CompilerParams(vmem_limit_bytes=vmem_limit),
        name="pack_owners",
    )(places, *speeds)


def unpack_kernel(capacity, place_ref, count_ref, arrived_ref, out_ref):
    slots = arrived_ref.shape[1]
    lane = lax.broadcasted_iota(i32, (1, slots), 1)

    def step(i, carry):
        for u in range(8):
            cluster = i * 8 + u
            place = place_ref[cluster]
            live = lane < count_ref[cluster]
            for k in range(3):
                value = arrived_ref[pl.ds(place + capacity * k, 1), :]
                out_ref[cluster, k : k + 1, :] = jnp.where(live, value, 0.0)
        return carry

    lax.fori_loop(0, place_ref.shape[0] // 8, step, 0)


def unpack_call(places, counts, arrived, capacity):
    slots = arrived.shape[1]
    return pl.pallas_call(
        functools.partial(unpack_kernel, capacity),
        out_shape=jax.ShapeDtypeStruct((places.shape[0], 3, slots), f32),
        in_specs=[smem, smem, vmem],
        out_specs=vmem,
        compiler_params=pltpu.CompilerParams(vmem_limit_bytes=vmem_limit),
        name="unpack_drops",
    )(places, counts, arrived)


def per_device(
    positions,
    normals,
    curvature,
    pair_targets,
    pair_sources,
    pair_count,
    node_counts,
    drop_clusters,
    drop_owner,
):
    local_count = positions.shape[0]
    slots = positions.shape[2]
    rows = lax.axis_size("row")
    cols = lax.axis_size("col")
    devices = rows * cols
    my_row = lax.axis_index("row")
    my_col = lax.axis_index("col")
    device = my_row * cols + my_col
    capacity = max(2, 2 * local_count // devices)
    per_drop = drop_clusters.shape[1]
    drops = drop_clusters.shape[0]
    drops_here = local_count // per_drop
    hypercube = cols == 4

    def swap(value, bit):
        return lax.ppermute(value, "col", [(c, c ^ bit) for c in range(cols)])

    position = (jnp.transpose(positions, (1, 0, 2)) * length_scale).reshape(3 * local_count, slots)

    to_right = [(r, r + 1) for r in range(rows - 1)]
    to_left = [(r + 1, r) for r in range(rows - 1)]
    right_position = lax.ppermute(position, "row", to_right)
    left_position = lax.ppermute(position, "row", to_left)

    if hypercube:
        core_mate = swap(position, 1)
        chip_mate = swap(position, 2)
        targets = [position, core_mate, chip_mate, swap(chip_mate, 1)]
    else:
        gathered = lax.all_gather(position, "col", axis=0, tiled=True)
        targets = [gathered[3 * local_count * h : 3 * local_count * (h + 1)] for h in range(cols)]

    flat_clusters = drop_clusters.reshape(-1)
    flat_facts = (node_counts + (drop_owner[:, None] << 16)).reshape(-1)
    mine = device * local_count + jnp.arange(local_count, dtype=i32)
    home_facts = jnp.sum(
        jnp.where(flat_clusters[:, None] == mine[None, :], flat_facts[:, None], 0), axis=0
    )
    home_counts = home_facts & 0xFFFF
    home_owner = home_facts >> 16
    slot_index = jnp.arange(slots, dtype=i32)
    strength = jnp.where(slot_index[None, :] < home_counts[:, None], curvature * force_scale, 0.0)
    force = (jnp.transpose(normals, (1, 0, 2)) * strength[None]).reshape(3 * local_count, slots)

    right_force = lax.ppermute(force, "row", to_right)
    left_force = lax.ppermute(force, "row", to_left)

    pair_slots = pair_targets.shape[1]
    entry = jnp.arange(pair_slots, dtype=i32)
    source_row = pair_sources[0] // local_count
    distance = jnp.abs(source_row - my_row)
    key = jnp.where(entry < pair_count[0], distance, rows)
    home = pair_targets[0] // local_count
    home = home ^ my_col if hypercube else home
    target = home * local_count + pair_targets[0] % local_count
    side = jnp.where(source_row > my_row, local_count, 0)
    packed = target | ((side + pair_sources[0] % local_count) << 16)
    ahead = (key[None, :] < key[:, None]) | ((key[None, :] == key[:, None]) & (entry[None, :] < entry[:, None]))
    place = jnp.sum(ahead.astype(i32), axis=1)
    pairs = jnp.sum(jnp.where(place[:, None] == entry[None, :], packed[:, None], 0), axis=0)
    bounds = jnp.sum((key[None, :] < jnp.arange(rows + 1, dtype=i32)[:, None]).astype(i32), axis=1)

    speed = hop_call(0, pairs, bounds, targets, [(position, force)], None)
    for hop in range(1, rows):
        if hop + 1 < rows:
            next_position = (
                lax.ppermute(right_position, "row", to_right),
                lax.ppermute(left_position, "row", to_left),
            )
            next_force = (
                lax.ppermute(right_force, "row", to_right),
                lax.ppermute(left_force, "row", to_left),
            )
        speed = hop_call(
            hop, pairs, bounds, targets, [(right_position, right_force), (left_position, left_force)], speed
        )
        if hop + 1 < rows:
            right_position, left_position = next_position
            right_force, left_force = next_force

    block = 3 * local_count
    if hypercube:
        parts = [speed[block * h : block * (h + 1)] for h in range(4)]
        from_mate = swap(jnp.concatenate([parts[1], parts[3]], axis=0), 1)
        across = swap(parts[2] + from_mate[block:], 2)
        home_speed = [parts[0], from_mate[:block], across]
    else:
        home_speed = [lax.psum_scatter(speed, "col", scatter_dimension=0, tiled=True)]

    local = jnp.arange(local_count, dtype=i32)
    earlier = (home_owner[None, :] == home_owner[:, None]) & (local[None, :] < local[:, None])
    send_rank = jnp.sum(earlier.astype(i32), axis=1)
    outgoing = pack_call(home_owner * (3 * capacity) + send_rank, home_speed, capacity, devices)
    arrived = lax.all_to_all(outgoing, ("row", "col"), split_axis=0, concat_axis=0, tiled=True)

    owned = drop_owner == device
    drop_index = jnp.arange(drops, dtype=i32)
    order = jnp.sum((owned[None, :] & (drop_index[None, :] < drop_index[:, None])).astype(i32), axis=1)
    chosen = owned[None, :] & (order[None, :] == jnp.arange(drops_here, dtype=i32)[:, None])
    drop_facts = drop_clusters | (node_counts << 16)
    owned_facts = jnp.sum(jnp.where(chosen[:, :, None], drop_facts[None], 0), axis=1).reshape(-1)
    owned_clusters = owned_facts & 0xFFFF
    owned_counts = owned_facts >> 16
    anchor = owned_clusters // local_count
    before = (anchor[None, :] == anchor[:, None]) & (owned_clusters[None, :] < owned_clusters[:, None])
    arrive_rank = jnp.sum(before.astype(i32), axis=1)
    return unpack_call(anchor * (3 * capacity) + arrive_rank, owned_counts, arrived, capacity)


def solution(mesh):
    in_specs = (
        P(("groups", "row", "col"), None, None),
        P(("groups", "row", "col"), None, None),
        P(("groups", "row", "col"), None),
        P(("groups", "row", "col"), None),
        P(("groups", "row", "col"), None),
        P(("groups", "row", "col")),
        P("groups", None),
        P("groups", None),
        P("groups"),
    )
    out_specs = P(("groups", "row", "col"), None, None)
    return jax.shard_map(
        per_device, mesh=mesh, in_specs=in_specs, out_specs=out_specs, check_vma=False
    )
```

time: 378 us -> 132 us (0.35)
  waiting for transfers between devices: 174 us -> 19.9 us
  starting transfers between devices: 5.14 us -> 84.9 us
  local copies, waits for them, and re-layouts: 70.9 us -> 3.31 us
  other arithmetic: 56.6 us -> 2.97 us
  blocking collectives: 48.1 us -> 0 us
  Pallas kernels: 0 us -> 20 us
  between operations: 16.2 us -> 1.11 us
  loops' own time: 3.85 us -> 0 us
    unnamed x2 -> x0, waiting for transfers between devices: 161 us -> none
    ppermute x0 -> x17, starting transfers between devices: none -> 50.7 us  [the longest x5 15 us: swap(): return lax.ppermute(value, 'col', [(c, c ^ bit) for c in range(cols)])]
    all_gather x3 -> x0, blocking collectives: 48.1 us -> none  [the longest x1 19.9 us: per_device(): lax.all_gather(positions, 'row', axis=0, tiled=True)]
    gather x37 -> x0, local copies, waits for them, and re-layouts: 38.2 us -> none  [the longest x6 11 us: accumulate(): targets[target_ids]]
    all_to_all x1, starting transfers between devices: 5.14 us -> 34.2 us  [per_device(): lax.all_to_all(outgoing, ('row', 'col'), split_axis=0, concat_axis=0, til...]
    reduce_sum x9 -> x8, other arithmetic: 29.2 us -> 2.67 us  [the longest x1 1.2 us: per_device(): jnp.sum(jnp.where(flat_clusters[:, None] == mine[None, :], flat_facts[:,...]
    scatter x2 -> x0, local copies, waits for them, and re-layouts: 20.5 us -> none  [the longest x1 12.5 us: per_device(): outgoing = outgoing.at[home_owner * capacity + send_rank].set(home_speed)]
    pallas_call x0 -> x6, Pallas kernels: none -> 20 us  [the longest x4 17.6 us: hop_call(): pl.pallas_call(functools.partial(hop_kernel, slots, hop, blocks, homes, b...]
  transfers between devices with their start and end apart: 2 -> 18, of which waited for: 2 -> 3; matrix products, arithmetic and copies ran while one was open for 2% -> 1% of each run, Pallas kernels for 0% -> 10%
where the time goes in v1:
time: 132 us
  starting transfers between devices  84.9 us (64%)
  Pallas kernels  20 us (15%)
  waiting for transfers between devices  19.9 us (15%)
  local copies, waits for them, and re-layouts  3.31 us (3%)
  other arithmetic  2.97 us (2%)
    all_to_all x1, starting transfers between devices, per_device(): lax.all_to_all(outgoing, ('row', 'col'), split_axis=0, concat_axis=0, til...  34.2 us
    pallas_call x4, Pallas kernels, hop_call(): pl.pallas_call(functools.partial(hop_kernel, slots, hop, blocks, homes, b...  17.6 us
    ppermute x5, starting transfers between devices, swap(): return lax.ppermute(value, 'col', [(c, c ^ bit) for c in range(cols)])  15 us
    all_to_all x1, waiting for transfers between devices, per_device(): lax.all_to_all(outgoing, ('row', 'col'), split_axis=0, concat_axis=0, til...  11.8 us
    ppermute x2, starting transfers between devices, per_device(): lax.ppermute(right_force, 'row', to_right)  9.74 us
    ppermute x2, starting transfers between devices, per_device(): lax.ppermute(right_position, 'row', to_right)  9.12 us
    ppermute x5, waiting for transfers between devices, swap(): return lax.ppermute(value, 'col', [(c, c ^ bit) for c in range(cols)])  8.03 us
    ppermute x1, starting transfers between devices, per_device(): right_force = lax.ppermute(force, 'row', to_right)  5.57 us
  transfers between devices with their start and end apart: 18, of which 3 were waited for; matrix products, arithmetic and copies ran while one was open for 1% of the time, Pallas kernels for 10%

profile of v1, /device:TPU:0, one launch (start us, length us, event | category | flops | bytes accessed | tf_op | source)
XLA Modules:
  0.0 132.2 jit_solution(13073260147350177364)
XLA Ops:
  0.0 0.7 copy-done.6
  0.7 0.1 copy.16
  0.8 0.6 copy-done.5
  1.4 0.1 copy.17
  1.5 0.0 copy-start
  1.5 0.1 broadcast_in_dim.56
  1.7 0.0 copy-start.2
  1.7 0.1 eq.95
  1.8 1.2 select_reduce_fusion.1
  3.0 0.2 convert_reduce_fusion.2
  3.2 0.1 multiply_select_fusion
  3.3 0.0 copy-start.1
  3.3 1.4 %collective-permute-start.12 = (f32[384,128]{1,0:T(8,128)S(1)}, f32[384,128]{1,0:T(8,128)S(1)}, u32[]{:S(2)}, u32[]{:S(2)}) collective-permute-start(f32[384,128]{1,0:T(8,128)S(1)} %bitcast.24), channel_id=1, source_target_pairs={{4,0},{8,4},{12,8},{5,1},{9,5},{13,9},{6,2},{10,6},{14,10},{7,3},{... | collective-permute-start | bytes 589832 | tf_op jit(solution)/shard_map/ppermute | solution.py:258
  4.8 5.6 %collective-permute-start.6 = (f32[384,128]{1,0:T(8,128)S(1)}, f32[384,128]{1,0:T(8,128)S(1)}, u32[]{:S(2)}, u32[]{:S(2)}) collective-permute-start(f32[384,128]{1,0:T(8,128)S(1)} %bitcast.25), channel_id=1, source_target_pairs={{0,4},{4,8},{8,12},{1,5},{5,9},{9,13},{2,6},{6,10},{10,14},{3,7},{... | collective-permute-start | bytes 589832 | tf_op jit(solution)/shard_map/ppermute | solution.py:257
  10.4 2.0 %collective-permute-start.1 = (f32[384,128]{1,0:T(8,128)S(1)}, f32[384,128]{1,0:T(8,128)S(1)}, u32[]{:S(2)}, u32[]{:S(2)}) collective-permute-start(f32[384,128]{1,0:T(8,128)S(1)} %bitcast.14), channel_id=1, source_target_pairs={{0,2},{1,3},{2,0},{3,1},{4,6},{5,7},{6,4},{7,5},{8,10},{9,11},{10,... | collective-permute-start | bytes 589832 | tf_op jit(solution)/shard_map/ppermute | solution.py:228
  12.4 3.5 %collective-permute-start.3 = (f32[384,128]{1,0:T(8,128)S(1)}, f32[384,128]{1,0:T(8,128)S(1)}, u32[]{:S(2)}, u32[]{:S(2)}) collective-permute-start(f32[384,128]{1,0:T(8,128)S(1)} %bitcast.15), channel_id=1, source_target_pairs={{0,4},{4,8},{8,12},{1,5},{5,9},{9,13},{2,6},{6,10},{10,14},{3,7},{... | collective-permute-start | bytes 589832 | tf_op jit(solution)/shard_map/ppermute | solution.py:234
  15.8 1.3 collective-permute-start.9
  17.8 0.0 copy-start.7
  17.8 0.0 copy-start.4
  17.8 0.7 copy-done.7
  18.5 0.0 copy-done.4
  18.5 0.0 collective-permute-done.1.refs_2_
  18.5 0.1 collective-permute-start
  18.6 0.0 collective-permute-done.12.refs_7_
  18.6 1.3 collective-permute-start.13
  19.9 0.0 collective-permute-done.6.refs_5_
  19.9 5.2 %collective-permute-start.7 = (f32[384,128]{1,0:T(8,128)S(1)}, f32[384,128]{1,0:T(8,128)S(1)}, u32[]{:S(2)}, u32[]{:S(2)}) collective-permute-start(f32[384,128]{1,0:T(8,128)S(1)} %collective-permute-done.6.refs_5_), channel_id=1, source_target_pairs={{0,4},{4,8},{8,12},{1,5},{5,9},{9,13},{2,6},{6,10},{10,14},{3,7},{... | collective-permute-start | bytes 589832 | tf_op jit(solution)/shard_map/ppermute | solution.py:283
  25.1 0.0 collective-permute-done.9.refs_6_
  25.1 1.3 collective-permute-start.10
  26.4 4.6 %collective-permute-start.4 = (f32[384,128]{1,0:T(8,128)S(1)}, f32[384,128]{1,0:T(8,128)S(1)}, u32[]{:S(2)}, u32[]{:S(2)}) collective-permute-start(f32[384,128]{1,0:T(8,128)S(1)} %collective-permute-done.3.refs_4_), channel_id=1, source_target_pairs={{0,4},{4,8},{8,12},{1,5},{5,9},{9,13},{2,6},{6,10},{10,14},{3,7},{... | collective-permute-start | bytes 589832 | tf_op jit(solution)/shard_map/ppermute | solution.py:279
  31.0 0.3 convert_reduce_fusion
  31.3 0.0 collective-permute-done.refs_1_
  31.3 0.1 collective-permute-start.2
  31.4 1.3 collective-permute-start.14
  32.7 0.0 collective-permute-done.7.refs_5_
  32.7 4.6 %collective-permute-start.8 = (f32[384,128]{1,0:T(8,128)S(1)}, f32[384,128]{1,0:T(8,128)S(1)}, u32[]{:S(2)}, u32[]{:S(2)}) collective-permute-start(f32[384,128]{1,0:T(8,128)S(1)} %collective-permute-done.7.refs_5_), channel_id=1, source_target_pairs={{0,4},{4,8},{8,12},{1,5},{5,9},{9,13},{2,6},{6,10},{10,14},{3,7},{... | collective-permute-start | bytes 589832 | tf_op jit(solution)/shard_map/ppermute | solution.py:283
  37.3 0.0 collective-permute-done.10.refs_6_
  37.3 1.3 collective-permute-start.11
  38.6 0.0 collective-permute-done.4.refs_4_
  38.6 4.6 %collective-permute-start.5 = (f32[384,128]{1,0:T(8,128)S(1)}, f32[384,128]{1,0:T(8,128)S(1)}, u32[]{:S(2)}, u32[]{:S(2)}) collective-permute-start(f32[384,128]{1,0:T(8,128)S(1)} %collective-permute-done.4.refs_4_), channel_id=1, source_target_pairs={{0,4},{4,8},{8,12},{1,5},{5,9},{9,13},{2,6},{6,10},{10,14},{3,7},{... | collective-permute-start | bytes 589832 | tf_op jit(solution)/shard_map/ppermute | solution.py:279
  43.2 0.1 convert_reduce_fusion.4.bounds_ref
  43.3 0.2 select_reduce_fusion.pairs_ref
  43.5 0.0 collective-permute-done.2.refs_3_
  43.5 4.7 %pairs_hop0.1.refs_8_ = f32[1536,128]{1,0:T(8,128)S(1)} custom-call(s32[512]{0:T(512)S(1)} %select_reduce_fusion.pairs_ref, s32[5]{0:T(128)S(1)} %convert_reduce_fusion.4.bounds_ref, f32[384,128]{1,0:T(8,128)S(1)} %bitcast.18, f32[384,128]{1,0:T(8,128)S(1)} %collective-permute-done.refs_1_, f32[384,128]{1,0:T(8,128)S(1)} %collective-permute-done.1.refs_2_, ...), custom_call_target="tpu_custom_call" | custom-call | flops 100000000 | bytes 4000000 | tf_op jit(solution)/shard_map/pairs_hop0/pallas_call | solution.py:124
  48.3 4.3 %pairs_hop1.1.refs_8_ = f32[1536,128]{1,0:T(8,128)S(1)} custom-call(s32[512]{0:T(512)S(1)} %select_reduce_fusion.pairs_ref, s32[5]{0:T(128)S(1)} %convert_reduce_fusion.4.bounds_ref, f32[384,128]{1,0:T(8,128)S(1)} %bitcast.20, f32[384,128]{1,0:T(8,128)S(1)} %collective-permute-done.refs_1_, f32[384,128]{1,0:T(8,128)S(1)} %collective-permute-done.1.refs_2_, ...), custom_call_target="tpu_custom_call" | custom-call | flops 100000000 | bytes 4000000 | tf_op jit(solution)/shard_map/pairs_hop1/pallas_call | solution.py:124
  52.6 4.3 %pairs_hop2.1.refs_8_ = f32[1536,128]{1,0:T(8,128)S(1)} custom-call(s32[512]{0:T(512)S(1)} %select_reduce_fusion.pairs_ref, s32[5]{0:T(128)S(1)} %convert_reduce_fusion.4.bounds_ref, f32[384,128]{1,0:T(8,128)S(1)} %bitcast.21, f32[384,128]{1,0:T(8,128)S(1)} %collective-permute-done.refs_1_, f32[384,128]{1,0:T(8,128)S(1)} %collective-permute-done.1.refs_2_, ...), custom_call_target="tpu_custom_call" | custom-call | flops 100000000 | bytes 4000000 | tf_op jit(solution)/shard_map/pairs_hop2/pallas_call | solution.py:124
  56.9 0.0 collective-permute-done.8.refs_5_
  56.9 0.0 collective-permute-done.11.refs_6_
  56.9 4.3 %pairs_hop3.1 = f32[1536,128]{1,0:T(8,128)S(1)} custom-call(s32[512]{0:T(512)S(1)} %select_reduce_fusion.pairs_ref, s32[5]{0:T(128)S(1)} %convert_reduce_fusion.4.bounds_ref, f32[384,128]{1,0:T(8,128)S(1)} %bitcast.22, f32[384,128]{1,0:T(8,128)S(1)} %collective-permute-done.refs_1_, f32[384,128]{1,0:T(8,128)S(1)} %collective-permute-done.1.refs_2_, ...), custom_call_target="tpu_custom_call" | custom-call | flops 100000000 | bytes 4000000 | tf_op jit(solution)/shard_map/pairs_hop3/pallas_call | solution.py:124
  61.3 12.7 %collective-permute-start.15 = (f32[768,128]{1,0:T(8,128)S(1)}, f32[768,128]{1,0:T(8,128)S(1)}, u32[]{:S(2)}, u32[]{:S(2)}) collective-permute-start(f32[768,128]{1,0:T(8,128)S(1)} %pad_maximum_fusion), channel_id=1, source_target_pairs={{0,1},{1,0},{2,3},{3,2},{4,5},{5,4},{6,7},{7,6},{8,9},{9,8},{10,11... | collective-permute-start | bytes 1179656 | tf_op jit(solution)/shard_map/ppermute | solution.py:228
  74.1 0.1 convert_reduce_fusion.1
  74.2 1.2 collective-permute-done.15
  75.4 0.1 slice_add_fusion
  75.5 0.1 collective-permute-start.16
  75.6 0.3 select_reduce_fusion.2
  75.9 6.8 %collective-permute-done.16.refs_2_ = f32[384,128]{1,0:T(8,128)S(1)} collective-permute-done((f32[384,128]{1,0:T(8,128)S(1)}, f32[384,128]{1,0:T(8,128)S(1)}, u32[]{:S(2)}, u32[]{:S(2)}) %collective-permute-start.16) | collective-permute-done | bytes 196640 | tf_op jit(solution)/shard_map/ppermute | solution.py:228
  82.7 1.6 %pack_owners.1 = f32[768,128]{1,0:T(8,128)} custom-call(s32[128]{0:T(128)S(1)} %get-tuple-element.17.place_ref, f32[384,128]{1,0:T(8,128)S(1)} %get-tuple-element.6.refs_0_, f32[384,128]{1,0:T(8,128)S(1)} %get-tuple-element.9.refs_1_, f32[384,128]{1,0:T(8,128)S(1)} %collective-permute-done.16.refs_2_), custom_call_target="tpu_custom_call" | custom-call | tf_op jit(solution)/shard_map/pack_owners/pallas_call | solution.py:162
  84.3 34.2 %all-to-all-start = ((f32[16,48,128]{2,1,0:T(8,128)}), f32[16,48,128]{2,1,0:T(8,128)S(1)}, u32[]{:S(2)}, u32[]{:S(2)}) async-start(f32[16,48,128]{2,1,0:T(8,128)} %bitcast.10), calls=%async_computation | async-start | bytes 786432 | tf_op jit(solution)/shard_map/all_to_all | solution.py:306
  118.5 0.1 and.142
  118.6 0.1 shift_right_arithmetic.17.count_ref
  118.7 0.2 convert_reduce_fusion.3
  118.9 11.8 %all-to-all-done = f32[16,48,128]{2,1,0:T(8,128)S(1)} async-done(((f32[16,48,128]{2,1,0:T(8,128)}), f32[16,48,128]{2,1,0:T(8,128)S(1)}, u32[]{:S(2)}, u32[]{:S(2)}) %all-to-all-start) | async-done | bytes 393248 | tf_op jit(solution)/shard_map/all_to_all | solution.py:306
  130.7 0.8 unpack_drops.1
  131.5 0.7 copy.18
  (27 shorter events, 0.2 us)
Async XLA Ops:
  0.0 0.7 copy-start.3
  0.0 0.7 copy-start.6
  0.7 0.7 copy-start.5
  1.5 1.7 %copy-start = (f32[128,3,128]{2,0,1:T(8,128)S(1)}, f32[128,3,128]{2,0,1:T(8,128)}, u32[]{:S(2)}) copy-start(f32[128,3,128]{2,0,1:T(8,128)} %param.10) | copy-start | bytes 589828
  1.7 1.5 %copy-start.2 = (f32[128,128]{1,0:T(8,128)S(1)}, f32[128,128]{1,0:T(8,128)}, u32[]{:S(2)}) copy-start(f32[128,128]{1,0:T(8,128)} %param.11) | copy-start | bytes 196612
  3.3 7.0 %copy-start.1 = (f32[128,3,128]{2,0,1:T(8,128)S(1)}, f32[128,3,128]{2,0,1:T(8,128)}, u32[]{:S(2)}) copy-start(f32[128,3,128]{2,0,1:T(8,128)} %param.9) | copy-start | bytes 589828
  3.3 15.3 %collective-permute-start.12 = (f32[384,128]{1,0:T(8,128)S(1)}, f32[384,128]{1,0:T(8,128)S(1)}, u32[]{:S(2)}, u32[]{:S(2)}) collective-permute-start(f32[384,128]{1,0:T(8,128)S(1)} %bitcast.24), channel_id=1, source_target_pairs={{4,0},{8,4},{12,8},{5,1},{9,5},{13,9},{6,2},{10,6},{14,10},{7,3},{... | collective-permute-start | bytes 589832 | tf_op jit(solution)/shard_map/ppermute | solution.py:258
  4.8 15.2 %collective-permute-start.6 = (f32[384,128]{1,0:T(8,128)S(1)}, f32[384,128]{1,0:T(8,128)S(1)}, u32[]{:S(2)}, u32[]{:S(2)}) collective-permute-start(f32[384,128]{1,0:T(8,128)S(1)} %bitcast.25), channel_id=1, source_target_pairs={{0,4},{4,8},{8,12},{1,5},{5,9},{9,13},{2,6},{6,10},{10,14},{3,7},{... | collective-permute-start | bytes 589832 | tf_op jit(solution)/shard_map/ppermute | solution.py:257
  10.4 8.1 %collective-permute-start.1 = (f32[384,128]{1,0:T(8,128)S(1)}, f32[384,128]{1,0:T(8,128)S(1)}, u32[]{:S(2)}, u32[]{:S(2)}) collective-permute-start(f32[384,128]{1,0:T(8,128)S(1)} %bitcast.14), channel_id=1, source_target_pairs={{0,2},{1,3},{2,0},{3,1},{4,6},{5,7},{6,4},{7,5},{8,10},{9,11},{10,... | collective-permute-start | bytes 589832 | tf_op jit(solution)/shard_map/ppermute | solution.py:228
  12.4 14.1 %collective-permute-start.3 = (f32[384,128]{1,0:T(8,128)S(1)}, f32[384,128]{1,0:T(8,128)S(1)}, u32[]{:S(2)}, u32[]{:S(2)}) collective-permute-start(f32[384,128]{1,0:T(8,128)S(1)} %bitcast.15), channel_id=1, source_target_pairs={{0,4},{4,8},{8,12},{1,5},{5,9},{9,13},{2,6},{6,10},{10,14},{3,7},{... | collective-permute-start | bytes 589832 | tf_op jit(solution)/shard_map/ppermute | solution.py:234
  15.8 9.3 %collective-permute-start.9 = (f32[384,128]{1,0:T(8,128)S(1)}, f32[384,128]{1,0:T(8,128)S(1)}, u32[]{:S(2)}, u32[]{:S(2)}) collective-permute-start(f32[384,128]{1,0:T(8,128)S(1)} %bitcast.16), channel_id=1, source_target_pairs={{4,0},{8,4},{12,8},{5,1},{9,5},{13,9},{6,2},{10,6},{14,10},{7,3},{... | collective-permute-start | bytes 589832 | tf_op jit(solution)/shard_map/ppermute | solution.py:235
  17.8 0.7 copy-start.7
  17.8 0.7 copy-start.4
  18.5 12.8 %collective-permute-start = (f32[384,128]{1,0:T(8,128)S(1)}, f32[384,128]{1,0:T(8,128)S(1)}, u32[]{:S(2)}, u32[]{:S(2)}) collective-permute-start(f32[384,128]{1,0:T(8,128)S(1)} %bitcast.17), channel_id=1, source_target_pairs={{0,1},{1,0},{2,3},{3,2},{4,5},{5,4},{6,7},{7,6},{8,9},{9,8},{10,11... | collective-permute-start | bytes 589832 | tf_op jit(solution)/shard_map/ppermute | solution.py:228
  18.6 12.8 %collective-permute-start.13 = (f32[384,128]{1,0:T(8,128)S(1)}, f32[384,128]{1,0:T(8,128)S(1)}, u32[]{:S(2)}, u32[]{:S(2)}) collective-permute-start(f32[384,128]{1,0:T(8,128)S(1)} %collective-permute-done.12.refs_7_), channel_id=1, source_target_pairs={{4,0},{8,4},{12,8},{5,1},{9,5},{13,9},{6,2},{10,6},{14,10},{7,3},{... | collective-permute-start | bytes 589832 | tf_op jit(solution)/shard_map/ppermute | solution.py:284
  19.9 12.8 %collective-permute-start.7 = (f32[384,128]{1,0:T(8,128)S(1)}, f32[384,128]{1,0:T(8,128)S(1)}, u32[]{:S(2)}, u32[]{:S(2)}) collective-permute-start(f32[384,128]{1,0:T(8,128)S(1)} %collective-permute-done.6.refs_5_), channel_id=1, source_target_pairs={{0,4},{4,8},{8,12},{1,5},{5,9},{9,13},{2,6},{6,10},{10,14},{3,7},{... | collective-permute-start | bytes 589832 | tf_op jit(solution)/shard_map/ppermute | solution.py:283
  25.1 12.2 %collective-permute-start.10 = (f32[384,128]{1,0:T(8,128)S(1)}, f32[384,128]{1,0:T(8,128)S(1)}, u32[]{:S(2)}, u32[]{:S(2)}) collective-permute-start(f32[384,128]{1,0:T(8,128)S(1)} %collective-permute-done.9.refs_6_), channel_id=1, source_target_pairs={{4,0},{8,4},{12,8},{5,1},{9,5},{13,9},{6,2},{10,6},{14,10},{7,3},{... | collective-permute-start | bytes 589832 | tf_op jit(solution)/shard_map/ppermute | solution.py:280
  26.4 12.2 %collective-permute-start.4 = (f32[384,128]{1,0:T(8,128)S(1)}, f32[384,128]{1,0:T(8,128)S(1)}, u32[]{:S(2)}, u32[]{:S(2)}) collective-permute-start(f32[384,128]{1,0:T(8,128)S(1)} %collective-permute-done.3.refs_4_), channel_id=1, source_target_pairs={{0,4},{4,8},{8,12},{1,5},{5,9},{9,13},{2,6},{6,10},{10,14},{3,7},{... | collective-permute-start | bytes 589832 | tf_op jit(solution)/shard_map/ppermute | solution.py:279
  31.3 12.2 %collective-permute-start.2 = (f32[384,128]{1,0:T(8,128)S(1)}, f32[384,128]{1,0:T(8,128)S(1)}, u32[]{:S(2)}, u32[]{:S(2)}) collective-permute-start(f32[384,128]{1,0:T(8,128)S(1)} %collective-permute-done.1.refs_2_), channel_id=1, source_target_pairs={{0,1},{1,0},{2,3},{3,2},{4,5},{5,4},{6,7},{7,6},{8,9},{9,8},{10,11... | collective-permute-start | bytes 589832 | tf_op jit(solution)/shard_map/ppermute | solution.py:228
  31.4 25.4 %collective-permute-start.14 = (f32[384,128]{1,0:T(8,128)S(1)}, f32[384,128]{1,0:T(8,128)S(1)}, u32[]{:S(2)}, u32[]{:S(2)}) collective-permute-start(f32[384,128]{1,0:T(8,128)S(1)} %collective-permute-done.13.refs_7_), channel_id=1, source_target_pairs={{4,0},{8,4},{12,8},{5,1},{9,5},{13,9},{6,2},{10,6},{14,10},{7,3},{... | collective-permute-start | bytes 589832 | tf_op jit(solution)/shard_map/ppermute | solution.py:284
  32.7 24.1 %collective-permute-start.8 = (f32[384,128]{1,0:T(8,128)S(1)}, f32[384,128]{1,0:T(8,128)S(1)}, u32[]{:S(2)}, u32[]{:S(2)}) collective-permute-start(f32[384,128]{1,0:T(8,128)S(1)} %collective-permute-done.7.refs_5_), channel_id=1, source_target_pairs={{0,4},{4,8},{8,12},{1,5},{5,9},{9,13},{2,6},{6,10},{10,14},{3,7},{... | collective-permute-start | bytes 589832 | tf_op jit(solution)/shard_map/ppermute | solution.py:283
  37.3 19.6 %collective-permute-start.11 = (f32[384,128]{1,0:T(8,128)S(1)}, f32[384,128]{1,0:T(8,128)S(1)}, u32[]{:S(2)}, u32[]{:S(2)}) collective-permute-start(f32[384,128]{1,0:T(8,128)S(1)} %collective-permute-done.10.refs_6_), channel_id=1, source_target_pairs={{4,0},{8,4},{12,8},{5,1},{9,5},{13,9},{6,2},{10,6},{14,10},{7,3},{... | collective-permute-start | bytes 589832 | tf_op jit(solution)/shard_map/ppermute | solution.py:280
  38.6 18.3 %collective-permute-start.5 = (f32[384,128]{1,0:T(8,128)S(1)}, f32[384,128]{1,0:T(8,128)S(1)}, u32[]{:S(2)}, u32[]{:S(2)}) collective-permute-start(f32[384,128]{1,0:T(8,128)S(1)} %collective-permute-done.4.refs_4_), channel_id=1, source_target_pairs={{0,4},{4,8},{8,12},{1,5},{5,9},{9,13},{2,6},{6,10},{10,14},{3,7},{... | collective-permute-start | bytes 589832 | tf_op jit(solution)/shard_map/ppermute | solution.py:279
  61.3 14.1 %collective-permute-start.15 = (f32[768,128]{1,0:T(8,128)S(1)}, f32[768,128]{1,0:T(8,128)S(1)}, u32[]{:S(2)}, u32[]{:S(2)}) collective-permute-start(f32[768,128]{1,0:T(8,128)S(1)} %pad_maximum_fusion), channel_id=1, source_target_pairs={{0,1},{1,0},{2,3},{3,2},{4,5},{5,4},{6,7},{7,6},{8,9},{9,8},{10,11... | collective-permute-start | bytes 1179656 | tf_op jit(solution)/shard_map/ppermute | solution.py:228
  75.5 7.2 %collective-permute-start.16 = (f32[384,128]{1,0:T(8,128)S(1)}, f32[384,128]{1,0:T(8,128)S(1)}, u32[]{:S(2)}, u32[]{:S(2)}) collective-permute-start(f32[384,128]{1,0:T(8,128)S(1)} %get-tuple-element.5), channel_id=1, source_target_pairs={{0,2},{1,3},{2,0},{3,1},{4,6},{5,7},{6,4},{7,5},{8,10},{9,11},{10,... | collective-permute-start | bytes 589832 | tf_op jit(solution)/shard_map/ppermute | solution.py:228
  84.3 46.4 %all-to-all-start = ((f32[16,48,128]{2,1,0:T(8,128)}), f32[16,48,128]{2,1,0:T(8,128)S(1)}, u32[]{:S(2)}, u32[]{:S(2)}) async-start(f32[16,48,128]{2,1,0:T(8,128)} %bitcast.10), calls=%async_computation | async-start | bytes 786432 | tf_op jit(solution)/shard_map/all_to_all | solution.py:306

commit v2 on v1

v2 whole, which is shorter than its diff:
```python
import functools
import math

import jax
import jax.numpy as jnp
from jax import lax
from jax.experimental import pallas as pl
from jax.experimental.pallas import tpu as pltpu
from jax.sharding import PartitionSpec as P

f32 = jnp.float32
bf16 = jnp.bfloat16
i32 = jnp.int32
regular_sq = 0.0025
length_scale = 1.0 / math.sqrt(regular_sq)
force_scale = length_scale / (8.0 * math.pi)
unroll = 8
vmem_limit = 24 * 2**20
kernel_flops = 2 * 10**10
vmem = pl.BlockSpec(memory_space=pltpu.VMEM)
smem = pl.BlockSpec(memory_space=pltpu.SMEM)


def split3(value):
    high = value.astype(bf16)
    rest = value - high.astype(f32)
    mid = rest.astype(bf16)
    low = (rest - mid.astype(f32)).astype(bf16)
    return high.astype(f32), mid.astype(f32), low.astype(f32)


def rows16(upper, lower):
    return jnp.concatenate([upper, lower], axis=0).astype(bf16)


def transposed_left(y, f, slots):
    row = lax.broadcasted_iota(i32, (8, slots), 0)
    dot = -(y[0] * f[0] + y[1] * f[1] + y[2] * f[2])
    tile = jnp.where(row == 7, dot, 0.0)
    for k in range(3):
        tile = jnp.where(row == k, y[k], jnp.where(row == 3 + k, f[k], tile))
    high, mid, low = split3(tile)
    first = row < 3
    high_one = jnp.where(first, 1.0, high)
    left = jnp.concatenate(
        [rows16(high, mid), rows16(low, high_one), rows16(high_one, jnp.where(first, 1.0, mid))], axis=0
    )
    return left.T


def products(left, x, slots):
    row = lax.broadcasted_iota(i32, (8, slots), 0)
    zero = jnp.zeros((8, slots), f32)
    tile = jnp.where(row == 7, 1.0, zero)
    for k in range(3):
        tile = jnp.where((row == k) | (row == 3 + k), x[k], tile)
    high, mid, low = split3(tile)
    columns = []
    for k in range(3):
        mine = row == k
        minus = jnp.where(mine, -1.0, zero)
        columns.append(
            [
                rows16(minus, minus),
                rows16(minus, jnp.where(mine, high, 0.0)),
                rows16(jnp.where(mine, mid, 0.0), jnp.where(mine, low, 0.0)),
            ]
        )
    first = row < 3
    high, mid, low = [jnp.where(first, 0.0, part) for part in (high, mid, low)]
    columns.append([rows16(high, high), rows16(high, mid), rows16(low, mid)])
    for k in range(2):
        pick = jnp.where(row == 3 + k, 1.0, zero)
        columns.append([rows16(pick, pick), rows16(pick, zero), rows16(zero, zero)])
    right = jnp.concatenate([jnp.concatenate(column, axis=0) for column in columns], axis=1)
    return lax.dot_general(left, right, (((1,), (0,)), ((), ())), preferred_element_type=f32)


def node_sums(product, force_z, slots):
    row = lax.broadcasted_iota(i32, (8, slots), 0)
    total = None
    for g in range(slots // 8):
        part = product[8 * g : 8 * g + 8]
        wx, wy, wz, dot, fx, fy = [part[:, slots * k : slots * (k + 1)] for k in range(6)]
        fz = force_z[8 * g : 8 * g + 8]
        inverse = lax.rsqrt(wx * wx + wy * wy + (wz * wz + 1.0))
        cube = inverse * inverse * inverse
        isotropic = inverse + cube
        project = dot * cube
        terms = (isotropic * fx + project * wx, isotropic * fy + project * wy, isotropic * fz + project * wz)
        total = terms if total is None else tuple(a + b for a, b in zip(total, terms))
    sums = [jnp.broadcast_to(jnp.sum(part, axis=0, keepdims=True), (8, slots)) for part in total]
    return jnp.where(row == 0, sums[0], jnp.where(row == 1, sums[1], jnp.where(row == 2, sums[2], 0.0)))


def hop_kernel(spec, pairs_ref, *refs):
    n, slots, hop, hops, homes, own, mate, first, last, split = spec
    refs = list(refs)
    if first:
        target_refs = [refs.pop(0) for _ in range(homes)]
    else:
        target_ref, before_ref = refs.pop(0), refs.pop(0)
    own_refs = [refs.pop(0) for _ in range(own)]
    mate_refs = [refs.pop(0) for _ in range(mate)]
    if first:
        total_ref, target_ref = refs.pop(0), refs.pop(0)
    else:
        total_ref = refs.pop(0)
        out_refs = [refs.pop(0) for _ in range((2 if split else 1) if last else 0)]
    source_ref, left_ref = refs
    clusters = homes * n
    shift = n.bit_length() - 1
    if first:
        for h in range(homes):
            target_ref[3 * n * h : 3 * n * (h + 1), :] = target_refs[h][: 3 * n, :]
        total_ref[...] = jnp.zeros_like(total_ref)
    for place, block in list(enumerate(own_refs)) + [(2 + b, block) for b, block in enumerate(mate_refs)]:
        source_ref[6 * n * place : 6 * n * (place + 1), :] = block[...]

    width = pairs_ref.shape[0] // 2
    slots_of = width - 128
    own_start, own_count, mate_start, mate_count = 0, 0, 0, 0
    if own:
        own_start = pairs_ref[slots_of + hop]
        own_count = (pairs_ref[slots_of + hop + 1] - own_start + 1) >> 1
    if mate:
        begin = pairs_ref[width + slots_of + hop - 1]
        end = pairs_ref[width + slots_of + hop]
        mate_start = width + begin + ((end - begin + 1) >> 1)
        mate_count = width + end - mate_start
    count = own_count + mate_count
    mate_start = mate_start - own_count

    def entry(index):
        live = index < count
        index = jnp.where(live, index, 0)
        place = index + jnp.where(index < own_count, own_start, mate_start)
        packed = pairs_ref[jnp.where(live, place, 0)]
        target = jnp.where(live, packed & 0xFFFF, 0)
        source = jnp.where(live, packed >> 16, 0)
        return live, target, source

    def source_rows(source):
        base = source + (source >> shift) * (5 * n)
        return [source_ref[pl.ds(base + n * k, 1), :] for k in range(6)]

    def wide(value):
        return jnp.broadcast_to(value, (8, slots))

    def fetch(index, u):
        _, _, source = entry(index)
        values = [wide(value) for value in source_rows(source)]
        left_ref[u] = transposed_left(values[:3], values[3:], slots)

    @pl.when(count > 0)
    def _():
        for u in range(unroll):
            fetch(u, u)

    def step(i, carry):
        results = []
        lefts = [left_ref[u] for u in range(unroll)]
        for u in range(unroll):
            live, target, source = entry(i * unroll + u)
            base = target + (target >> shift) * (2 * n)
            x = [wide(target_ref[pl.ds(base + n * k, 1), :]) for k in range(3)]
            product = products(lefts[u], x, slots)
            force_z = source_ref[pl.ds(source + (source >> shift) * (5 * n) + 5 * n, 1), :]
            force_z = jnp.broadcast_to(force_z, (slots, slots)).T
            results.append((jnp.where(live, target, clusters), node_sums(product, force_z, slots)))
        for u in range(unroll):
            fetch((i + 1) * unroll + u, u)
        for target, result in results:
            total_ref[pl.ds(pl.multiple_of(target * 8, 8), 8), :] += result
        return carry

    lax.fori_loop(0, (count + unroll - 1) // unroll, step, 0)
    if last:
        totals = total_ref.reshape(total_ref.shape[0] // 8, 8, slots)
        for h in range(homes):
            out_ref = out_refs[h % 2] if split else out_refs[0]
            place = h // 2 if split else h
            for k in range(3):
                rows = slice(n * (3 * place + k), n * (3 * place + k + 1))
                out_ref[rows, :] = totals[n * h : n * (h + 1), k, :]


def hop_call(n, hop, hops, pairs, targets, total, own, mate, split):
    first, last = hop == 0, hop == hops
    slots = own[0].shape[1] if own else mate[0].shape[1]
    homes = len(targets) if first else targets[0].shape[0] // (3 * n)
    total_shape = jax.ShapeDtypeStruct((homes * n * 8 + 8, slots), f32)
    aliases = {}
    operands = [pairs, *targets]
    if not first:
        operands.append(total)
    if first:
        out_shape = [total_shape, jax.ShapeDtypeStruct((homes * 3 * n, slots), f32)]
    elif last:
        parts = 2 if split else 1
        out_shape = [total_shape] + [jax.ShapeDtypeStruct((homes * 3 * n // parts, slots), f32)] * parts
    else:
        out_shape = [total_shape]
    if not first:
        aliases = {len(operands) - 1: 0}
    operands += [*own, *mate]
    spec = (n, slots, hop, hops, homes, len(own), len(mate), first, last, split)
    return pl.pallas_call(
        functools.partial(hop_kernel, spec),
        out_shape=out_shape,
        in_specs=[smem] + [vmem] * (len(operands) - 1),
        out_specs=[vmem] * len(out_shape),
        scratch_shapes=[
            pltpu.VMEM((4 * 6 * n, slots), f32),
            pltpu.VMEM((unroll, slots, 48), bf16),
        ],
        input_output_aliases=aliases,
        compiler_params=pltpu.CompilerParams(vmem_limit_bytes=vmem_limit),
        cost_estimate=pl.CostEstimate(flops=kernel_flops, bytes_accessed=10**6, transcendentals=10**6),
        name=f"pairs_hop{hop}",
    )(*operands)


def prep_kernel(n, base_ref, position_ref, normal_ref, curvature_ref, cluster_ref, count_ref, out_ref, own_ref):
    slots = position_ref.shape[1]
    scaled = position_ref[...] * length_scale
    out_ref[: 3 * n, :] = scaled
    own_ref[...] = scaled
    mine = base_ref[0] + lax.broadcasted_iota(i32, (n, 128), 0)
    total = jnp.zeros((n, 128), f32)
    for k in range(cluster_ref.shape[0]):
        for j in range(cluster_ref.shape[1] // 128):
            part = slice(128 * j, 128 * (j + 1))
            cluster = jnp.broadcast_to(cluster_ref[k : k + 1, part], (n, 128))
            count = jnp.broadcast_to(count_ref[k : k + 1, part].astype(f32), (n, 128))
            total = total + jnp.where(cluster == mine, count, 0.0)
    live_count = jnp.sum(total, axis=1, keepdims=True)
    lane = lax.broadcasted_iota(i32, (n, slots), 1).astype(f32)
    strength = jnp.where(lane < live_count, curvature_ref[...] * force_scale, 0.0)
    for k in range(3):
        out_ref[n * (3 + k) : n * (4 + k), :] = normal_ref[n * k : n * (k + 1), :] * strength


def prep_call(base, position, normal, curvature, clusters, counts):
    n, slots = curvature.shape
    return pl.pallas_call(
        functools.partial(prep_kernel, n),
        out_shape=[jax.ShapeDtypeStruct((6 * n, slots), f32), jax.ShapeDtypeStruct((3 * n, slots), f32)],
        in_specs=[smem] + [vmem] * 5,
        out_specs=[vmem, vmem],
        compiler_params=pltpu.CompilerParams(vmem_limit_bytes=vmem_limit),
        name="prep_sources",
    )(base, position, normal, curvature, clusters, counts)


def pack_kernel(n, capacity, place_ref, *refs):
    *speed_refs, out_ref, speed_ref = refs
    total = speed_refs[0][: 3 * n, :]
    for part in speed_refs[1:]:
        total = total + part[: 3 * n, :]
    speed_ref[...] = total
    out_ref[...] = jnp.zeros_like(out_ref)

    def step(i, carry):
        for u in range(16):
            cluster = i * 16 + u
            place = place_ref[cluster]
            for k in range(3):
                out_ref[pl.ds(place + capacity * k, 1), :] = speed_ref[pl.ds(cluster + n * k, 1), :]
        return carry

    lax.fori_loop(0, n // 16, step, 0)


def pack_call(places, speeds, capacity, devices):
    n = places.shape[0]
    slots = speeds[0].shape[1]
    return pl.pallas_call(
        functools.partial(pack_kernel, n, capacity),
        out_shape=jax.ShapeDtypeStruct((devices * capacity * 3, slots), f32),
        in_specs=[smem] + [vmem] * len(speeds),
        out_specs=vmem,
        scratch_shapes=[pltpu.VMEM((3 * n, slots), f32)],
        compiler_params=pltpu.CompilerParams(vmem_limit_bytes=vmem_limit),
        name="pack_owners",
    )(places, *speeds)


def unpack_kernel(n, capacity, place_ref, count_ref, arrived_ref, out_ref):
    slots = arrived_ref.shape[1]
    lane = lax.broadcasted_iota(i32, (1, slots), 1)

    def step(i, carry):
        for u in range(16):
            cluster = i * 16 + u
            place = place_ref[cluster]
            live = lane < count_ref[cluster]
            for k in range(3):
                value = arrived_ref[pl.ds(place + capacity * k, 1), :]
                out_ref[pl.ds(cluster + n * k, 1), :] = jnp.where(live, value, 0.0)
        return carry

    lax.fori_loop(0, n // 16, step, 0)


def unpack_call(places, counts, arrived, capacity):
    n, slots = places.shape[0], arrived.shape[1]
    return pl.pallas_call(
        functools.partial(unpack_kernel, n, capacity),
        out_shape=jax.ShapeDtypeStruct((3 * n, slots), f32),
        in_specs=[smem, smem, vmem],
        out_specs=vmem,
        compiler_params=pltpu.CompilerParams(vmem_limit_bytes=vmem_limit),
        name="unpack_drops",
    )(places, counts, arrived)


def per_device(
    positions,
    normals,
    curvature,
    pair_targets,
    pair_sources,
    pair_count,
    node_counts,
    drop_clusters,
    drop_owner,
):
    n, slots = curvature.shape
    rows = lax.axis_size("row")
    cols = lax.axis_size("col")
    devices = rows * cols
    my_row = lax.axis_index("row")
    my_col = lax.axis_index("col")
    device = my_row * cols + my_col
    capacity = max(2, 2 * n // devices)
    drops, per_drop = drop_clusters.shape
    drops_here = n // per_drop
    hypercube = cols == 4

    def swap(value, bit):
        return lax.ppermute(value, "col", [(c, c ^ bit) for c in range(cols)])

    def component_major(value):
        return jnp.transpose(value, (1, 0, 2)).reshape(3 * n, slots)

    block, position = prep_call(
        (device * n).reshape(1),
        component_major(positions),
        component_major(normals),
        curvature,
        drop_clusters.T,
        node_counts.T,
    )
    to_right = [(r, r + 1) for r in range(rows - 1)]
    to_left = [(r + 1, r) for r in range(rows - 1)]
    right = lax.ppermute(block, "row", to_right)
    left = lax.ppermute(block, "row", to_left)
    mate_block = swap(block, 1)
    if hypercube:
        across = swap(position, 2)
        targets = [position, mate_block, across, swap(across, 1)]
    else:
        gathered = lax.all_gather(position, "col", axis=0, tiled=True)
        targets = [gathered[3 * n * h : 3 * n * (h + 1)] for h in range(cols)]

    pair_slots = pair_targets.shape[1]
    entry = jnp.arange(pair_slots, dtype=i32)
    source_row = pair_sources[0] // n
    key = jnp.where(entry < pair_count[0], jnp.abs(source_row - my_row), rows)
    home = pair_targets[0] // n
    home = home ^ my_col if hypercube else home
    target = home * n + pair_targets[0] % n
    packed = target | ((jnp.where(source_row > my_row, n, 0) + pair_sources[0] % n) << 16)
    ahead = (key[None, :] < key[:, None]) | ((key[None, :] == key[:, None]) & (entry[None, :] < entry[:, None]))
    place = jnp.sum(ahead.astype(i32), axis=1)
    ordered = jnp.sum(jnp.where(place[:, None] == entry[None, :], packed[:, None], 0), axis=0)
    bounds = jnp.sum((key[None, :] < jnp.arange(128, dtype=i32)[:, None]).astype(i32), axis=1)
    listed = jnp.concatenate([ordered, bounds])
    mate_listed = swap(listed, 1)
    flip = n if hypercube else 0
    mate_pairs = jnp.where(
        jnp.arange(pair_slots + 128) < pair_slots, (mate_listed ^ flip) + ((2 * n) << 16), mate_listed
    )
    pairs = jnp.concatenate([listed, mate_pairs])

    total, all_targets = hop_call(n, 0, rows, pairs, targets, None, [block], [], hypercube)
    mate = [mate_block]
    for hop in range(1, rows):
        right, left, total = lax.optimization_barrier((right, left, total))
        own = [right, left]
        if hop + 1 < rows:
            right = lax.ppermute(right, "row", to_right)
            left = lax.ppermute(left, "row", to_left)
        next_mate = [swap(own[0], 1), swap(own[1], 1)]
        (total,) = hop_call(n, hop, rows, pairs, [all_targets], total, own, mate, hypercube)
        mate = next_mate
    _, *speed = hop_call(n, rows, rows, pairs, [all_targets], total, [], mate, hypercube)

    if hypercube:
        kept, sent = speed
        from_mate = swap(sent, 1)
        across = swap(kept[3 * n :] + from_mate[3 * n :], 2)
        home_speed = [kept, from_mate, across]
    else:
        home_speed = [lax.psum_scatter(speed[0], "col", scatter_dimension=0, tiled=True)]

    flat_clusters = drop_clusters.reshape(-1)
    flat_owner = jnp.broadcast_to(drop_owner[:, None], drop_clusters.shape).reshape(-1)
    local = jnp.arange(n, dtype=i32)
    home_owner = jnp.sum(
        jnp.where(flat_clusters[:, None] == (device * n + local)[None, :], flat_owner[:, None], 0), axis=0
    )
    earlier = (home_owner[None, :] == home_owner[:, None]) & (local[None, :] < local[:, None])
    send_rank = jnp.sum(earlier.astype(i32), axis=1)
    outgoing = pack_call(home_owner * (3 * capacity) + send_rank, home_speed, capacity, devices)
    arrived = lax.all_to_all(outgoing, ("row", "col"), split_axis=0, concat_axis=0, tiled=True)

    owned = drop_owner == device
    drop_index = jnp.arange(drops, dtype=i32)
    order = jnp.sum((owned[None, :] & (drop_index[None, :] < drop_index[:, None])).astype(i32), axis=1)
    chosen = owned[None, :] & (order[None, :] == jnp.arange(drops_here, dtype=i32)[:, None])
    drop_facts = drop_clusters | (node_counts << 16)
    owned_facts = jnp.sum(jnp.where(chosen[:, :, None], drop_facts[None], 0), axis=1).reshape(-1)
    owned_clusters = owned_facts & 0xFFFF
    owned_counts = owned_facts >> 16
    anchor = owned_clusters // n
    before = (anchor[None, :] == anchor[:, None]) & (owned_clusters[None, :] < owned_clusters[:, None])
    arrive_rank = jnp.sum(before.astype(i32), axis=1)
    result = unpack_call(anchor * (3 * capacity) + arrive_rank, owned_counts, arrived, capacity)
    return jnp.transpose(result.reshape(3, n, slots), (1, 0, 2))


def solution(mesh):
    in_specs = (
        P(("groups", "row", "col"), None, None),
        P(("groups", "row", "col"), None, None),
        P(("groups", "row", "col"), None),
        P(("groups", "row", "col"), None),
        P(("groups", "row", "col"), None),
        P(("groups", "row", "col")),
        P("groups", None),
        P("groups", None),
        P("groups"),
    )
    out_specs = P(("groups", "row", "col"), None, None)
    return jax.shard_map(
        per_device, mesh=mesh, in_specs=in_specs, out_specs=out_specs, check_vma=False
    )
```

time: 132 us -> 107 us (0.81); the launches traced: 132 us -> 109 us
  starting transfers between devices: 84.9 us -> 27.9 us
  waiting for transfers between devices: 19.9 us -> 44.1 us
  Pallas kernels: 20 us -> 24.6 us
  local copies, waits for them, and re-layouts: 3.31 us -> 6.07 us
  other arithmetic: 2.97 us -> 4.88 us
    all_to_all x1, starting transfers between devices: 34.2 us -> 7.69 us  [per_device(): lax.all_to_all(outgoing, ('row', 'col'), split_axis=0, concat_axis=0, til...]
    ppermute x12 -> x6, waiting for transfers between devices: 0.03 us -> 21.1 us  [the longest x2 17.2 us: per_device(): left = lax.ppermute(left, 'row', to_left)]
    ppermute x12 -> x6, starting transfers between devices: 35.8 us -> 15.9 us  [the longest x2 7.57 us: per_device(): right = lax.ppermute(right, 'row', to_right)]
    ppermute x5 -> x12, starting transfers between devices: 15 us -> 4.23 us  [swap(): return lax.ppermute(value, 'col', [(c, c ^ bit) for c in range(cols)])]
    pallas_call x6 -> x8, Pallas kernels: 20 us -> 24.6 us  [the longest x5 21.5 us: hop_call(): pl.pallas_call(functools.partial(hop_kernel, spec), out_shape=out_shape,...]
    ppermute x5 -> x12, waiting for transfers between devices: 8.03 us -> 11.2 us  [swap(): return lax.ppermute(value, 'col', [(c, c ^ bit) for c in range(cols)])]
    unnamed x17 -> x15, local copies, waits for them, and re-layouts: 2.08 us -> 4.91 us
  transfers between devices with their start and end apart: 18 -> 19, of which waited for: 3 -> 9; matrix products, arithmetic and copies ran while one was open for 1% -> 6% of each run, Pallas kernels for 10% -> 16%
where the time goes in v2:
time: 107 us; the launch traced here: 109 us
  waiting for transfers between devices  44.1 us (41%)
  starting transfers between devices  27.9 us (26%)
  Pallas kernels  24.6 us (23%)
  local copies, waits for them, and re-layouts  6.07 us (6%)
  other arithmetic  4.88 us (5%)
    pallas_call x5, Pallas kernels, hop_call(): pl.pallas_call(functools.partial(hop_kernel, spec), out_shape=out_shape,...  21.5 us
    ppermute x2, waiting for transfers between devices, per_device(): left = lax.ppermute(left, 'row', to_left)  17.2 us
    all_to_all x1, waiting for transfers between devices, per_device(): lax.all_to_all(outgoing, ('row', 'col'), split_axis=0, concat_axis=0, til...  11.8 us
    ppermute x12, waiting for transfers between devices, swap(): return lax.ppermute(value, 'col', [(c, c ^ bit) for c in range(cols)])  11.2 us
    all_to_all x1, starting transfers between devices, per_device(): lax.all_to_all(outgoing, ('row', 'col'), split_axis=0, concat_axis=0, til...  7.69 us
    ppermute x2, starting transfers between devices, per_device(): right = lax.ppermute(right, 'row', to_right)  7.57 us
    unnamed x15, local copies, waits for them, and re-layouts  4.91 us
    ppermute x1, starting transfers between devices, per_device(): right = lax.ppermute(block, 'row', to_right)  4.51 us
  transfers between devices with their start and end apart: 19, of which 9 were waited for; matrix products, arithmetic and copies ran while one was open for 6% of the time, Pallas kernels for 16%

profile of v2, /device:TPU:0, one launch (start us, length us, event | category | flops | bytes accessed | tf_op | source)
XLA Modules:
  0.0 108.5 jit_solution(6204212648369037752)
XLA Ops:
  0.0 0.9 copy-done
  0.9 0.9 copy-done.1
  1.9 0.7 copy-done.2
  2.6 0.8 copy-done.4
  3.4 0.7 copy-done.5
  4.1 0.2 prep_sources.1
  4.3 0.5 collective-permute-start.1
  4.8 4.5 %collective-permute-start.4 = (f32[768,128]{1,0:T(8,128)S(1)}, f32[768,128]{1,0:T(8,128)S(1)}, u32[]{:S(2)}, u32[]{:S(2)}) collective-permute-start(f32[768,128]{1,0:T(8,128)S(1)} %get-tuple-element.21.refs_4_), channel_id=1, source_target_pairs={{0,4},{4,8},{8,12},{1,5},{5,9},{9,13},{2,6},{6,10},{10,14},{3,7},{... | collective-permute-start | bytes 1179656 | tf_op jit(solution)/shard_map/ppermute | solution.py:357
  9.3 1.3 %collective-permute-start.5 = (f32[768,128]{1,0:T(8,128)S(1)}, f32[768,128]{1,0:T(8,128)S(1)}, u32[]{:S(2)}, u32[]{:S(2)}) collective-permute-start(f32[768,128]{1,0:T(8,128)S(1)} %get-tuple-element.21.refs_4_), channel_id=1, source_target_pairs={{4,0},{8,4},{12,8},{5,1},{9,5},{13,9},{6,2},{10,6},{14,10},{7,3},{... | collective-permute-start | bytes 1179656 | tf_op jit(solution)/shard_map/ppermute | solution.py:358
  11.3 0.7 compare_select_fusion
  12.0 0.1 convert_reduce_fusion.1
  12.1 0.7 abs_select_fusion
  12.8 0.3 convert_reduce_fusion
  13.1 0.2 select_reduce_fusion
  13.4 0.3 collective-permute-start
  13.6 1.5 %collective-permute-start.2 = (f32[384,128]{1,0:T(8,128)S(1)}, f32[384,128]{1,0:T(8,128)S(1)}, u32[]{:S(2)}, u32[]{:S(2)}) collective-permute-start(f32[384,128]{1,0:T(8,128)S(1)} %get-tuple-element.20.refs_0_), channel_id=1, source_target_pairs={{0,2},{1,3},{2,0},{3,1},{4,6},{5,7},{6,4},{7,5},{8,10},{9,11},{10,... | collective-permute-start | bytes 589832 | tf_op jit(solution)/shard_map/ppermute | solution.py:342
  15.1 0.8 copy.17
  15.9 0.7 broadcast_compare_fusion.1
  16.6 0.8 broadcast_in_dim.54
  17.4 0.1 broadcast_in_dim.55
  17.5 0.1 eq.95
  17.6 0.1 convert_reduce_fusion.2
  17.8 1.2 %select_reduce_fusion.1 = s32[128]{0:T(128)S(1)} fusion(s32[2048]{0:T(1024)S(1)} %broadcast_in_dim.55, s32[128]{0:T(128)S(1)} %iota_add_fusion, s32[2048]{0:T(1024)S(1)} %eq.95), kind=kLoop, calls=%fused_computation.4 | loop fusion | flops 786304 | bytes 17408 | tf_op jit(solution)/shard_map/reduce_sum | solution.py:411
  19.0 1.8 %collective-permute-done.2.refs_2_ = f32[384,128]{1,0:T(8,128)S(1)} collective-permute-done((f32[384,128]{1,0:T(8,128)S(1)}, f32[384,128]{1,0:T(8,128)S(1)}, u32[]{:S(2)}, u32[]{:S(2)}) %collective-permute-start.2) | collective-permute-done | bytes 196640 | tf_op jit(solution)/shard_map/ppermute | solution.py:342
  20.7 0.0 collective-permute-start.3
  20.7 0.0 collective-permute-done
  20.8 1.4 %collective-permute-done.3.refs_3_ = f32[384,128]{1,0:T(8,128)S(1)} collective-permute-done((f32[384,128]{1,0:T(8,128)S(1)}, f32[384,128]{1,0:T(8,128)S(1)}, u32[]{:S(2)}, u32[]{:S(2)}) %collective-permute-start.3) | collective-permute-done | bytes 196640 | tf_op jit(solution)/shard_map/ppermute | solution.py:342
  22.2 3.0 %pairs_hop0.1 = (f32[4104,128]{1,0:T(8,128)S(1)}, f32[1536,128]{1,0:T(8,128)S(1)}) custom-call(s32[1280]{0:T(1024)S(1)} %pad_add_fusion.pairs_ref, f32[384,128]{1,0:T(8,128)S(1)} %get-tuple-element.20.refs_0_, f32[768,128]{1,0:T(8,128)S(1)} %collective-permute-done.1.refs_1_.refs_4_, f32[384,128]{1,0:T(8,128)S(1)} %collective-permute-done.2.refs_2_, ...), custom_call_target="tpu_custom_call" | custom-call | flops 20000000000 | bytes 1000000 | tf_op jit(solution)/shard_map/pairs_hop0/pallas_call | solution.py:208
  25.2 0.0 collective-permute-done.4.refs_2_
  25.2 0.0 collective-permute-done.5.refs_3_
  25.2 3.9 %collective-permute-start.6 = (f32[768,128]{1,0:T(8,128)S(1)}, f32[768,128]{1,0:T(8,128)S(1)}, u32[]{:S(2)}, u32[]{:S(2)}) collective-permute-start(f32[768,128]{1,0:T(8,128)S(1)} %collective-permute-done.4.refs_2_), channel_id=1, source_target_pairs={{0,4},{4,8},{8,12},{1,5},{5,9},{9,13},{2,6},{6,10},{10,14},{3,7},{... | collective-permute-start | bytes 1179656 | tf_op jit(solution)/shard_map/ppermute | solution.py:393
  29.1 0.6 collective-permute-start.10
  29.7 1.3 %collective-permute-start.7 = (f32[768,128]{1,0:T(8,128)S(1)}, f32[768,128]{1,0:T(8,128)S(1)}, u32[]{:S(2)}, u32[]{:S(2)}) collective-permute-start(f32[768,128]{1,0:T(8,128)S(1)} %collective-permute-done.5.refs_3_), channel_id=1, source_target_pairs={{4,0},{8,4},{12,8},{5,1},{9,5},{13,9},{6,2},{10,6},{14,10},{7,3},{... | collective-permute-start | bytes 1179656 | tf_op jit(solution)/shard_map/ppermute | solution.py:394
  31.0 0.1 collective-permute-start.11
  31.1 4.9 %pairs_hop1.1.refs_1_ = f32[4104,128]{1,0:T(8,128)S(1)} custom-call(s32[1280]{0:T(1024)S(1)} %pad_add_fusion.pairs_ref, f32[1536,128]{1,0:T(8,128)S(1)} %get-tuple-element.22.refs_0_, f32[4104,128]{1,0:T(8,128)S(1)} %get-tuple-element.26.refs_1_, f32[768,128]{1,0:T(8,128)S(1)} %collective-permute-done.4.refs_2_, ...), custom_call_target="tpu_custom_call", output_to_operand_aliasing={{}: (2, {})} | custom-call | flops 20000000000 | bytes 1000000 | tf_op jit(solution)/shard_map/pairs_hop1/pallas_call | solution.py:208
  35.9 2.5 %collective-permute-done.6.refs_2_ = f32[768,128]{1,0:T(8,128)S(1)} collective-permute-done((f32[768,128]{1,0:T(8,128)S(1)}, f32[768,128]{1,0:T(8,128)S(1)}, u32[]{:S(2)}, u32[]{:S(2)}) %collective-permute-start.6) | collective-permute-done | bytes 393248 | tf_op jit(solution)/shard_map/ppermute | solution.py:393
  38.4 8.0 %collective-permute-done.7.refs_3_ = f32[768,128]{1,0:T(8,128)S(1)} collective-permute-done((f32[768,128]{1,0:T(8,128)S(1)}, f32[768,128]{1,0:T(8,128)S(1)}, u32[]{:S(2)}, u32[]{:S(2)}) %collective-permute-start.7) | collective-permute-done | bytes 393248 | tf_op jit(solution)/shard_map/ppermute | solution.py:394
  46.4 3.7 %collective-permute-start.8 = (f32[768,128]{1,0:T(8,128)S(1)}, f32[768,128]{1,0:T(8,128)S(1)}, u32[]{:S(2)}, u32[]{:S(2)}) collective-permute-start(f32[768,128]{1,0:T(8,128)S(1)} %collective-permute-done.6.refs_2_), channel_id=1, source_target_pairs={{0,4},{4,8},{8,12},{1,5},{5,9},{9,13},{2,6},{6,10},{10,14},{3,7},{... | collective-permute-start | bytes 1179656 | tf_op jit(solution)/shard_map/ppermute | solution.py:393
  50.1 0.1 collective-permute-start.12
  50.1 1.3 %collective-permute-start.9 = (f32[768,128]{1,0:T(8,128)S(1)}, f32[768,128]{1,0:T(8,128)S(1)}, u32[]{:S(2)}, u32[]{:S(2)}) collective-permute-start(f32[768,128]{1,0:T(8,128)S(1)} %collective-permute-done.7.refs_3_), channel_id=1, source_target_pairs={{4,0},{8,4},{12,8},{5,1},{9,5},{13,9},{6,2},{10,6},{14,10},{7,3},{... | collective-permute-start | bytes 1179656 | tf_op jit(solution)/shard_map/ppermute | solution.py:394
  51.4 0.0 collective-permute-done.10.refs_4_
  51.4 0.6 collective-permute-start.13
  52.0 0.0 collective-permute-done.11.refs_5_
  52.0 4.9 %pairs_hop2.1.refs_1_ = f32[4104,128]{1,0:T(8,128)S(1)} custom-call(s32[1280]{0:T(1024)S(1)} %pad_add_fusion.pairs_ref, f32[1536,128]{1,0:T(8,128)S(1)} %get-tuple-element.22.refs_0_, f32[4104,128]{1,0:T(8,128)S(1)} %pairs_hop1.1.refs_1_, f32[768,128]{1,0:T(8,128)S(1)} %collective-permute-done.6.refs_2_, ...), custom_call_target="tpu_custom_call", output_to_operand_aliasing={{}: (2, {})} | custom-call | flops 20000000000 | bytes 1000000 | tf_op jit(solution)/shard_map/pairs_hop2/pallas_call | solution.py:208
  56.9 1.4 %collective-permute-done.8.refs_2_ = f32[768,128]{1,0:T(8,128)S(1)} collective-permute-done((f32[768,128]{1,0:T(8,128)S(1)}, f32[768,128]{1,0:T(8,128)S(1)}, u32[]{:S(2)}, u32[]{:S(2)}) %collective-permute-start.8) | collective-permute-done | bytes 393248 | tf_op jit(solution)/shard_map/ppermute | solution.py:393
  58.3 9.2 %collective-permute-done.9.refs_3_ = f32[768,128]{1,0:T(8,128)S(1)} collective-permute-done((f32[768,128]{1,0:T(8,128)S(1)}, f32[768,128]{1,0:T(8,128)S(1)}, u32[]{:S(2)}, u32[]{:S(2)}) %collective-permute-start.9) | collective-permute-done | bytes 393248 | tf_op jit(solution)/shard_map/ppermute | solution.py:394
  67.5 0.5 collective-permute-start.15
  68.0 4.2 %pairs_hop3.1.refs_1_ = f32[4104,128]{1,0:T(8,128)S(1)} custom-call(s32[1280]{0:T(1024)S(1)} %pad_add_fusion.pairs_ref, f32[1536,128]{1,0:T(8,128)S(1)} %get-tuple-element.22.refs_0_, f32[4104,128]{1,0:T(8,128)S(1)} %pairs_hop2.1.refs_1_, f32[768,128]{1,0:T(8,128)S(1)} %collective-permute-done.8.refs_2_, ...), custom_call_target="tpu_custom_call", output_to_operand_aliasing={{}: (2, {})} | custom-call | flops 20000000000 | bytes 1000000 | tf_op jit(solution)/shard_map/pairs_hop3/pallas_call | solution.py:208
  72.2 0.0 copy-start.3
  72.2 0.0 copy-start.6
  72.2 4.6 %pairs_hop4.1 = (f32[4104,128]{1,0:T(8,128)S(1)}, f32[768,128]{1,0:T(8,128)S(1)}, f32[768,128]{1,0:T(8,128)S(1)}) custom-call(s32[1280]{0:T(1024)S(1)} %pad_add_fusion.pairs_ref, f32[1536,128]{1,0:T(8,128)S(1)} %get-tuple-element.22.refs_0_, f32[4104,128]{1,0:T(8,128)S(1)} %pairs_hop3.1.refs_1_, ...), custom_call_target="tpu_custom_call", output_to_operand_aliasing={{0}: (2, {})} | custom-call | flops 20000000000 | bytes 1000000 | tf_op jit(solution)/shard_map/pairs_hop4/pallas_call | solution.py:208
  76.8 0.1 collective-permute-start.16
  76.9 0.2 convert_reduce_fusion.3
  77.1 0.3 select_reduce_fusion.2
  77.5 1.1 %collective-permute-done.16.refs_1_ = f32[768,128]{1,0:T(8,128)S(1)} collective-permute-done((f32[768,128]{1,0:T(8,128)S(1)}, f32[768,128]{1,0:T(8,128)S(1)}, u32[]{:S(2)}, u32[]{:S(2)}) %collective-permute-start.16) | collective-permute-done | bytes 393248 | tf_op jit(solution)/shard_map/ppermute | solution.py:342
  78.6 0.1 collective-permute-start.17
  78.7 6.9 %collective-permute-done.17.refs_2_ = f32[384,128]{1,0:T(8,128)S(1)} collective-permute-done((f32[384,128]{1,0:T(8,128)S(1)}, f32[384,128]{1,0:T(8,128)S(1)}, u32[]{:S(2)}, u32[]{:S(2)}) %collective-permute-start.17) | collective-permute-done | bytes 196640 | tf_op jit(solution)/shard_map/ppermute | solution.py:342
  85.6 1.5 %pack_owners.1 = f32[768,128]{1,0:T(8,128)} custom-call(s32[128]{0:T(128)S(1)} %multiply_add_fusion.place_ref, f32[768,128]{1,0:T(8,128)S(1)} %get-tuple-element.33.refs_0_, f32[768,128]{1,0:T(8,128)S(1)} %collective-permute-done.16.refs_1_, f32[384,128]{1,0:T(8,128)S(1)} %collective-permute-done.17.refs_2_), custom_call_target="tpu_custom_call" | custom-call | tf_op jit(solution)/shard_map/pack_owners/pallas_call | solution.py:278
  87.2 7.7 %all-to-all-start = ((f32[16,48,128]{2,1,0:T(8,128)}), f32[16,48,128]{2,1,0:T(8,128)S(1)}, u32[]{:S(2)}, u32[]{:S(2)}) async-start(f32[16,48,128]{2,1,0:T(8,128)} %bitcast.11), calls=%async_computation | async-start | bytes 786432 | tf_op jit(solution)/shard_map/all_to_all | solution.py:417
  94.9 0.1 and.139
  95.0 0.1 shift_right_arithmetic.10.count_ref
  95.1 0.2 convert_reduce_fusion.4
  95.3 11.8 %all-to-all-done = f32[16,48,128]{2,1,0:T(8,128)S(1)} async-done(((f32[16,48,128]{2,1,0:T(8,128)}), f32[16,48,128]{2,1,0:T(8,128)S(1)}, u32[]{:S(2)}, u32[]{:S(2)}) %all-to-all-start) | async-done | bytes 393248 | tf_op jit(solution)/shard_map/all_to_all | solution.py:417
  107.1 1.5 %unpack_drops.1 = f32[384,128]{1,0:T(8,128)} custom-call(s32[128]{0:T(128)S(1)} %multiply_add_fusion.1.place_ref, s32[128]{0:T(128)S(1)} %shift_right_arithmetic.10.count_ref, f32[768,128]{1,0:T(8,128)S(1)} %bitcast.20), custom_call_target="tpu_custom_call" | custom-call | tf_op jit(solution)/shard_map/unpack_drops/pallas_call | solution.py:308
  (24 shorter events, 0.1 us)
Async XLA Ops:
  0.0 0.9 copy-start
  0.9 0.9 copy-start.1
  1.9 0.7 copy-start.2
  2.6 0.8 copy-start.4
  3.4 0.7 copy-start.5
  4.3 16.5 %collective-permute-start.1 = (f32[768,128]{1,0:T(8,128)S(1)}, f32[768,128]{1,0:T(8,128)S(1)}, u32[]{:S(2)}, u32[]{:S(2)}) collective-permute-start(f32[768,128]{1,0:T(8,128)S(1)} %get-tuple-element.21.refs_4_), channel_id=1, source_target_pairs={{0,1},{1,0},{2,3},{3,2},{4,5},{5,4},{6,7},{7,6},{8,9},{9,8},{10,11... | collective-permute-start | bytes 1179656 | tf_op jit(solution)/shard_map/ppermute | solution.py:342
  4.8 20.4 %collective-permute-start.4 = (f32[768,128]{1,0:T(8,128)S(1)}, f32[768,128]{1,0:T(8,128)S(1)}, u32[]{:S(2)}, u32[]{:S(2)}) collective-permute-start(f32[768,128]{1,0:T(8,128)S(1)} %get-tuple-element.21.refs_4_), channel_id=1, source_target_pairs={{0,4},{4,8},{8,12},{1,5},{5,9},{9,13},{2,6},{6,10},{10,14},{3,7},{... | collective-permute-start | bytes 1179656 | tf_op jit(solution)/shard_map/ppermute | solution.py:357
  9.3 15.9 %collective-permute-start.5 = (f32[768,128]{1,0:T(8,128)S(1)}, f32[768,128]{1,0:T(8,128)S(1)}, u32[]{:S(2)}, u32[]{:S(2)}) collective-permute-start(f32[768,128]{1,0:T(8,128)S(1)} %get-tuple-element.21.refs_4_), channel_id=1, source_target_pairs={{4,0},{8,4},{12,8},{5,1},{9,5},{13,9},{6,2},{10,6},{14,10},{7,3},{... | collective-permute-start | bytes 1179656 | tf_op jit(solution)/shard_map/ppermute | solution.py:358
  13.4 7.4 %collective-permute-start = (s32[640]{0:T(1024)S(1)}, s32[640]{0:T(1024)S(1)}, u32[]{:S(2)}, u32[]{:S(2)}) collective-permute-start(s32[640]{0:T(1024)S(1)} %pad_add_fusion.1), channel_id=1, source_target_pairs={{0,1},{1,0},{2,3},{3,2},{4,5},{5,4},{6,7},{7,6},{8,9},{9,8},{10,11... | collective-permute-start | bytes 7688 | tf_op jit(solution)/shard_map/ppermute | solution.py:342
  13.6 7.1 %collective-permute-start.2 = (f32[384,128]{1,0:T(8,128)S(1)}, f32[384,128]{1,0:T(8,128)S(1)}, u32[]{:S(2)}, u32[]{:S(2)}) collective-permute-start(f32[384,128]{1,0:T(8,128)S(1)} %get-tuple-element.20.refs_0_), channel_id=1, source_target_pairs={{0,2},{1,3},{2,0},{3,1},{4,6},{5,7},{6,4},{7,5},{8,10},{9,11},{10,... | collective-permute-start | bytes 589832 | tf_op jit(solution)/shard_map/ppermute | solution.py:342
  20.7 1.4 %collective-permute-start.3 = (f32[384,128]{1,0:T(8,128)S(1)}, f32[384,128]{1,0:T(8,128)S(1)}, u32[]{:S(2)}, u32[]{:S(2)}) collective-permute-start(f32[384,128]{1,0:T(8,128)S(1)} %collective-permute-done.2.refs_2_), channel_id=1, source_target_pairs={{0,1},{1,0},{2,3},{3,2},{4,5},{5,4},{6,7},{7,6},{8,9},{9,8},{10,11... | collective-permute-start | bytes 589832 | tf_op jit(solution)/shard_map/ppermute | solution.py:342
  25.2 13.2 %collective-permute-start.6 = (f32[768,128]{1,0:T(8,128)S(1)}, f32[768,128]{1,0:T(8,128)S(1)}, u32[]{:S(2)}, u32[]{:S(2)}) collective-permute-start(f32[768,128]{1,0:T(8,128)S(1)} %collective-permute-done.4.refs_2_), channel_id=1, source_target_pairs={{0,4},{4,8},{8,12},{1,5},{5,9},{9,13},{2,6},{6,10},{10,14},{3,7},{... | collective-permute-start | bytes 1179656 | tf_op jit(solution)/shard_map/ppermute | solution.py:393
  29.1 22.3 %collective-permute-start.10 = (f32[768,128]{1,0:T(8,128)S(1)}, f32[768,128]{1,0:T(8,128)S(1)}, u32[]{:S(2)}, u32[]{:S(2)}) collective-permute-start(f32[768,128]{1,0:T(8,128)S(1)} %collective-permute-done.4.refs_2_), channel_id=1, source_target_pairs={{0,1},{1,0},{2,3},{3,2},{4,5},{5,4},{6,7},{7,6},{8,9},{9,8},{10,11... | collective-permute-start | bytes 1179656 | tf_op jit(solution)/shard_map/ppermute | solution.py:342
  29.7 16.7 %collective-permute-start.7 = (f32[768,128]{1,0:T(8,128)S(1)}, f32[768,128]{1,0:T(8,128)S(1)}, u32[]{:S(2)}, u32[]{:S(2)}) collective-permute-start(f32[768,128]{1,0:T(8,128)S(1)} %collective-permute-done.5.refs_3_), channel_id=1, source_target_pairs={{4,0},{8,4},{12,8},{5,1},{9,5},{13,9},{6,2},{10,6},{14,10},{7,3},{... | collective-permute-start | bytes 1179656 | tf_op jit(solution)/shard_map/ppermute | solution.py:394
  31.0 21.0 %collective-permute-start.11 = (f32[768,128]{1,0:T(8,128)S(1)}, f32[768,128]{1,0:T(8,128)S(1)}, u32[]{:S(2)}, u32[]{:S(2)}) collective-permute-start(f32[768,128]{1,0:T(8,128)S(1)} %collective-permute-done.5.refs_3_), channel_id=1, source_target_pairs={{0,1},{1,0},{2,3},{3,2},{4,5},{5,4},{6,7},{7,6},{8,9},{9,8},{10,11... | collective-permute-start | bytes 1179656 | tf_op jit(solution)/shard_map/ppermute | solution.py:342
  46.4 11.9 %collective-permute-start.8 = (f32[768,128]{1,0:T(8,128)S(1)}, f32[768,128]{1,0:T(8,128)S(1)}, u32[]{:S(2)}, u32[]{:S(2)}) collective-permute-start(f32[768,128]{1,0:T(8,128)S(1)} %collective-permute-done.6.refs_2_), channel_id=1, source_target_pairs={{0,4},{4,8},{8,12},{1,5},{5,9},{9,13},{2,6},{6,10},{10,14},{3,7},{... | collective-permute-start | bytes 1179656 | tf_op jit(solution)/shard_map/ppermute | solution.py:393
  50.1 17.9 %collective-permute-start.12 = (f32[768,128]{1,0:T(8,128)S(1)}, f32[768,128]{1,0:T(8,128)S(1)}, u32[]{:S(2)}, u32[]{:S(2)}) collective-permute-start(f32[768,128]{1,0:T(8,128)S(1)} %collective-permute-done.6.refs_2_), channel_id=1, source_target_pairs={{0,1},{1,0},{2,3},{3,2},{4,5},{5,4},{6,7},{7,6},{8,9},{9,8},{10,11... | collective-permute-start | bytes 1179656 | tf_op jit(solution)/shard_map/ppermute | solution.py:342
  50.1 17.3 %collective-permute-start.9 = (f32[768,128]{1,0:T(8,128)S(1)}, f32[768,128]{1,0:T(8,128)S(1)}, u32[]{:S(2)}, u32[]{:S(2)}) collective-permute-start(f32[768,128]{1,0:T(8,128)S(1)} %collective-permute-done.7.refs_3_), channel_id=1, source_target_pairs={{4,0},{8,4},{12,8},{5,1},{9,5},{13,9},{6,2},{10,6},{14,10},{7,3},{... | collective-permute-start | bytes 1179656 | tf_op jit(solution)/shard_map/ppermute | solution.py:394
  51.4 16.5 %collective-permute-start.13 = (f32[768,128]{1,0:T(8,128)S(1)}, f32[768,128]{1,0:T(8,128)S(1)}, u32[]{:S(2)}, u32[]{:S(2)}) collective-permute-start(f32[768,128]{1,0:T(8,128)S(1)} %collective-permute-done.7.refs_3_), channel_id=1, source_target_pairs={{0,1},{1,0},{2,3},{3,2},{4,5},{5,4},{6,7},{7,6},{8,9},{9,8},{10,11... | collective-permute-start | bytes 1179656 | tf_op jit(solution)/shard_map/ppermute | solution.py:342
  67.5 4.8 %collective-permute-start.14 = (f32[768,128]{1,0:T(8,128)S(1)}, f32[768,128]{1,0:T(8,128)S(1)}, u32[]{:S(2)}, u32[]{:S(2)}) collective-permute-start(f32[768,128]{1,0:T(8,128)S(1)} %collective-permute-done.8.refs_2_), channel_id=1, source_target_pairs={{0,1},{1,0},{2,3},{3,2},{4,5},{5,4},{6,7},{7,6},{8,9},{9,8},{10,11... | collective-permute-start | bytes 1179656 | tf_op jit(solution)/shard_map/ppermute | solution.py:342
  67.5 4.8 %collective-permute-start.15 = (f32[768,128]{1,0:T(8,128)S(1)}, f32[768,128]{1,0:T(8,128)S(1)}, u32[]{:S(2)}, u32[]{:S(2)}) collective-permute-start(f32[768,128]{1,0:T(8,128)S(1)} %collective-permute-done.9.refs_3_), channel_id=1, source_target_pairs={{0,1},{1,0},{2,3},{3,2},{4,5},{5,4},{6,7},{7,6},{8,9},{9,8},{10,11... | collective-permute-start | bytes 1179656 | tf_op jit(solution)/shard_map/ppermute | solution.py:342
  72.2 4.9 %copy-start.3 = (s32[256,8]{0,1:T(8,128)S(1)}, s32[256,8]{0,1:T(8,128)}, u32[]{:S(2)}) copy-start(s32[256,8]{0,1:T(8,128)} %param.16) | copy-start | bytes 24580
  72.2 4.9 %copy-start.6 = (s32[256,8]{0,1:T(8,128)S(1)}, s32[256,8]{0,1:T(8,128)}, u32[]{:S(2)}) copy-start(s32[256,8]{0,1:T(8,128)} %param.15) | copy-start | bytes 24580
  76.8 1.8 %collective-permute-start.16 = (f32[768,128]{1,0:T(8,128)S(1)}, f32[768,128]{1,0:T(8,128)S(1)}, u32[]{:S(2)}, u32[]{:S(2)}) collective-permute-start(f32[768,128]{1,0:T(8,128)S(1)} %get-tuple-element.34), channel_id=1, source_target_pairs={{0,1},{1,0},{2,3},{3,2},{4,5},{5,4},{6,7},{7,6},{8,9},{9,8},{10,11... | collective-permute-start | bytes 1179656 | tf_op jit(solution)/shard_map/ppermute | solution.py:342
  78.6 7.0 %collective-permute-start.17 = (f32[384,128]{1,0:T(8,128)S(1)}, f32[384,128]{1,0:T(8,128)S(1)}, u32[]{:S(2)}, u32[]{:S(2)}) collective-permute-start(f32[384,128]{1,0:T(8,128)S(1)} %slice_add_fusion), channel_id=1, source_target_pairs={{0,2},{1,3},{2,0},{3,1},{4,6},{5,7},{6,4},{7,5},{8,10},{9,11},{10,... | collective-permute-start | bytes 589832 | tf_op jit(solution)/shard_map/ppermute | solution.py:342
  87.2 19.9 %all-to-all-start = ((f32[16,48,128]{2,1,0:T(8,128)}), f32[16,48,128]{2,1,0:T(8,128)S(1)}, u32[]{:S(2)}, u32[]{:S(2)}) async-start(f32[16,48,128]{2,1,0:T(8,128)} %bitcast.11), calls=%async_computation | async-start | bytes 786432 | tf_op jit(solution)/shard_map/all_to_all | solution.py:417

commit v3 on v2

--- a/solution.py
+++ b/solution.py
@@ -19,6 +19,7 @@
 kernel_flops = 2 * 10**10
 vmem = pl.BlockSpec(memory_space=pltpu.VMEM)
 smem = pl.BlockSpec(memory_space=pltpu.SMEM)
+hbm = pl.BlockSpec(memory_space=pltpu.HBM)
 
 
 def split3(value):
@@ -93,8 +94,8 @@
     return jnp.where(row == 0, sums[0], jnp.where(row == 1, sums[1], jnp.where(row == 2, sums[2], 0.0)))
 
 
-def hop_kernel(spec, pairs_ref, *refs):
-    n, slots, hop, hops, homes, own, mate, first, last, split = spec
+def hop_kernel(spec, list_ref, mate_list_ref, *refs):
+    n, slots, hop, homes, own, mate, first, last, split = spec
     refs = list(refs)
     if first:
         target_refs = [refs.pop(0) for _ in range(homes)]
@@ -117,28 +118,35 @@
     for place, block in list(enumerate(own_refs)) + [(2 + b, block) for b, block in enumerate(mate_refs)]:
         source_ref[6 * n * place : 6 * n * (place + 1), :] = block[...]
 
-    width = pairs_ref.shape[0] // 2
-    slots_of = width - 128
+    bound_row = list_ref.shape[0] - 1
     own_start, own_count, mate_start, mate_count = 0, 0, 0, 0
     if own:
-        own_start = pairs_ref[slots_of + hop]
-        own_count = (pairs_ref[slots_of + hop + 1] - own_start + 1) >> 1
+        own_start = list_ref[bound_row, hop]
+        own_count = (list_ref[bound_row, hop + 1] - own_start + 1) >> 1
     if mate:
-        begin = pairs_ref[width + slots_of + hop - 1]
-        end = pairs_ref[width + slots_of + hop]
-        mate_start = width + begin + ((end - begin + 1) >> 1)
-        mate_count = width + end - mate_start
+        begin = mate_list_ref[bound_row, hop - 1]
+        end = mate_list_ref[bound_row, hop]
+        mate_start = begin + ((end - begin + 1) >> 1)
+        mate_count = end - mate_start
     count = own_count + mate_count
     mate_start = mate_start - own_count
 
     def entry(index):
         live = index < count
-        index = jnp.where(live, index, 0)
-        place = index + jnp.where(index < own_count, own_start, mate_start)
-        packed = pairs_ref[jnp.where(live, place, 0)]
-        target = jnp.where(live, packed & 0xFFFF, 0)
-        source = jnp.where(live, packed >> 16, 0)
-        return live, target, source
+        mine = index < own_count
+        place = jnp.where(live, index + jnp.where(mine, own_start, mate_start), 0)
+        row, lane = place >> 7, place & 127
+        target, source = 0, 0
+        if own:
+            packed = list_ref[row, lane]
+            target, source = packed & 0xFFF, packed >> 12
+        if mate:
+            packed = mate_list_ref[row, lane]
+            flip = n if split else 0
+            mate_target, mate_source = (packed & 0xFFF) ^ flip, (packed >> 12) + 2 * n
+            target = jnp.where(mine, target, mate_target)
+            source = jnp.where(mine, source, mate_source)
+        return live, jnp.where(live, target, 0), jnp.where(live, source, 0)
 
     def source_rows(source):
         base = source + (source >> shift) * (5 * n)
@@ -176,22 +184,26 @@
 
     lax.fori_loop(0, (count + unroll - 1) // unroll, step, 0)
     if last:
-        totals = total_ref.reshape(total_ref.shape[0] // 8, 8, slots)
         for h in range(homes):
             out_ref = out_refs[h % 2] if split else out_refs[0]
-            place = h // 2 if split else h
-            for k in range(3):
-                rows = slice(n * (3 * place + k), n * (3 * place + k + 1))
-                out_ref[rows, :] = totals[n * h : n * (h + 1), k, :]
-
-
-def hop_call(n, hop, hops, pairs, targets, total, own, mate, split):
+            first_row = 3 * n * (h // 2 if split else h)
+
+            def move(i, carry, h=h, out_ref=out_ref, first_row=first_row):
+                for u in range(8):
+                    tile = total_ref[pl.ds(pl.multiple_of((n * h + i * 8 + u) * 8, 8), 8), :]
+                    out_ref[pl.ds(first_row + i * 24 + 3 * u, 3), :] = tile[:3]
+                return carry
+
+            lax.fori_loop(0, n // 8, move, 0)
+
+
+def hop_call(n, hop, hops, lists, targets, total, own, mate, split):
     first, last = hop == 0, hop == hops
     slots = own[0].shape[1] if own else mate[0].shape[1]
     homes = len(targets) if first else targets[0].shape[0] // (3 * n)
     total_shape = jax.ShapeDtypeStruct((homes * n * 8 + 8, slots), f32)
     aliases = {}
-    operands = [pairs, *targets]
+    operands = [*lists, *targets]
     if not first:
         operands.append(total)
     if first:
@@ -204,11 +216,11 @@
     if not first:
         aliases = {len(operands) - 1: 0}
     operands += [*own, *mate]
-    spec = (n, slots, hop, hops, homes, len(own), len(mate), first, last, split)
+    spec = (n, slots, hop, homes, len(own), len(mate), first, last, split)
     return pl.pallas_call(
         functools.partial(hop_kernel, spec),
         out_shape=out_shape,
-        in_specs=[smem] + [vmem] * (len(operands) - 1),
+        in_specs=[smem, smem] + [vmem] * (len(operands) - 2),
         out_specs=[vmem] * len(out_shape),
         scratch_shapes=[
             pltpu.VMEM((4 * 6 * n, slots), f32),
@@ -221,7 +233,22 @@
     )(*operands)
 
 
-def prep_kernel(n, base_ref, position_ref, normal_ref, curvature_ref, cluster_ref, count_ref, out_ref, own_ref):
+def fetch_all(pairs, sems):
+    copies = [pltpu.make_async_copy(a, b, sems.at[k]) for k, (a, b) in enumerate(pairs)]
+    for copy in copies:
+        copy.start()
+    for copy in copies:
+        copy.wait()
+
+
+def column(row, rows):
+    return jnp.broadcast_to(row, (rows, 128)).T
+
+
+def prep_kernel(n, base_ref, *refs):
+    ins, (out_ref, own_ref), held, sems = refs[:5], refs[5:7], refs[7:12], refs[12]
+    fetch_all(list(zip(ins, held)), sems)
+    position_ref, normal_ref, curvature_ref, cluster_ref, count_ref = held
     slots = position_ref.shape[1]
     scaled = position_ref[...] * length_scale
     out_ref[: 3 * n, :] = scaled
@@ -241,19 +268,116 @@
         out_ref[n * (3 + k) : n * (4 + k), :] = normal_ref[n * k : n * (k + 1), :] * strength
 
 
-def prep_call(base, position, normal, curvature, clusters, counts):
-    n, slots = curvature.shape
+def prep_call(base, *operands):
+    n, slots = operands[2].shape
     return pl.pallas_call(
         functools.partial(prep_kernel, n),
         out_shape=[jax.ShapeDtypeStruct((6 * n, slots), f32), jax.ShapeDtypeStruct((3 * n, slots), f32)],
-        in_specs=[smem] + [vmem] * 5,
+        in_specs=[smem] + [hbm] * 5,
         out_specs=[vmem, vmem],
+        scratch_shapes=[pltpu.VMEM(x.shape, x.dtype) for x in operands] + [pltpu.SemaphoreType.DMA((5,))],
         compiler_params=pltpu.CompilerParams(vmem_limit_bytes=vmem_limit),
         name="prep_sources",
-    )(base, position, normal, curvature, clusters, counts)
-
-
-def pack_kernel(n, capacity, place_ref, *refs):
+    )(base, *operands)
+
+
+def index_kernel(spec, facts_ref, *refs):
+    n, rows, cols, capacity, split = spec
+    ins, (list_ref, place_ref), held, sems = refs[:5], refs[5:7], refs[7:12], refs[12]
+    fetch_all(list(zip(ins, held)), sems)
+    target_ref, source_ref, cluster_ref, count_ref, owner_ref = held
+    my_row, my_col, device, live_pairs = [facts_ref[k] for k in range(4)]
+    shift = n.bit_length() - 1
+    wide = (128, 128)
+    lane_row = lax.broadcasted_iota(i32, (1, 128), 1)
+    sub = lax.broadcasted_iota(i32, wide, 0)
+    lane = lax.broadcasted_iota(i32, wide, 1)
+
+    blocks = target_ref.shape[1] // 128
+    keys, packs = [], []
+    for b in range(blocks):
+        target = target_ref[:, 128 * b : 128 * (b + 1)]
+        source = source_ref[:, 128 * b : 128 * (b + 1)]
+        source_row = source >> shift
+        index = lane_row + 128 * b
+        key = jnp.where(index < live_pairs, jnp.abs(source_row - my_row), rows)
+        keys.append(key * (128 * blocks) + index)
+        home = target >> shift
+        if split:
+            home = home ^ my_col
+        side = jnp.where(source_row > my_row, n, 0)
+        packs.append((home * n + (target & (n - 1)) + (side + (source & (n - 1))) * 4096).astype(f32))
+    key_columns = [column(key, 128) for key in keys]
+    order_columns = []
+    for b in range(blocks):
+        before = jnp.zeros(wide, f32)
+        for c in range(blocks):
+            before = before + jnp.where(key_columns[c] < jnp.broadcast_to(keys[b], wide), 1.0, 0.0)
+        order_columns.append(column(jnp.sum(before, axis=0, keepdims=True), 128))
+    pack_columns = [column(pack, 128) for pack in packs]
+    lanes = lane.astype(f32)
+    for b in range(blocks):
+        ordered = jnp.zeros(wide, f32)
+        for c in range(blocks):
+            ordered = ordered + jnp.where(order_columns[c] == lanes + 128.0 * b, pack_columns[c], 0.0)
+        list_ref[b : b + 1, :] = jnp.sum(ordered, axis=0, keepdims=True).astype(i32)
+    below = jnp.zeros(wide, f32)
+    for c in range(blocks):
+        below = below + jnp.where(key_columns[c] < lane * (128 * blocks), 1.0, 0.0)
+    list_ref[blocks : blocks + 1, :] = jnp.sum(below, axis=0, keepdims=True).astype(i32)
+
+    per_drop = cluster_ref.shape[0]
+    mine = device * n + sub
+    drop_blocks = owner_ref.shape[1] // 128
+
+    def scan(j, carry):
+        owner_sum, chosen, owned_before = carry
+        part = pl.ds(pl.multiple_of(j * 128, 128), 128)
+        owner = owner_ref[:, part]
+        is_mine = jnp.where(owner == device, 1.0, 0.0)
+        mine_column = column(is_mine, 128)
+        rank = jnp.sum(jnp.where(sub < lane, mine_column, 0.0), axis=0, keepdims=True) + owned_before
+        slot = jnp.where(owner == device, rank, -1.0)
+        picked = column(slot, 128) == (lane // per_drop).astype(f32)
+        for k in range(per_drop):
+            cluster = cluster_ref[k : k + 1, part]
+            fact = (cluster + count_ref[k : k + 1, part] * 16384).astype(f32)
+            chosen = chosen + jnp.where(picked & (lane % per_drop == k), column(fact, 128), 0.0)
+            wide_owner = jnp.broadcast_to(owner.astype(f32), wide)
+            owner_sum = owner_sum + jnp.where(jnp.broadcast_to(cluster, wide) == mine, wide_owner, 0.0)
+        return owner_sum, chosen, owned_before + jnp.sum(is_mine, axis=1, keepdims=True)
+
+    start = (jnp.zeros(wide, f32), jnp.zeros(wide, f32), jnp.zeros((1, 1), f32))
+    owner_sum, chosen, _ = lax.fori_loop(0, drop_blocks, scan, start)
+    home_owner = jnp.broadcast_to(jnp.sum(owner_sum, axis=1, keepdims=True), wide)
+    owner_lanes = home_owner.T
+    rank = jnp.sum(jnp.where((home_owner == owner_lanes) & (sub < lane), 1.0, 0.0), axis=0, keepdims=True)
+    place_ref[0:1, :] = ((owner_lanes[0:1] * capacity + rank) * 3.0).astype(i32)
+    fact = jnp.sum(chosen, axis=0, keepdims=True).astype(i32)
+    cluster = fact & 16383
+    anchor = cluster >> shift
+    cluster_column = column(cluster, 128)
+    cluster_wide = jnp.broadcast_to(cluster, wide)
+    same = (cluster_column >> shift) == (cluster_wide >> shift)
+    rank = jnp.sum(jnp.where(same & (cluster_column < cluster_wide), 1.0, 0.0), axis=0, keepdims=True)
+    place_ref[1:2, :] = (anchor * capacity + rank.astype(i32)) * 3
+    place_ref[2:3, :] = fact >> 14
+
+
+def index_call(spec, facts, *operands):
+    blocks = operands[0].shape[1] // 128
+    return pl.pallas_call(
+        functools.partial(index_kernel, spec),
+        out_shape=[jax.ShapeDtypeStruct((blocks + 1, 128), i32), jax.ShapeDtypeStruct((3, 128), i32)],
+        in_specs=[smem] + [hbm] * 5,
+        out_specs=[vmem, vmem],
+        scratch_shapes=[pltpu.VMEM(x.shape, x.dtype) for x in operands] + [pltpu.SemaphoreType.DMA((5,))],
+        compiler_params=pltpu.CompilerParams(vmem_limit_bytes=vmem_limit),
+        name="index_work",
+    )(facts, *operands)
+
+
+def pack_kernel(n, place_ref, *refs):
     *speed_refs, out_ref, speed_ref = refs
     total = speed_refs[0][: 3 * n, :]
     for part in speed_refs[1:]:
@@ -264,19 +388,16 @@
     def step(i, carry):
         for u in range(16):
             cluster = i * 16 + u
-            place = place_ref[cluster]
-            for k in range(3):
-                out_ref[pl.ds(place + capacity * k, 1), :] = speed_ref[pl.ds(cluster + n * k, 1), :]
+            out_ref[pl.ds(place_ref[0, cluster], 3), :] = speed_ref[pl.ds(3 * cluster, 3), :]
         return carry
 
     lax.fori_loop(0, n // 16, step, 0)
 
 
-def pack_call(places, speeds, capacity, devices):
-    n = places.shape[0]
+def pack_call(places, speeds, n, capacity, devices):
     slots = speeds[0].shape[1]
     return pl.pallas_call(
-        functools.partial(pack_kernel, n, capacity),
+        functools.partial(pack_kernel, n),
         out_shape=jax.ShapeDtypeStruct((devices * capacity * 3, slots), f32),
         in_specs=[smem] + [vmem] * len(speeds),
         out_specs=vmem,
@@ -286,33 +407,33 @@
     )(places, *speeds)
 
 
-def unpack_kernel(n, capacity, place_ref, count_ref, arrived_ref, out_ref):
+def unpack_kernel(n, place_ref, arrived_ref, out_ref, tile_ref):
     slots = arrived_ref.shape[1]
-    lane = lax.broadcasted_iota(i32, (1, slots), 1)
+    lane = lax.broadcasted_iota(i32, (3, slots), 1)
 
     def step(i, carry):
         for u in range(16):
             cluster = i * 16 + u
-            place = place_ref[cluster]
-            live = lane < count_ref[cluster]
-            for k in range(3):
-                value = arrived_ref[pl.ds(place + capacity * k, 1), :]
-                out_ref[pl.ds(cluster + n * k, 1), :] = jnp.where(live, value, 0.0)
+            value = arrived_ref[pl.ds(place_ref[1, cluster], 3), :]
+            tile_ref[cluster, :3, :] = jnp.where(lane < place_ref[2, cluster], value, 0.0)
         return carry
 
     lax.fori_loop(0, n // 16, step, 0)
-
-
-def unpack_call(places, counts, arrived, capacity):
-    n, slots = places.shape[0], arrived.shape[1]
+    for k in range(3):
+        out_ref[n * k : n * (k + 1), :] = tile_ref[:, k, :]
+
+
+def unpack_call(places, arrived, n):
+    slots = arrived.shape[1]
     return pl.pallas_call(
-        functools.partial(unpack_kernel, n, capacity),
+        functools.partial(unpack_kernel, n),
         out_shape=jax.ShapeDtypeStruct((3 * n, slots), f32),
-        in_specs=[smem, smem, vmem],
+        in_specs=[smem, vmem],
         out_specs=vmem,
+        scratch_shapes=[pltpu.VMEM((n, 8, slots), f32)],
         compiler_params=pltpu.CompilerParams(vmem_limit_bytes=vmem_limit),
         name="unpack_drops",
-    )(places, counts, arrived)
+    )(places, arrived)
 
 
 def per_device(
@@ -334,8 +455,6 @@
     my_col = lax.axis_index("col")
     device = my_row * cols + my_col
     capacity = max(2, 2 * n // devices)
-    drops, per_drop = drop_clusters.shape
-    drops_here = n // per_drop
     hypercube = cols == 4
 
     def swap(value, bit):
@@ -344,58 +463,51 @@
     def component_major(value):
         return jnp.transpose(value, (1, 0, 2)).reshape(3 * n, slots)
 
+    clusters, counts = drop_clusters.T, node_counts.T
     block, position = prep_call(
         (device * n).reshape(1),
         component_major(positions),
         component_major(normals),
         curvature,
-        drop_clusters.T,
-        node_counts.T,
+        clusters,
+        counts,
     )
+    mate_block = swap(block, 1)
+    if hypercube:
+        across = swap(position, 2)
     to_right = [(r, r + 1) for r in range(rows - 1)]
     to_left = [(r + 1, r) for r in range(rows - 1)]
     right = lax.ppermute(block, "row", to_right)
     left = lax.ppermute(block, "row", to_left)
-    mate_block = swap(block, 1)
     if hypercube:
-        across = swap(position, 2)
         targets = [position, mate_block, across, swap(across, 1)]
     else:
         gathered = lax.all_gather(position, "col", axis=0, tiled=True)
         targets = [gathered[3 * n * h : 3 * n * (h + 1)] for h in range(cols)]
-
-    pair_slots = pair_targets.shape[1]
-    entry = jnp.arange(pair_slots, dtype=i32)
-    source_row = pair_sources[0] // n
-    key = jnp.where(entry < pair_count[0], jnp.abs(source_row - my_row), rows)
-    home = pair_targets[0] // n
-    home = home ^ my_col if hypercube else home
-    target = home * n + pair_targets[0] % n
-    packed = target | ((jnp.where(source_row > my_row, n, 0) + pair_sources[0] % n) << 16)
-    ahead = (key[None, :] < key[:, None]) | ((key[None, :] == key[:, None]) & (entry[None, :] < entry[:, None]))
-    place = jnp.sum(ahead.astype(i32), axis=1)
-    ordered = jnp.sum(jnp.where(place[:, None] == entry[None, :], packed[:, None], 0), axis=0)
-    bounds = jnp.sum((key[None, :] < jnp.arange(128, dtype=i32)[:, None]).astype(i32), axis=1)
-    listed = jnp.concatenate([ordered, bounds])
-    mate_listed = swap(listed, 1)
-    flip = n if hypercube else 0
-    mate_pairs = jnp.where(
-        jnp.arange(pair_slots + 128) < pair_slots, (mate_listed ^ flip) + ((2 * n) << 16), mate_listed
+    listed, places = index_call(
+        (n, rows, cols, capacity, hypercube),
+        jnp.stack([my_row, my_col, device, pair_count[0]]),
+        pair_targets,
+        pair_sources,
+        clusters,
+        counts,
+        drop_owner.reshape(1, -1),
     )
-    pairs = jnp.concatenate([listed, mate_pairs])
-
-    total, all_targets = hop_call(n, 0, rows, pairs, targets, None, [block], [], hypercube)
+    lists = [listed, swap(listed, 1)]
+
+    total, all_targets = hop_call(n, 0, rows, lists, targets, None, [block], [], hypercube)
     mate = [mate_block]
     for hop in range(1, rows):
-        right, left, total = lax.optimization_barrier((right, left, total))
-        own = [right, left]
+        right_here, left_here = right, left
         if hop + 1 < rows:
+            right, total = lax.optimization_barrier((right, total))
             right = lax.ppermute(right, "row", to_right)
+            left, total = lax.optimization_barrier((left, total))
             left = lax.ppermute(left, "row", to_left)
-        next_mate = [swap(own[0], 1), swap(own[1], 1)]
-        (total,) = hop_call(n, hop, rows, pairs, [all_targets], total, own, mate, hypercube)
+        next_mate = [swap(right_here, 1), swap(left_here, 1)]
+        (total,) = hop_call(n, hop, rows, lists, [all_targets], total, [right_here, left_here], mate, hypercube)
         mate = next_mate
-    _, *speed = hop_call(n, rows, rows, pairs, [all_targets], total, [], mate, hypercube)
+    _, *speed = hop_call(n, rows, rows, lists, [all_targets], total, [], mate, hypercube)
 
     if hypercube:
         kept, sent = speed
@@ -405,29 +517,9 @@
     else:
         home_speed = [lax.psum_scatter(speed[0], "col", scatter_dimension=0, tiled=True)]
 
-    flat_clusters = drop_clusters.reshape(-1)
-    flat_owner = jnp.broadcast_to(drop_owner[:, None], drop_clusters.shape).reshape(-1)
-    local = jnp.arange(n, dtype=i32)
-    home_owner = jnp.sum(
-        jnp.where(flat_clusters[:, None] == (device * n + local)[None, :], flat_owner[:, None], 0), axis=0
-    )
-    earlier = (home_owner[None, :] == home_owner[:, None]) & (local[None, :] < local[:, None])
-    send_rank = jnp.sum(earlier.astype(i32), axis=1)
-    outgoing = pack_call(home_owner * (3 * capacity) + send_rank, home_speed, capacity, devices)
+    outgoing = pack_call(places, home_speed, n, capacity, devices)
     arrived = lax.all_to_all(outgoing, ("row", "col"), split_axis=0, concat_axis=0, tiled=True)
-
-    owned = drop_owner == device
-    drop_index = jnp.arange(drops, dtype=i32)
-    order = jnp.sum((owned[None, :] & (drop_index[None, :] < drop_index[:, None])).astype(i32), axis=1)
-    chosen = owned[None, :] & (order[None, :] == jnp.arange(drops_here, dtype=i32)[:, None])
-    drop_facts = drop_clusters | (node_counts << 16)
-    owned_facts = jnp.sum(jnp.where(chosen[:, :, None], drop_facts[None], 0), axis=1).reshape(-1)
-    owned_clusters = owned_facts & 0xFFFF
-    owned_counts = owned_facts >> 16
-    anchor = owned_clusters // n
-    before = (anchor[None, :] == anchor[:, None]) & (owned_clusters[None, :] < owned_clusters[:, None])
-    arrive_rank = jnp.sum(before.astype(i32), axis=1)
-    result = unpack_call(anchor * (3 * capacity) + arrive_rank, owned_counts, arrived, capacity)
+    result = unpack_call(places, arrived, n)
     return jnp.transpose(result.reshape(3, n, slots), (1, 0, 2))
 
 

time: 107 us -> 113 us (1.056)
  the two profiles are of different devices: /device:TPU:0 before, /device:TPU:5 now
where the time goes in v3:
time: 113 us; the launch traced here: 112 us
  blocking collectives  28.7 us (25%)
  Pallas kernels  25.1 us (22%)
  starting transfers between devices  25.1 us (22%)
  waiting for transfers between devices  24.3 us (22%)
  local copies, waits for them, and re-layouts  7.52 us (7%)
    all_to_all x1, blocking collectives, per_device(): lax.all_to_all(outgoing, ('row', 'col'), split_axis=0, concat_axis=0, til...  28.7 us
    pallas_call x5, Pallas kernels, hop_call(): pl.pallas_call(functools.partial(hop_kernel, spec), out_shape=out_shape,...  19.9 us
    ppermute x12, waiting for transfers between devices, swap(): return lax.ppermute(value, 'col', [(c, c ^ bit) for c in range(cols)])  13.3 us
    ppermute x12, starting transfers between devices, swap(): return lax.ppermute(value, 'col', [(c, c ^ bit) for c in range(cols)])  10.1 us
    ppermute x2, starting transfers between devices, per_device(): right = lax.ppermute(right, 'row', to_right)  7.93 us
    unnamed x20, local copies, waits for them, and re-layouts  7.52 us
    ppermute x1, waiting for transfers between devices, per_device(): right = lax.ppermute(block, 'row', to_right)  4.25 us
    ppermute x1, waiting for transfers between devices, per_device(): left = lax.ppermute(block, 'row', to_left)  3.82 us
  transfers between devices with their start and end apart: 18, of which 6 were waited for; matrix products, arithmetic and copies ran while one was open for 0% of the time, Pallas kernels for 16%

profile of v3, /device:TPU:5, one launch (start us, length us, event | category | flops | bytes accessed | tf_op | source)
XLA Modules:
  0.0 111.7 jit_solution(6066073368699624482)
XLA Ops:
  0.0 0.0 copy-start
  0.0 0.9 copy-done
  0.9 0.0 copy-start.1
  0.9 0.9 copy-done.1
  1.9 0.0 copy-start.2
  1.9 0.8 copy-done.2
  2.7 0.0 copy-start.3
  2.7 0.7 copy-done.3
  3.4 0.0 copy-start.5
  3.4 0.7 copy-done.5
  4.1 0.8 prep_sources.1
  4.9 0.7 collective-permute-start.1
  5.7 1.2 %collective-permute-start.2 = (f32[384,128]{1,0:T(8,128)S(1)}, f32[384,128]{1,0:T(8,128)S(1)}, u32[]{:S(2)}, u32[]{:S(2)}) collective-permute-start(f32[384,128]{1,0:T(8,128)S(1)} %get-tuple-element.23.refs_0_), channel_id=1, source_target_pairs={{0,2},{1,3},{2,0},{3,1},{4,6},{5,7},{6,4},{7,5},{8,10},{9,11},{10,... | collective-permute-start | bytes 589832 | tf_op jit(solution)/shard_map/ppermute | solution.py:461
  6.9 5.3 %collective-permute-done.2.refs_2_ = f32[384,128]{1,0:T(8,128)S(1)} collective-permute-done((f32[384,128]{1,0:T(8,128)S(1)}, f32[384,128]{1,0:T(8,128)S(1)}, u32[]{:S(2)}, u32[]{:S(2)}) %collective-permute-start.2) | collective-permute-done | bytes 196640 | tf_op jit(solution)/shard_map/ppermute | solution.py:461
  12.2 0.8 collective-permute-start.3
  13.7 0.1 pad_add_fusion.facts_ref
  13.7 0.0 copy-start.4
  13.7 0.7 copy-done.4
  14.4 0.0 copy-start.6
  14.4 0.7 copy-done.6
  15.1 0.7 copy-done.7
  15.8 0.7 copy-done.8
  16.5 0.7 copy-done.9
  17.2 1.9 %index_work.1 = (s32[5,128]{1,0:T(8,128)S(1)}, s32[3,128]{1,0:T(4,128)S(1)}) custom-call(s32[4]{0:T(128)S(1)} %pad_add_fusion.facts_ref, s32[1,512]{1,0:T(1,128)S(1)} %copy-done.7, s32[1,512]{1,0:T(1,128)S(1)} %copy-done.8, s32[8,256]{1,0:T(8,128)S(1)} %bitcast.23, s32[8,256]{1,0:T(8,128)S(1)} %bitcast.25, s32[1,256]{1,0:T(1,128)S(1)} %bitcast.26), custom_call_target="tpu_custom_call" | custom-call | tf_op jit(solution)/shard_map/index_work/pallas_call | solution.py:369
  19.1 0.1 collective-permute-start
  19.2 3.2 %collective-permute-start.5 = (f32[768,128]{1,0:T(8,128)S(1)}, f32[768,128]{1,0:T(8,128)S(1)}, u32[]{:S(2)}, u32[]{:S(2)}) collective-permute-start(f32[768,128]{1,0:T(8,128)S(1)} %get-tuple-element.24.refs_4_), channel_id=1, source_target_pairs={{0,4},{4,8},{8,12},{1,5},{5,9},{9,13},{2,6},{6,10},{10,14},{3,7},{... | collective-permute-start | bytes 1179656 | tf_op jit(solution)/shard_map/ppermute | solution.py:480
  22.4 1.3 %collective-permute-start.4 = (f32[768,128]{1,0:T(8,128)S(1)}, f32[768,128]{1,0:T(8,128)S(1)}, u32[]{:S(2)}, u32[]{:S(2)}) collective-permute-start(f32[768,128]{1,0:T(8,128)S(1)} %get-tuple-element.24.refs_4_), channel_id=1, source_target_pairs={{4,0},{8,4},{12,8},{5,1},{9,5},{13,9},{6,2},{10,6},{14,10},{7,3},{... | collective-permute-start | bytes 1179656 | tf_op jit(solution)/shard_map/ppermute | solution.py:481
  23.7 0.0 collective-permute-done.mate_list_ref
  23.7 0.0 collective-permute-done.1.refs_1_.refs_4_
  23.7 0.0 collective-permute-done.3.refs_3_
  23.7 2.4 %pairs_hop0.1 = (f32[4104,128]{1,0:T(8,128)S(1)}, f32[1536,128]{1,0:T(8,128)S(1)}) custom-call(s32[5,128]{1,0:T(8,128)S(1)} %get-tuple-element.22.list_ref, s32[5,128]{1,0:T(8,128)S(1)} %collective-permute-done.mate_list_ref, f32[384,128]{1,0:T(8,128)S(1)} %get-tuple-element.23.refs_0_, f32[768,128]{1,0:T(8,128)S(1)} %collective-permute-done.1.refs_1_.refs_4_, ...), custom_call_target="tpu_custom_call" | custom-call | flops 20000000000 | bytes 1000000 | tf_op jit(solution)/shard_map/pairs_hop0/pallas_call | solution.py:220
  26.1 4.2 %collective-permute-done.5.refs_2_ = f32[768,128]{1,0:T(8,128)S(1)} collective-permute-done((f32[768,128]{1,0:T(8,128)S(1)}, f32[768,128]{1,0:T(8,128)S(1)}, u32[]{:S(2)}, u32[]{:S(2)}) %collective-permute-start.5) | collective-permute-done | bytes 393248 | tf_op jit(solution)/shard_map/ppermute | solution.py:480
  30.4 3.8 %collective-permute-done.4.refs_3_ = f32[768,128]{1,0:T(8,128)S(1)} collective-permute-done((f32[768,128]{1,0:T(8,128)S(1)}, f32[768,128]{1,0:T(8,128)S(1)}, u32[]{:S(2)}, u32[]{:S(2)}) %collective-permute-start.4) | collective-permute-done | bytes 393248 | tf_op jit(solution)/shard_map/ppermute | solution.py:481
  34.2 3.2 %collective-permute-start.7 = (f32[768,128]{1,0:T(8,128)S(1)}, f32[768,128]{1,0:T(8,128)S(1)}, u32[]{:S(2)}, u32[]{:S(2)}) collective-permute-start(f32[768,128]{1,0:T(8,128)S(1)} %collective-permute-done.5.refs_2_), channel_id=1, source_target_pairs={{0,4},{4,8},{8,12},{1,5},{5,9},{9,13},{2,6},{6,10},{10,14},{3,7},{... | collective-permute-start | bytes 1179656 | tf_op jit(solution)/shard_map/ppermute | solution.py:504
  37.4 1.3 %collective-permute-start.6 = (f32[768,128]{1,0:T(8,128)S(1)}, f32[768,128]{1,0:T(8,128)S(1)}, u32[]{:S(2)}, u32[]{:S(2)}) collective-permute-start(f32[768,128]{1,0:T(8,128)S(1)} %collective-permute-done.4.refs_3_), channel_id=1, source_target_pairs={{4,0},{8,4},{12,8},{5,1},{9,5},{13,9},{6,2},{10,6},{14,10},{7,3},{... | collective-permute-start | bytes 1179656 | tf_op jit(solution)/shard_map/ppermute | solution.py:506
  38.7 2.0 %collective-permute-start.8 = (f32[768,128]{1,0:T(8,128)S(1)}, f32[768,128]{1,0:T(8,128)S(1)}, u32[]{:S(2)}, u32[]{:S(2)}) collective-permute-start(f32[768,128]{1,0:T(8,128)S(1)} %collective-permute-done.5.refs_2_), channel_id=1, source_target_pairs={{0,1},{1,0},{2,3},{3,2},{4,5},{5,4},{6,7},{7,6},{8,9},{9,8},{10,11... | collective-permute-start | bytes 1179656 | tf_op jit(solution)/shard_map/ppermute | solution.py:461
  40.7 0.1 collective-permute-start.9
  40.8 4.3 %pairs_hop1.1.refs_1_ = f32[4104,128]{1,0:T(8,128)S(1)} custom-call(s32[5,128]{1,0:T(8,128)S(1)} %get-tuple-element.22.list_ref, s32[5,128]{1,0:T(8,128)S(1)} %collective-permute-done.mate_list_ref, f32[1536,128]{1,0:T(8,128)S(1)} %get-tuple-element.25.refs_0_, f32[4104,128]{1,0:T(8,128)S(1)} %get-tuple-element.30.refs_1_, ...), custom_call_target="tpu_custom_call", output_to_operand_aliasing={{}: (3, {})} | custom-call | flops 20000000000 | bytes 1000000 | tf_op jit(solution)/shard_map/pairs_hop1/pallas_call | solution.py:220
  45.0 0.0 collective-permute-done.7.refs_2_
  45.0 2.9 %collective-permute-done.6.refs_3_ = f32[768,128]{1,0:T(8,128)S(1)} collective-permute-done((f32[768,128]{1,0:T(8,128)S(1)}, f32[768,128]{1,0:T(8,128)S(1)}, u32[]{:S(2)}, u32[]{:S(2)}) %collective-permute-start.6) | collective-permute-done | bytes 393248 | tf_op jit(solution)/shard_map/ppermute | solution.py:506
  48.0 1.3 %collective-permute-start.11 = (f32[768,128]{1,0:T(8,128)S(1)}, f32[768,128]{1,0:T(8,128)S(1)}, u32[]{:S(2)}, u32[]{:S(2)}) collective-permute-start(f32[768,128]{1,0:T(8,128)S(1)} %collective-permute-done.6.refs_3_), channel_id=1, source_target_pairs={{4,0},{8,4},{12,8},{5,1},{9,5},{13,9},{6,2},{10,6},{14,10},{7,3},{... | collective-permute-start | bytes 1179656 | tf_op jit(solution)/shard_map/ppermute | solution.py:506
  49.2 4.7 %collective-permute-start.10 = (f32[768,128]{1,0:T(8,128)S(1)}, f32[768,128]{1,0:T(8,128)S(1)}, u32[]{:S(2)}, u32[]{:S(2)}) collective-permute-start(f32[768,128]{1,0:T(8,128)S(1)} %collective-permute-done.7.refs_2_), channel_id=1, source_target_pairs={{0,4},{4,8},{8,12},{1,5},{5,9},{9,13},{2,6},{6,10},{10,14},{3,7},{... | collective-permute-start | bytes 1179656 | tf_op jit(solution)/shard_map/ppermute | solution.py:504
  54.0 2.8 %collective-permute-start.13 = (f32[768,128]{1,0:T(8,128)S(1)}, f32[768,128]{1,0:T(8,128)S(1)}, u32[]{:S(2)}, u32[]{:S(2)}) collective-permute-start(f32[768,128]{1,0:T(8,128)S(1)} %collective-permute-done.6.refs_3_), channel_id=1, source_target_pairs={{0,1},{1,0},{2,3},{3,2},{4,5},{5,4},{6,7},{7,6},{8,9},{9,8},{10,11... | collective-permute-start | bytes 1179656 | tf_op jit(solution)/shard_map/ppermute | solution.py:461
  56.7 0.0 collective-permute-done.8.refs_4_
  56.7 0.1 collective-permute-start.12
  56.8 0.0 collective-permute-done.9.refs_5_
  56.8 4.3 %pairs_hop2.1.refs_1_ = f32[4104,128]{1,0:T(8,128)S(1)} custom-call(s32[5,128]{1,0:T(8,128)S(1)} %get-tuple-element.22.list_ref, s32[5,128]{1,0:T(8,128)S(1)} %collective-permute-done.mate_list_ref, f32[1536,128]{1,0:T(8,128)S(1)} %get-tuple-element.25.refs_0_, f32[4104,128]{1,0:T(8,128)S(1)} %pairs_hop1.1.refs_1_, ...), custom_call_target="tpu_custom_call", output_to_operand_aliasing={{}: (3, {})} | custom-call | flops 20000000000 | bytes 1000000 | tf_op jit(solution)/shard_map/pairs_hop2/pallas_call | solution.py:220
  61.1 0.0 collective-permute-done.11.refs_3_
  61.1 1.2 %collective-permute-start.15 = (f32[768,128]{1,0:T(8,128)S(1)}, f32[768,128]{1,0:T(8,128)S(1)}, u32[]{:S(2)}, u32[]{:S(2)}) collective-permute-start(f32[768,128]{1,0:T(8,128)S(1)} %collective-permute-done.11.refs_3_), channel_id=1, source_target_pairs={{0,1},{1,0},{2,3},{3,2},{4,5},{5,4},{6,7},{7,6},{8,9},{9,8},{10,11... | collective-permute-start | bytes 1179656 | tf_op jit(solution)/shard_map/ppermute | solution.py:461
  62.3 0.0 collective-permute-done.10.refs_2_
  62.3 1.0 collective-permute-start.14
  63.3 0.0 collective-permute-done.13.refs_5_
  63.3 0.0 collective-permute-done.12.refs_4_
  63.3 5.0 %pairs_hop3.1.refs_1_ = f32[4104,128]{1,0:T(8,128)S(1)} custom-call(s32[5,128]{1,0:T(8,128)S(1)} %get-tuple-element.22.list_ref, s32[5,128]{1,0:T(8,128)S(1)} %collective-permute-done.mate_list_ref, f32[1536,128]{1,0:T(8,128)S(1)} %get-tuple-element.25.refs_0_, f32[4104,128]{1,0:T(8,128)S(1)} %pairs_hop2.1.refs_1_, ...), custom_call_target="tpu_custom_call", output_to_operand_aliasing={{}: (3, {})} | custom-call | flops 20000000000 | bytes 1000000 | tf_op jit(solution)/shard_map/pairs_hop3/pallas_call | solution.py:220
  68.3 0.0 collective-permute-done.15.refs_3_
  68.3 0.0 collective-permute-done.14.refs_2_
  68.3 4.0 %pairs_hop4.1 = (f32[4104,128]{1,0:T(8,128)S(1)}, f32[768,128]{1,0:T(8,128)S(1)}, f32[768,128]{1,0:T(8,128)S(1)}) custom-call(s32[5,128]{1,0:T(8,128)S(1)} %get-tuple-element.22.list_ref, s32[5,128]{1,0:T(8,128)S(1)} %collective-permute-done.mate_list_ref, f32[1536,128]{1,0:T(8,128)S(1)} %get-tuple-element.25.refs_0_, ...), custom_call_target="tpu_custom_call", output_to_operand_aliasing={{0}: (3, {})} | custom-call | flops 20000000000 | bytes 1000000 | tf_op jit(solution)/shard_map/pairs_hop4/pallas_call | solution.py:220
  72.2 0.1 collective-permute-start.16
  72.3 1.7 %collective-permute-done.16.refs_1_ = f32[768,128]{1,0:T(8,128)S(1)} collective-permute-done((f32[768,128]{1,0:T(8,128)S(1)}, f32[768,128]{1,0:T(8,128)S(1)}, u32[]{:S(2)}, u32[]{:S(2)}) %collective-permute-start.16) | collective-permute-done | bytes 393248 | tf_op jit(solution)/shard_map/ppermute | solution.py:461
  74.1 0.1 collective-permute-start.17
  74.1 6.3 %collective-permute-done.17.refs_2_ = f32[384,128]{1,0:T(8,128)S(1)} collective-permute-done((f32[384,128]{1,0:T(8,128)S(1)}, f32[384,128]{1,0:T(8,128)S(1)}, u32[]{:S(2)}, u32[]{:S(2)}) %collective-permute-start.17) | collective-permute-done | bytes 196640 | tf_op jit(solution)/shard_map/ppermute | solution.py:461
  80.5 0.7 pack_owners.1
  81.2 28.7 %all_to_all.11 = f32[16,48,128]{2,1,0:T(8,128)S(1)} all-to-all(f32[16,48,128]{2,1,0:T(8,128)S(1)} %bitcast.19), channel_id=1, replica_groups=mesh['groups'=2,'row'=4,'col'=4] {'row','col'}, dimensions={0} | all-to-all | bytes 786432 | tf_op jit(solution)/shard_map/all_to_all | solution.py:521
  109.9 1.8 %unpack_drops.1 = f32[384,128]{1,0:T(8,128)} custom-call(s32[3,128]{1,0:T(4,128)S(1)} %get-tuple-element.21.place_ref, f32[768,128]{1,0:T(8,128)S(1)} %bitcast.18), custom_call_target="tpu_custom_call" | custom-call | tf_op jit(solution)/shard_map/unpack_drops/pallas_call | solution.py:428
  (4 shorter events, 0.0 us)
Async XLA Ops:
  0.0 0.9 copy-start
  0.9 0.9 copy-start.1
  1.9 0.8 copy-start.2
  2.7 0.7 copy-start.3
  3.4 0.7 copy-start.5
  4.9 18.8 %collective-permute-start.1 = (f32[768,128]{1,0:T(8,128)S(1)}, f32[768,128]{1,0:T(8,128)S(1)}, u32[]{:S(2)}, u32[]{:S(2)}) collective-permute-start(f32[768,128]{1,0:T(8,128)S(1)} %get-tuple-element.24.refs_4_), channel_id=1, source_target_pairs={{0,1},{1,0},{2,3},{3,2},{4,5},{5,4},{6,7},{7,6},{8,9},{9,8},{10,11... | collective-permute-start | bytes 1179656 | tf_op jit(solution)/shard_map/ppermute | solution.py:461
  5.7 6.5 %collective-permute-start.2 = (f32[384,128]{1,0:T(8,128)S(1)}, f32[384,128]{1,0:T(8,128)S(1)}, u32[]{:S(2)}, u32[]{:S(2)}) collective-permute-start(f32[384,128]{1,0:T(8,128)S(1)} %get-tuple-element.23.refs_0_), channel_id=1, source_target_pairs={{0,2},{1,3},{2,0},{3,1},{4,6},{5,7},{6,4},{7,5},{8,10},{9,11},{10,... | collective-permute-start | bytes 589832 | tf_op jit(solution)/shard_map/ppermute | solution.py:461
  12.2 11.6 %collective-permute-start.3 = (f32[384,128]{1,0:T(8,128)S(1)}, f32[384,128]{1,0:T(8,128)S(1)}, u32[]{:S(2)}, u32[]{:S(2)}) collective-permute-start(f32[384,128]{1,0:T(8,128)S(1)} %collective-permute-done.2.refs_2_), channel_id=1, source_target_pairs={{0,1},{1,0},{2,3},{3,2},{4,5},{5,4},{6,7},{7,6},{8,9},{9,8},{10,11... | collective-permute-start | bytes 589832 | tf_op jit(solution)/shard_map/ppermute | solution.py:461
  13.7 0.7 copy-start.4
  14.4 0.7 copy-start.6
  15.1 0.7 copy-start.7
  15.8 0.7 copy-start.8
  16.5 0.7 copy-start.9
  19.1 4.6 %collective-permute-start = (s32[5,128]{1,0:T(8,128)S(1)}, s32[5,128]{1,0:T(8,128)S(1)}, u32[]{:S(2)}, u32[]{:S(2)}) collective-permute-start(s32[5,128]{1,0:T(8,128)S(1)} %get-tuple-element.22.list_ref), channel_id=1, source_target_pairs={{0,1},{1,0},{2,3},{3,2},{4,5},{5,4},{6,7},{7,6},{8,9},{9,8},{10,11... | collective-permute-start | bytes 7688 | tf_op jit(solution)/shard_map/ppermute | solution.py:461
  19.2 11.2 %collective-permute-start.5 = (f32[768,128]{1,0:T(8,128)S(1)}, f32[768,128]{1,0:T(8,128)S(1)}, u32[]{:S(2)}, u32[]{:S(2)}) collective-permute-start(f32[768,128]{1,0:T(8,128)S(1)} %get-tuple-element.24.refs_4_), channel_id=1, source_target_pairs={{0,4},{4,8},{8,12},{1,5},{5,9},{9,13},{2,6},{6,10},{10,14},{3,7},{... | collective-permute-start | bytes 1179656 | tf_op jit(solution)/shard_map/ppermute | solution.py:480
  22.4 11.8 %collective-permute-start.4 = (f32[768,128]{1,0:T(8,128)S(1)}, f32[768,128]{1,0:T(8,128)S(1)}, u32[]{:S(2)}, u32[]{:S(2)}) collective-permute-start(f32[768,128]{1,0:T(8,128)S(1)} %get-tuple-element.24.refs_4_), channel_id=1, source_target_pairs={{4,0},{8,4},{12,8},{5,1},{9,5},{13,9},{6,2},{10,6},{14,10},{7,3},{... | collective-permute-start | bytes 1179656 | tf_op jit(solution)/shard_map/ppermute | solution.py:481
  34.2 10.9 %collective-permute-start.7 = (f32[768,128]{1,0:T(8,128)S(1)}, f32[768,128]{1,0:T(8,128)S(1)}, u32[]{:S(2)}, u32[]{:S(2)}) collective-permute-start(f32[768,128]{1,0:T(8,128)S(1)} %collective-permute-done.5.refs_2_), channel_id=1, source_target_pairs={{0,4},{4,8},{8,12},{1,5},{5,9},{9,13},{2,6},{6,10},{10,14},{3,7},{... | collective-permute-start | bytes 1179656 | tf_op jit(solution)/shard_map/ppermute | solution.py:504
  37.4 10.6 %collective-permute-start.6 = (f32[768,128]{1,0:T(8,128)S(1)}, f32[768,128]{1,0:T(8,128)S(1)}, u32[]{:S(2)}, u32[]{:S(2)}) collective-permute-start(f32[768,128]{1,0:T(8,128)S(1)} %collective-permute-done.4.refs_3_), channel_id=1, source_target_pairs={{4,0},{8,4},{12,8},{5,1},{9,5},{13,9},{6,2},{10,6},{14,10},{7,3},{... | collective-permute-start | bytes 1179656 | tf_op jit(solution)/shard_map/ppermute | solution.py:506
  38.7 18.1 %collective-permute-start.8 = (f32[768,128]{1,0:T(8,128)S(1)}, f32[768,128]{1,0:T(8,128)S(1)}, u32[]{:S(2)}, u32[]{:S(2)}) collective-permute-start(f32[768,128]{1,0:T(8,128)S(1)} %collective-permute-done.5.refs_2_), channel_id=1, source_target_pairs={{0,1},{1,0},{2,3},{3,2},{4,5},{5,4},{6,7},{7,6},{8,9},{9,8},{10,11... | collective-permute-start | bytes 1179656 | tf_op jit(solution)/shard_map/ppermute | solution.py:461
  40.7 16.2 %collective-permute-start.9 = (f32[768,128]{1,0:T(8,128)S(1)}, f32[768,128]{1,0:T(8,128)S(1)}, u32[]{:S(2)}, u32[]{:S(2)}) collective-permute-start(f32[768,128]{1,0:T(8,128)S(1)} %collective-permute-done.4.refs_3_), channel_id=1, source_target_pairs={{0,1},{1,0},{2,3},{3,2},{4,5},{5,4},{6,7},{7,6},{8,9},{9,8},{10,11... | collective-permute-start | bytes 1179656 | tf_op jit(solution)/shard_map/ppermute | solution.py:461
  48.0 13.2 %collective-permute-start.11 = (f32[768,128]{1,0:T(8,128)S(1)}, f32[768,128]{1,0:T(8,128)S(1)}, u32[]{:S(2)}, u32[]{:S(2)}) collective-permute-start(f32[768,128]{1,0:T(8,128)S(1)} %collective-permute-done.6.refs_3_), channel_id=1, source_target_pairs={{4,0},{8,4},{12,8},{5,1},{9,5},{13,9},{6,2},{10,6},{14,10},{7,3},{... | collective-permute-start | bytes 1179656 | tf_op jit(solution)/shard_map/ppermute | solution.py:506
  49.2 13.1 %collective-permute-start.10 = (f32[768,128]{1,0:T(8,128)S(1)}, f32[768,128]{1,0:T(8,128)S(1)}, u32[]{:S(2)}, u32[]{:S(2)}) collective-permute-start(f32[768,128]{1,0:T(8,128)S(1)} %collective-permute-done.7.refs_2_), channel_id=1, source_target_pairs={{0,4},{4,8},{8,12},{1,5},{5,9},{9,13},{2,6},{6,10},{10,14},{3,7},{... | collective-permute-start | bytes 1179656 | tf_op jit(solution)/shard_map/ppermute | solution.py:504
  54.0 9.3 %collective-permute-start.13 = (f32[768,128]{1,0:T(8,128)S(1)}, f32[768,128]{1,0:T(8,128)S(1)}, u32[]{:S(2)}, u32[]{:S(2)}) collective-permute-start(f32[768,128]{1,0:T(8,128)S(1)} %collective-permute-done.6.refs_3_), channel_id=1, source_target_pairs={{0,1},{1,0},{2,3},{3,2},{4,5},{5,4},{6,7},{7,6},{8,9},{9,8},{10,11... | collective-permute-start | bytes 1179656 | tf_op jit(solution)/shard_map/ppermute | solution.py:461
  56.7 6.5 %collective-permute-start.12 = (f32[768,128]{1,0:T(8,128)S(1)}, f32[768,128]{1,0:T(8,128)S(1)}, u32[]{:S(2)}, u32[]{:S(2)}) collective-permute-start(f32[768,128]{1,0:T(8,128)S(1)} %collective-permute-done.7.refs_2_), channel_id=1, source_target_pairs={{0,1},{1,0},{2,3},{3,2},{4,5},{5,4},{6,7},{7,6},{8,9},{9,8},{10,11... | collective-permute-start | bytes 1179656 | tf_op jit(solution)/shard_map/ppermute | solution.py:461
  61.1 7.1 %collective-permute-start.15 = (f32[768,128]{1,0:T(8,128)S(1)}, f32[768,128]{1,0:T(8,128)S(1)}, u32[]{:S(2)}, u32[]{:S(2)}) collective-permute-start(f32[768,128]{1,0:T(8,128)S(1)} %collective-permute-done.11.refs_3_), channel_id=1, source_target_pairs={{0,1},{1,0},{2,3},{3,2},{4,5},{5,4},{6,7},{7,6},{8,9},{9,8},{10,11... | collective-permute-start | bytes 1179656 | tf_op jit(solution)/shard_map/ppermute | solution.py:461
  62.3 6.0 %collective-permute-start.14 = (f32[768,128]{1,0:T(8,128)S(1)}, f32[768,128]{1,0:T(8,128)S(1)}, u32[]{:S(2)}, u32[]{:S(2)}) collective-permute-start(f32[768,128]{1,0:T(8,128)S(1)} %collective-permute-done.10.refs_2_), channel_id=1, source_target_pairs={{0,1},{1,0},{2,3},{3,2},{4,5},{5,4},{6,7},{7,6},{8,9},{9,8},{10,11... | collective-permute-start | bytes 1179656 | tf_op jit(solution)/shard_map/ppermute | solution.py:461
  72.2 1.8 %collective-permute-start.16 = (f32[768,128]{1,0:T(8,128)S(1)}, f32[768,128]{1,0:T(8,128)S(1)}, u32[]{:S(2)}, u32[]{:S(2)}) collective-permute-start(f32[768,128]{1,0:T(8,128)S(1)} %get-tuple-element.36), channel_id=1, source_target_pairs={{0,1},{1,0},{2,3},{3,2},{4,5},{5,4},{6,7},{7,6},{8,9},{9,8},{10,11... | collective-permute-start | bytes 1179656 | tf_op jit(solution)/shard_map/ppermute | solution.py:461
  74.1 6.4 %collective-permute-start.17 = (f32[384,128]{1,0:T(8,128)S(1)}, f32[384,128]{1,0:T(8,128)S(1)}, u32[]{:S(2)}, u32[]{:S(2)}) collective-permute-start(f32[384,128]{1,0:T(8,128)S(1)} %slice_add_fusion), channel_id=1, source_target_pairs={{0,2},{1,3},{2,0},{3,1},{4,6},{5,7},{6,4},{7,5},{8,10},{9,11},{10,... | collective-permute-start | bytes 589832 | tf_op jit(solution)/shard_map/ppermute | solution.py:461

commit v4 on v3

--- a/solution.py
+++ b/solution.py
@@ -16,7 +16,8 @@
 force_scale = length_scale / (8.0 * math.pi)
 unroll = 8
 vmem_limit = 24 * 2**20
-kernel_flops = 2 * 10**10
+kernel_flops = 8 * 10**9
+whole_vmem = 60 * 2**20
 vmem = pl.BlockSpec(memory_space=pltpu.VMEM)
 smem = pl.BlockSpec(memory_space=pltpu.SMEM)
 hbm = pl.BlockSpec(memory_space=pltpu.HBM)
@@ -228,27 +229,23 @@
         ],
         input_output_aliases=aliases,
         compiler_params=pltpu.CompilerParams(vmem_limit_bytes=vmem_limit),
-        cost_estimate=pl.CostEstimate(flops=kernel_flops, bytes_accessed=10**6, transcendentals=10**6),
+        cost_estimate=pl.CostEstimate(flops=kernel_flops if hop else kernel_flops // 8, bytes_accessed=10**6, transcendentals=10**6),
         name=f"pairs_hop{hop}",
     )(*operands)
 
 
-def fetch_all(pairs, sems):
-    copies = [pltpu.make_async_copy(a, b, sems.at[k]) for k, (a, b) in enumerate(pairs)]
+def column(row, rows):
+    return jnp.broadcast_to(row, (rows, 128)).T
+
+
+def prep_kernel(n, base_ref, *refs):
+    ins, (out_ref, own_ref, small_ref), held, sems = refs[:8], refs[8:11], refs[11:19], refs[19]
+    copies = [pltpu.make_async_copy(a, b, sems.at[k]) for k, (a, b) in enumerate(zip(ins, held))]
     for copy in copies:
         copy.start()
     for copy in copies:
         copy.wait()
-
-
-def column(row, rows):
-    return jnp.broadcast_to(row, (rows, 128)).T
-
-
-def prep_kernel(n, base_ref, *refs):
-    ins, (out_ref, own_ref), held, sems = refs[:5], refs[5:7], refs[7:12], refs[12]
-    fetch_all(list(zip(ins, held)), sems)
-    position_ref, normal_ref, curvature_ref, cluster_ref, count_ref = held
+    position_ref, normal_ref, curvature_ref, cluster_ref, count_ref, owner_ref, target_ref, source_ref = held
     slots = position_ref.shape[1]
     scaled = position_ref[...] * length_scale
     out_ref[: 3 * n, :] = scaled
@@ -266,26 +263,33 @@
     strength = jnp.where(lane < live_count, curvature_ref[...] * force_scale, 0.0)
     for k in range(3):
         out_ref[n * (3 + k) : n * (4 + k), :] = normal_ref[n * k : n * (k + 1), :] * strength
+    per_drop, drops = cluster_ref.shape
+    pairs = target_ref.shape[1]
+    small_ref[:per_drop, :drops] = cluster_ref[...] + (count_ref[...] << 14)
+    small_ref[per_drop : per_drop + 1, :drops] = owner_ref[...]
+    small_ref[per_drop + 1 : per_drop + 2, :pairs] = target_ref[...]
+    small_ref[per_drop + 2 : per_drop + 3, :pairs] = source_ref[...]
 
 
 def prep_call(base, *operands):
     n, slots = operands[2].shape
+    per_drop, drops = operands[3].shape
+    small = (per_drop + 8, max(drops, operands[6].shape[1]))
+    shapes = [((6 * n, slots), f32), ((3 * n, slots), f32), (small, i32)]
     return pl.pallas_call(
         functools.partial(prep_kernel, n),
-        out_shape=[jax.ShapeDtypeStruct((6 * n, slots), f32), jax.ShapeDtypeStruct((3 * n, slots), f32)],
-        in_specs=[smem] + [hbm] * 5,
-        out_specs=[vmem, vmem],
-        scratch_shapes=[pltpu.VMEM(x.shape, x.dtype) for x in operands] + [pltpu.SemaphoreType.DMA((5,))],
-        compiler_params=pltpu.CompilerParams(vmem_limit_bytes=vmem_limit),
+        out_shape=[jax.ShapeDtypeStruct(*shape) for shape in shapes],
+        in_specs=[smem] + [hbm] * 8,
+        out_specs=[vmem] * 3,
+        scratch_shapes=[pltpu.VMEM(x.shape, x.dtype) for x in operands] + [pltpu.SemaphoreType.DMA((8,))],
+        compiler_params=pltpu.CompilerParams(vmem_limit_bytes=whole_vmem),
         name="prep_sources",
     )(base, *operands)
 
 
 def index_kernel(spec, facts_ref, *refs):
-    n, rows, cols, capacity, split = spec
-    ins, (list_ref, place_ref), held, sems = refs[:5], refs[5:7], refs[7:12], refs[12]
-    fetch_all(list(zip(ins, held)), sems)
-    target_ref, source_ref, cluster_ref, count_ref, owner_ref = held
+    n, rows, capacity, per_drop, drops, pair_slots, split = spec
+    small_ref, list_ref, place_ref = refs
     my_row, my_col, device, live_pairs = [facts_ref[k] for k in range(4)]
     shift = n.bit_length() - 1
     wide = (128, 128)
@@ -293,11 +297,11 @@
     sub = lax.broadcasted_iota(i32, wide, 0)
     lane = lax.broadcasted_iota(i32, wide, 1)
 
-    blocks = target_ref.shape[1] // 128
+    blocks = pair_slots // 128
     keys, packs = [], []
     for b in range(blocks):
-        target = target_ref[:, 128 * b : 128 * (b + 1)]
-        source = source_ref[:, 128 * b : 128 * (b + 1)]
+        target = small_ref[per_drop + 1 : per_drop + 2, 128 * b : 128 * (b + 1)]
+        source = small_ref[per_drop + 2 : per_drop + 3, 128 * b : 128 * (b + 1)]
         source_row = source >> shift
         index = lane_row + 128 * b
         key = jnp.where(index < live_pairs, jnp.abs(source_row - my_row), rows)
@@ -326,29 +330,27 @@
         below = below + jnp.where(key_columns[c] < lane * (128 * blocks), 1.0, 0.0)
     list_ref[blocks : blocks + 1, :] = jnp.sum(below, axis=0, keepdims=True).astype(i32)
 
-    per_drop = cluster_ref.shape[0]
     mine = device * n + sub
-    drop_blocks = owner_ref.shape[1] // 128
 
     def scan(j, carry):
         owner_sum, chosen, owned_before = carry
         part = pl.ds(pl.multiple_of(j * 128, 128), 128)
-        owner = owner_ref[:, part]
+        owner = small_ref[per_drop : per_drop + 1, part]
         is_mine = jnp.where(owner == device, 1.0, 0.0)
         mine_column = column(is_mine, 128)
         rank = jnp.sum(jnp.where(sub < lane, mine_column, 0.0), axis=0, keepdims=True) + owned_before
         slot = jnp.where(owner == device, rank, -1.0)
         picked = column(slot, 128) == (lane // per_drop).astype(f32)
         for k in range(per_drop):
-            cluster = cluster_ref[k : k + 1, part]
-            fact = (cluster + count_ref[k : k + 1, part] * 16384).astype(f32)
-            chosen = chosen + jnp.where(picked & (lane % per_drop == k), column(fact, 128), 0.0)
+            fact = small_ref[k : k + 1, part]
+            cluster = fact & 16383
+            chosen = chosen + jnp.where(picked & (lane % per_drop == k), column(fact.astype(f32), 128), 0.0)
             wide_owner = jnp.broadcast_to(owner.astype(f32), wide)
             owner_sum = owner_sum + jnp.where(jnp.broadcast_to(cluster, wide) == mine, wide_owner, 0.0)
         return owner_sum, chosen, owned_before + jnp.sum(is_mine, axis=1, keepdims=True)
 
     start = (jnp.zeros(wide, f32), jnp.zeros(wide, f32), jnp.zeros((1, 1), f32))
-    owner_sum, chosen, _ = lax.fori_loop(0, drop_blocks, scan, start)
+    owner_sum, chosen, _ = lax.fori_loop(0, drops // 128, scan, start)
     home_owner = jnp.broadcast_to(jnp.sum(owner_sum, axis=1, keepdims=True), wide)
     owner_lanes = home_owner.T
     rank = jnp.sum(jnp.where((home_owner == owner_lanes) & (sub < lane), 1.0, 0.0), axis=0, keepdims=True)
@@ -364,17 +366,15 @@
     place_ref[2:3, :] = fact >> 14
 
 
-def index_call(spec, facts, *operands):
-    blocks = operands[0].shape[1] // 128
+def index_call(spec, facts, small):
     return pl.pallas_call(
         functools.partial(index_kernel, spec),
-        out_shape=[jax.ShapeDtypeStruct((blocks + 1, 128), i32), jax.ShapeDtypeStruct((3, 128), i32)],
-        in_specs=[smem] + [hbm] * 5,
+        out_shape=[jax.ShapeDtypeStruct((spec[5] // 128 + 1, 128), i32), jax.ShapeDtypeStruct((3, 128), i32)],
+        in_specs=[smem, vmem],
         out_specs=[vmem, vmem],
-        scratch_shapes=[pltpu.VMEM(x.shape, x.dtype) for x in operands] + [pltpu.SemaphoreType.DMA((5,))],
         compiler_params=pltpu.CompilerParams(vmem_limit_bytes=vmem_limit),
         name="index_work",
-    )(facts, *operands)
+    )(facts, small)
 
 
 def pack_kernel(n, place_ref, *refs):
@@ -463,14 +463,16 @@
     def component_major(value):
         return jnp.transpose(value, (1, 0, 2)).reshape(3 * n, slots)
 
-    clusters, counts = drop_clusters.T, node_counts.T
-    block, position = prep_call(
+    block, position, small = prep_call(
         (device * n).reshape(1),
         component_major(positions),
         component_major(normals),
         curvature,
-        clusters,
-        counts,
+        drop_clusters.T,
+        node_counts.T,
+        drop_owner.reshape(1, -1),
+        pair_targets,
+        pair_sources,
     )
     mate_block = swap(block, 1)
     if hypercube:
@@ -485,13 +487,9 @@
         gathered = lax.all_gather(position, "col", axis=0, tiled=True)
         targets = [gathered[3 * n * h : 3 * n * (h + 1)] for h in range(cols)]
     listed, places = index_call(
-        (n, rows, cols, capacity, hypercube),
+        (n, rows, capacity, drop_clusters.shape[1], drop_clusters.shape[0], pair_targets.shape[1], hypercube),
         jnp.stack([my_row, my_col, device, pair_count[0]]),
-        pair_targets,
-        pair_sources,
-        clusters,
-        counts,
-        drop_owner.reshape(1, -1),
+        small,
     )
     lists = [listed, swap(listed, 1)]
 

time: 113 us -> 98.4 us (0.87)
  the two profiles are of different devices: /device:TPU:5 before, /device:TPU:0 now
where the time goes in v4:
time: 98.4 us; the launch traced here: 97.3 us
  starting transfers between devices  30.1 us (31%)
  Pallas kernels  23.5 us (24%)
  waiting for transfers between devices  20.9 us (21%)
  blocking collectives  19.2 us (20%)
  local copies, waits for them, and re-layouts  2.68 us (3%)
    all_to_all x1, blocking collectives, per_device(): lax.all_to_all(outgoing, ('row', 'col'), split_axis=0, concat_axis=0, til...  19.2 us
    pallas_call x5, Pallas kernels, hop_call(): pl.pallas_call(functools.partial(hop_kernel, spec), out_shape=out_shape,...  17.1 us
    ppermute x12, starting transfers between devices, swap(): return lax.ppermute(value, 'col', [(c, c ^ bit) for c in range(cols)])  14.7 us
    ppermute x12, waiting for transfers between devices, swap(): return lax.ppermute(value, 'col', [(c, c ^ bit) for c in range(cols)])  8.89 us
    ppermute x2, starting transfers between devices, per_device(): right = lax.ppermute(right, 'row', to_right)  8.04 us
    ppermute x2, waiting for transfers between devices, per_device(): left = lax.ppermute(left, 'row', to_left)  6.94 us
    ppermute x1, starting transfers between devices, per_device(): right = lax.ppermute(block, 'row', to_right)  3.49 us
    unnamed x6, local copies, waits for them, and re-layouts  2.68 us
  transfers between devices with their start and end apart: 18, of which 9 were waited for; matrix products, arithmetic and copies ran while one was open for 0% of the time, Pallas kernels for 15%

profile of v4, /device:TPU:0, one launch (start us, length us, event | category | flops | bytes accessed | tf_op | source)
XLA Modules:
  0.0 97.3 jit_solution(13110508822154603610)
XLA Ops:
  0.0 2.1 %prep_sources.1 = (f32[768,128]{1,0:T(8,128)}, f32[384,128]{1,0:T(8,128)}, s32[16,512]{1,0:T(8,128)}) custom-call(s32[1]{0:T(128)} %bitcast.3.base_ref, f32[384,128]{1,0:T(8,128)} %bitcast.20, f32[384,128]{1,0:T(8,128)} %bitcast.21, f32[128,128]{1,0:T(8,128)} %refs_2_.1, s32[8,256]{1,0:T(8,128)} %bitcast.22, s32[8,256]{1,0:T(8,128)} %bitcast.23, ...), custom_call_target="tpu_custom_call" | custom-call | tf_op jit(solution)/shard_map/prep_sources/pallas_call | solution.py:279
  2.1 0.5 collective-permute-start.1
  2.6 2.6 %collective-permute-start.2 = (f32[384,128]{1,0:T(8,128)}, f32[384,128]{1,0:T(8,128)S(1)}, u32[]{:S(2)}, u32[]{:S(2)}) collective-permute-start(f32[384,128]{1,0:T(8,128)} %get-tuple-element.25.refs_0_), channel_id=1, source_target_pairs={{0,2},{1,3},{2,0},{3,1},{4,6},{5,7},{6,4},{7,5},{8,10},{9,11},{10,... | collective-permute-start | bytes 589832 | tf_op jit(solution)/shard_map/ppermute | solution.py:461
  5.2 3.5 %collective-permute-start.5 = (f32[768,128]{1,0:T(8,128)}, f32[768,128]{1,0:T(8,128)S(1)}, u32[]{:S(2)}, u32[]{:S(2)}) collective-permute-start(f32[768,128]{1,0:T(8,128)} %get-tuple-element.26.refs_4_), channel_id=1, source_target_pairs={{0,4},{4,8},{8,12},{1,5},{5,9},{9,13},{2,6},{6,10},{10,14},{3,7},{... | collective-permute-start | bytes 1179656 | tf_op jit(solution)/shard_map/ppermute | solution.py:482
  8.7 1.3 %collective-permute-start.4 = (f32[768,128]{1,0:T(8,128)}, f32[768,128]{1,0:T(8,128)S(1)}, u32[]{:S(2)}, u32[]{:S(2)}) collective-permute-start(f32[768,128]{1,0:T(8,128)} %get-tuple-element.26.refs_4_), channel_id=1, source_target_pairs={{4,0},{8,4},{12,8},{5,1},{9,5},{13,9},{6,2},{10,6},{14,10},{7,3},{... | collective-permute-start | bytes 1179656 | tf_op jit(solution)/shard_map/ppermute | solution.py:483
  10.0 0.9 collective-permute-done.2.refs_2_
  10.9 0.0 collective-permute-start.3
  11.5 0.1 pad_add_fusion.facts_ref
  11.6 0.0 copy-start
  11.6 0.8 copy-done
  12.4 1.8 %index_work.1 = (s32[5,128]{1,0:T(8,128)S(1)}, s32[3,128]{1,0:T(4,128)S(1)}) custom-call(s32[4]{0:T(128)S(1)} %pad_add_fusion.facts_ref, s32[16,512]{1,0:T(8,128)S(1)} %copy-done), custom_call_target="tpu_custom_call" | custom-call | tf_op jit(solution)/shard_map/index_work/pallas_call | solution.py:370
  14.1 0.6 collective-permute-start
  14.7 0.8 collective-permute-done.mate_list_ref
  15.5 0.0 collective-permute-done.1.refs_1_.refs_4_
  15.5 0.0 collective-permute-done.3.refs_3_
  15.5 0.0 copy-start.1
  15.5 1.0 %copy-done.1 = f32[768,128]{1,0:T(8,128)S(1)} copy-done((f32[768,128]{1,0:T(8,128)S(1)}, f32[768,128]{1,0:T(8,128)}, u32[]{:S(2)}) %copy-start.1) | copy-done | bytes 393240
  16.5 0.0 copy-start.2
  16.5 0.9 copy-done.2
  17.5 1.7 %pairs_hop0.1 = (f32[4104,128]{1,0:T(8,128)S(1)}, f32[1536,128]{1,0:T(8,128)S(1)}) custom-call(s32[5,128]{1,0:T(8,128)S(1)} %get-tuple-element.24.list_ref, s32[5,128]{1,0:T(8,128)S(1)} %collective-permute-done.mate_list_ref, f32[384,128]{1,0:T(8,128)S(1)} %copy-done.2, f32[768,128]{1,0:T(8,128)S(1)} %collective-permute-done.1.refs_1_.refs_4_, ...), custom_call_target="tpu_custom_call" | custom-call | flops 1000000000 | bytes 1000000 | tf_op jit(solution)/shard_map/pairs_hop0/pallas_call | solution.py:221
  19.2 0.0 collective-permute-done.5.refs_2_
  19.2 2.5 %collective-permute-done.4.refs_3_ = f32[768,128]{1,0:T(8,128)S(1)} collective-permute-done((f32[768,128]{1,0:T(8,128)}, f32[768,128]{1,0:T(8,128)S(1)}, u32[]{:S(2)}, u32[]{:S(2)}) %collective-permute-start.4) | collective-permute-done | bytes 393248 | tf_op jit(solution)/shard_map/ppermute | solution.py:483
  21.7 3.5 %collective-permute-start.7 = (f32[768,128]{1,0:T(8,128)S(1)}, f32[768,128]{1,0:T(8,128)S(1)}, u32[]{:S(2)}, u32[]{:S(2)}) collective-permute-start(f32[768,128]{1,0:T(8,128)S(1)} %collective-permute-done.5.refs_2_), channel_id=1, source_target_pairs={{0,4},{4,8},{8,12},{1,5},{5,9},{9,13},{2,6},{6,10},{10,14},{3,7},{... | collective-permute-start | bytes 1179656 | tf_op jit(solution)/shard_map/ppermute | solution.py:502
  25.2 1.3 %collective-permute-start.6 = (f32[768,128]{1,0:T(8,128)S(1)}, f32[768,128]{1,0:T(8,128)S(1)}, u32[]{:S(2)}, u32[]{:S(2)}) collective-permute-start(f32[768,128]{1,0:T(8,128)S(1)} %collective-permute-done.4.refs_3_), channel_id=1, source_target_pairs={{4,0},{8,4},{12,8},{5,1},{9,5},{13,9},{6,2},{10,6},{14,10},{7,3},{... | collective-permute-start | bytes 1179656 | tf_op jit(solution)/shard_map/ppermute | solution.py:504
  26.5 0.1 collective-permute-start.8
  26.5 0.5 collective-permute-start.9
  27.0 4.3 %pairs_hop1.1.refs_1_ = f32[4104,128]{1,0:T(8,128)S(1)} custom-call(s32[5,128]{1,0:T(8,128)S(1)} %get-tuple-element.24.list_ref, s32[5,128]{1,0:T(8,128)S(1)} %collective-permute-done.mate_list_ref, f32[1536,128]{1,0:T(8,128)S(1)} %get-tuple-element.27.refs_0_, f32[4104,128]{1,0:T(8,128)S(1)} %get-tuple-element.32.refs_1_, ...), custom_call_target="tpu_custom_call", output_to_operand_aliasing={{}: (3, {})} | custom-call | flops 8000000000 | bytes 1000000 | tf_op jit(solution)/shard_map/pairs_hop1/pallas_call | solution.py:221
  31.3 1.4 %collective-permute-done.7.refs_2_ = f32[768,128]{1,0:T(8,128)S(1)} collective-permute-done((f32[768,128]{1,0:T(8,128)S(1)}, f32[768,128]{1,0:T(8,128)S(1)}, u32[]{:S(2)}, u32[]{:S(2)}) %collective-permute-start.7) | collective-permute-done | bytes 393248 | tf_op jit(solution)/shard_map/ppermute | solution.py:502
  32.7 5.1 %collective-permute-done.6.refs_3_ = f32[768,128]{1,0:T(8,128)S(1)} collective-permute-done((f32[768,128]{1,0:T(8,128)S(1)}, f32[768,128]{1,0:T(8,128)S(1)}, u32[]{:S(2)}, u32[]{:S(2)}) %collective-permute-start.6) | collective-permute-done | bytes 393248 | tf_op jit(solution)/shard_map/ppermute | solution.py:504
  37.8 1.3 %collective-permute-start.11 = (f32[768,128]{1,0:T(8,128)S(1)}, f32[768,128]{1,0:T(8,128)S(1)}, u32[]{:S(2)}, u32[]{:S(2)}) collective-permute-start(f32[768,128]{1,0:T(8,128)S(1)} %collective-permute-done.6.refs_3_), channel_id=1, source_target_pairs={{4,0},{8,4},{12,8},{5,1},{9,5},{13,9},{6,2},{10,6},{14,10},{7,3},{... | collective-permute-start | bytes 1179656 | tf_op jit(solution)/shard_map/ppermute | solution.py:504
  39.1 4.6 %collective-permute-start.10 = (f32[768,128]{1,0:T(8,128)S(1)}, f32[768,128]{1,0:T(8,128)S(1)}, u32[]{:S(2)}, u32[]{:S(2)}) collective-permute-start(f32[768,128]{1,0:T(8,128)S(1)} %collective-permute-done.7.refs_2_), channel_id=1, source_target_pairs={{0,4},{4,8},{8,12},{1,5},{5,9},{9,13},{2,6},{6,10},{10,14},{3,7},{... | collective-permute-start | bytes 1179656 | tf_op jit(solution)/shard_map/ppermute | solution.py:502
  43.6 0.1 collective-permute-start.13
  43.7 0.0 collective-permute-done.8.refs_4_
  43.7 0.5 collective-permute-start.12
  44.2 0.0 collective-permute-done.9.refs_5_
  44.2 3.6 %pairs_hop2.1.refs_1_ = f32[4104,128]{1,0:T(8,128)S(1)} custom-call(s32[5,128]{1,0:T(8,128)S(1)} %get-tuple-element.24.list_ref, s32[5,128]{1,0:T(8,128)S(1)} %collective-permute-done.mate_list_ref, f32[1536,128]{1,0:T(8,128)S(1)} %get-tuple-element.27.refs_0_, f32[4104,128]{1,0:T(8,128)S(1)} %pairs_hop1.1.refs_1_, ...), custom_call_target="tpu_custom_call", output_to_operand_aliasing={{}: (3, {})} | custom-call | flops 8000000000 | bytes 1000000 | tf_op jit(solution)/shard_map/pairs_hop2/pallas_call | solution.py:221
  47.8 1.8 %collective-permute-done.11.refs_3_ = f32[768,128]{1,0:T(8,128)S(1)} collective-permute-done((f32[768,128]{1,0:T(8,128)S(1)}, f32[768,128]{1,0:T(8,128)S(1)}, u32[]{:S(2)}, u32[]{:S(2)}) %collective-permute-start.11) | collective-permute-done | bytes 393248 | tf_op jit(solution)/shard_map/ppermute | solution.py:504
  49.7 0.0 collective-permute-start.15
  49.7 1.2 %collective-permute-done.10.refs_2_ = f32[768,128]{1,0:T(8,128)S(1)} collective-permute-done((f32[768,128]{1,0:T(8,128)S(1)}, f32[768,128]{1,0:T(8,128)S(1)}, u32[]{:S(2)}, u32[]{:S(2)}) %collective-permute-start.10) | collective-permute-done | bytes 393248 | tf_op jit(solution)/shard_map/ppermute | solution.py:502
  50.9 0.0 collective-permute-start.14
  50.9 0.0 collective-permute-done.13.refs_5_
  50.9 0.0 collective-permute-done.12.refs_4_
  50.9 3.6 %pairs_hop3.1.refs_1_ = f32[4104,128]{1,0:T(8,128)S(1)} custom-call(s32[5,128]{1,0:T(8,128)S(1)} %get-tuple-element.24.list_ref, s32[5,128]{1,0:T(8,128)S(1)} %collective-permute-done.mate_list_ref, f32[1536,128]{1,0:T(8,128)S(1)} %get-tuple-element.27.refs_0_, f32[4104,128]{1,0:T(8,128)S(1)} %pairs_hop2.1.refs_1_, ...), custom_call_target="tpu_custom_call", output_to_operand_aliasing={{}: (3, {})} | custom-call | flops 8000000000 | bytes 1000000 | tf_op jit(solution)/shard_map/pairs_hop3/pallas_call | solution.py:221
  54.5 0.0 collective-permute-done.15.refs_3_
  54.5 0.0 collective-permute-done.14.refs_2_
  54.5 4.0 %pairs_hop4.1 = (f32[4104,128]{1,0:T(8,128)S(1)}, f32[768,128]{1,0:T(8,128)S(1)}, f32[768,128]{1,0:T(8,128)S(1)}) custom-call(s32[5,128]{1,0:T(8,128)S(1)} %get-tuple-element.24.list_ref, s32[5,128]{1,0:T(8,128)S(1)} %collective-permute-done.mate_list_ref, f32[1536,128]{1,0:T(8,128)S(1)} %get-tuple-element.27.refs_0_, ...), custom_call_target="tpu_custom_call", output_to_operand_aliasing={{0}: (3, {})} | custom-call | flops 8000000000 | bytes 1000000 | tf_op jit(solution)/shard_map/pairs_hop4/pallas_call | solution.py:221
  58.5 0.1 collective-permute-start.16
  58.6 1.7 %collective-permute-done.16.refs_1_ = f32[768,128]{1,0:T(8,128)S(1)} collective-permute-done((f32[768,128]{1,0:T(8,128)S(1)}, f32[768,128]{1,0:T(8,128)S(1)}, u32[]{:S(2)}, u32[]{:S(2)}) %collective-permute-start.16) | collective-permute-done | bytes 393248 | tf_op jit(solution)/shard_map/ppermute | solution.py:461
  60.3 9.8 %collective-permute-start.17 = (f32[384,128]{1,0:T(8,128)S(1)}, f32[384,128]{1,0:T(8,128)S(1)}, u32[]{:S(2)}, u32[]{:S(2)}) collective-permute-start(f32[384,128]{1,0:T(8,128)S(1)} %slice_add_fusion), channel_id=1, source_target_pairs={{0,2},{1,3},{2,0},{3,1},{4,6},{5,7},{6,4},{7,5},{8,10},{9,11},{10,... | collective-permute-start | bytes 589832 | tf_op jit(solution)/shard_map/ppermute | solution.py:461
  70.1 5.4 %collective-permute-done.17.refs_2_ = f32[384,128]{1,0:T(8,128)S(1)} collective-permute-done((f32[384,128]{1,0:T(8,128)S(1)}, f32[384,128]{1,0:T(8,128)S(1)}, u32[]{:S(2)}, u32[]{:S(2)}) %collective-permute-start.17) | collective-permute-done | bytes 196640 | tf_op jit(solution)/shard_map/ppermute | solution.py:461
  75.5 0.7 pack_owners.1
  76.3 19.2 %all_to_all.11 = f32[16,48,128]{2,1,0:T(8,128)S(1)} all-to-all(f32[16,48,128]{2,1,0:T(8,128)S(1)} %bitcast.19), channel_id=1, replica_groups=mesh['groups'=2,'row'=4,'col'=4] {'row','col'}, dimensions={0} | all-to-all | bytes 786432 | tf_op jit(solution)/shard_map/all_to_all | solution.py:519
  95.5 1.8 %unpack_drops.1 = f32[384,128]{1,0:T(8,128)} custom-call(s32[3,128]{1,0:T(4,128)S(1)} %get-tuple-element.23.place_ref, f32[768,128]{1,0:T(8,128)S(1)} %bitcast.18), custom_call_target="tpu_custom_call" | custom-call | tf_op jit(solution)/shard_map/unpack_drops/pallas_call | solution.py:428
  (1 shorter events, 0.0 us)
Async XLA Ops:
  2.1 13.5 %collective-permute-start.1 = (f32[768,128]{1,0:T(8,128)}, f32[768,128]{1,0:T(8,128)S(1)}, u32[]{:S(2)}, u32[]{:S(2)}) collective-permute-start(f32[768,128]{1,0:T(8,128)} %get-tuple-element.26.refs_4_), channel_id=1, source_target_pairs={{0,1},{1,0},{2,3},{3,2},{4,5},{5,4},{6,7},{7,6},{8,9},{9,8},{10,11... | collective-permute-start | bytes 1179656 | tf_op jit(solution)/shard_map/ppermute | solution.py:461
  2.6 8.3 %collective-permute-start.2 = (f32[384,128]{1,0:T(8,128)}, f32[384,128]{1,0:T(8,128)S(1)}, u32[]{:S(2)}, u32[]{:S(2)}) collective-permute-start(f32[384,128]{1,0:T(8,128)} %get-tuple-element.25.refs_0_), channel_id=1, source_target_pairs={{0,2},{1,3},{2,0},{3,1},{4,6},{5,7},{6,4},{7,5},{8,10},{9,11},{10,... | collective-permute-start | bytes 589832 | tf_op jit(solution)/shard_map/ppermute | solution.py:461
  5.2 14.0 %collective-permute-start.5 = (f32[768,128]{1,0:T(8,128)}, f32[768,128]{1,0:T(8,128)S(1)}, u32[]{:S(2)}, u32[]{:S(2)}) collective-permute-start(f32[768,128]{1,0:T(8,128)} %get-tuple-element.26.refs_4_), channel_id=1, source_target_pairs={{0,4},{4,8},{8,12},{1,5},{5,9},{9,13},{2,6},{6,10},{10,14},{3,7},{... | collective-permute-start | bytes 1179656 | tf_op jit(solution)/shard_map/ppermute | solution.py:482
  8.7 13.0 %collective-permute-start.4 = (f32[768,128]{1,0:T(8,128)}, f32[768,128]{1,0:T(8,128)S(1)}, u32[]{:S(2)}, u32[]{:S(2)}) collective-permute-start(f32[768,128]{1,0:T(8,128)} %get-tuple-element.26.refs_4_), channel_id=1, source_target_pairs={{4,0},{8,4},{12,8},{5,1},{9,5},{13,9},{6,2},{10,6},{14,10},{7,3},{... | collective-permute-start | bytes 1179656 | tf_op jit(solution)/shard_map/ppermute | solution.py:483
  10.9 4.7 %collective-permute-start.3 = (f32[384,128]{1,0:T(8,128)S(1)}, f32[384,128]{1,0:T(8,128)S(1)}, u32[]{:S(2)}, u32[]{:S(2)}) collective-permute-start(f32[384,128]{1,0:T(8,128)S(1)} %collective-permute-done.2.refs_2_), channel_id=1, source_target_pairs={{0,1},{1,0},{2,3},{3,2},{4,5},{5,4},{6,7},{7,6},{8,9},{9,8},{10,11... | collective-permute-start | bytes 589832 | tf_op jit(solution)/shard_map/ppermute | solution.py:461
  11.6 0.8 copy-start
  14.1 1.4 %collective-permute-start = (s32[5,128]{1,0:T(8,128)S(1)}, s32[5,128]{1,0:T(8,128)S(1)}, u32[]{:S(2)}, u32[]{:S(2)}) collective-permute-start(s32[5,128]{1,0:T(8,128)S(1)} %get-tuple-element.24.list_ref), channel_id=1, source_target_pairs={{0,1},{1,0},{2,3},{3,2},{4,5},{5,4},{6,7},{7,6},{8,9},{9,8},{10,11... | collective-permute-start | bytes 7688 | tf_op jit(solution)/shard_map/ppermute | solution.py:461
  15.5 1.0 %copy-start.1 = (f32[768,128]{1,0:T(8,128)S(1)}, f32[768,128]{1,0:T(8,128)}, u32[]{:S(2)}) copy-start(f32[768,128]{1,0:T(8,128)} %get-tuple-element.26.refs_4_) | copy-start | bytes 1179652
  16.5 0.9 copy-start.2
  21.7 11.0 %collective-permute-start.7 = (f32[768,128]{1,0:T(8,128)S(1)}, f32[768,128]{1,0:T(8,128)S(1)}, u32[]{:S(2)}, u32[]{:S(2)}) collective-permute-start(f32[768,128]{1,0:T(8,128)S(1)} %collective-permute-done.5.refs_2_), channel_id=1, source_target_pairs={{0,4},{4,8},{8,12},{1,5},{5,9},{9,13},{2,6},{6,10},{10,14},{3,7},{... | collective-permute-start | bytes 1179656 | tf_op jit(solution)/shard_map/ppermute | solution.py:502
  25.2 12.6 %collective-permute-start.6 = (f32[768,128]{1,0:T(8,128)S(1)}, f32[768,128]{1,0:T(8,128)S(1)}, u32[]{:S(2)}, u32[]{:S(2)}) collective-permute-start(f32[768,128]{1,0:T(8,128)S(1)} %collective-permute-done.4.refs_3_), channel_id=1, source_target_pairs={{4,0},{8,4},{12,8},{5,1},{9,5},{13,9},{6,2},{10,6},{14,10},{7,3},{... | collective-permute-start | bytes 1179656 | tf_op jit(solution)/shard_map/ppermute | solution.py:504
  26.5 17.3 %collective-permute-start.8 = (f32[768,128]{1,0:T(8,128)S(1)}, f32[768,128]{1,0:T(8,128)S(1)}, u32[]{:S(2)}, u32[]{:S(2)}) collective-permute-start(f32[768,128]{1,0:T(8,128)S(1)} %collective-permute-done.5.refs_2_), channel_id=1, source_target_pairs={{0,1},{1,0},{2,3},{3,2},{4,5},{5,4},{6,7},{7,6},{8,9},{9,8},{10,11... | collective-permute-start | bytes 1179656 | tf_op jit(solution)/shard_map/ppermute | solution.py:461
  26.5 17.7 %collective-permute-start.9 = (f32[768,128]{1,0:T(8,128)S(1)}, f32[768,128]{1,0:T(8,128)S(1)}, u32[]{:S(2)}, u32[]{:S(2)}) collective-permute-start(f32[768,128]{1,0:T(8,128)S(1)} %collective-permute-done.4.refs_3_), channel_id=1, source_target_pairs={{0,1},{1,0},{2,3},{3,2},{4,5},{5,4},{6,7},{7,6},{8,9},{9,8},{10,11... | collective-permute-start | bytes 1179656 | tf_op jit(solution)/shard_map/ppermute | solution.py:461
  37.8 11.9 %collective-permute-start.11 = (f32[768,128]{1,0:T(8,128)S(1)}, f32[768,128]{1,0:T(8,128)S(1)}, u32[]{:S(2)}, u32[]{:S(2)}) collective-permute-start(f32[768,128]{1,0:T(8,128)S(1)} %collective-permute-done.6.refs_3_), channel_id=1, source_target_pairs={{4,0},{8,4},{12,8},{5,1},{9,5},{13,9},{6,2},{10,6},{14,10},{7,3},{... | collective-permute-start | bytes 1179656 | tf_op jit(solution)/shard_map/ppermute | solution.py:504
  39.1 11.8 %collective-permute-start.10 = (f32[768,128]{1,0:T(8,128)S(1)}, f32[768,128]{1,0:T(8,128)S(1)}, u32[]{:S(2)}, u32[]{:S(2)}) collective-permute-start(f32[768,128]{1,0:T(8,128)S(1)} %collective-permute-done.7.refs_2_), channel_id=1, source_target_pairs={{0,4},{4,8},{8,12},{1,5},{5,9},{9,13},{2,6},{6,10},{10,14},{3,7},{... | collective-permute-start | bytes 1179656 | tf_op jit(solution)/shard_map/ppermute | solution.py:502
  43.6 7.2 %collective-permute-start.13 = (f32[768,128]{1,0:T(8,128)S(1)}, f32[768,128]{1,0:T(8,128)S(1)}, u32[]{:S(2)}, u32[]{:S(2)}) collective-permute-start(f32[768,128]{1,0:T(8,128)S(1)} %collective-permute-done.6.refs_3_), channel_id=1, source_target_pairs={{0,1},{1,0},{2,3},{3,2},{4,5},{5,4},{6,7},{7,6},{8,9},{9,8},{10,11... | collective-permute-start | bytes 1179656 | tf_op jit(solution)/shard_map/ppermute | solution.py:461
  43.7 7.1 %collective-permute-start.12 = (f32[768,128]{1,0:T(8,128)S(1)}, f32[768,128]{1,0:T(8,128)S(1)}, u32[]{:S(2)}, u32[]{:S(2)}) collective-permute-start(f32[768,128]{1,0:T(8,128)S(1)} %collective-permute-done.7.refs_2_), channel_id=1, source_target_pairs={{0,1},{1,0},{2,3},{3,2},{4,5},{5,4},{6,7},{7,6},{8,9},{9,8},{10,11... | collective-permute-start | bytes 1179656 | tf_op jit(solution)/shard_map/ppermute | solution.py:461
  49.7 4.8 %collective-permute-start.15 = (f32[768,128]{1,0:T(8,128)S(1)}, f32[768,128]{1,0:T(8,128)S(1)}, u32[]{:S(2)}, u32[]{:S(2)}) collective-permute-start(f32[768,128]{1,0:T(8,128)S(1)} %collective-permute-done.11.refs_3_), channel_id=1, source_target_pairs={{0,1},{1,0},{2,3},{3,2},{4,5},{5,4},{6,7},{7,6},{8,9},{9,8},{10,11... | collective-permute-start | bytes 1179656 | tf_op jit(solution)/shard_map/ppermute | solution.py:461
  50.9 3.6 %collective-permute-start.14 = (f32[768,128]{1,0:T(8,128)S(1)}, f32[768,128]{1,0:T(8,128)S(1)}, u32[]{:S(2)}, u32[]{:S(2)}) collective-permute-start(f32[768,128]{1,0:T(8,128)S(1)} %collective-permute-done.10.refs_2_), channel_id=1, source_target_pairs={{0,1},{1,0},{2,3},{3,2},{4,5},{5,4},{6,7},{7,6},{8,9},{9,8},{10,11... | collective-permute-start | bytes 1179656 | tf_op jit(solution)/shard_map/ppermute | solution.py:461
  58.5 1.8 %collective-permute-start.16 = (f32[768,128]{1,0:T(8,128)S(1)}, f32[768,128]{1,0:T(8,128)S(1)}, u32[]{:S(2)}, u32[]{:S(2)}) collective-permute-start(f32[768,128]{1,0:T(8,128)S(1)} %get-tuple-element.38), channel_id=1, source_target_pairs={{0,1},{1,0},{2,3},{3,2},{4,5},{5,4},{6,7},{7,6},{8,9},{9,8},{10,11... | collective-permute-start | bytes 1179656 | tf_op jit(solution)/shard_map/ppermute | solution.py:461
  60.3 15.2 %collective-permute-start.17 = (f32[384,128]{1,0:T(8,128)S(1)}, f32[384,128]{1,0:T(8,128)S(1)}, u32[]{:S(2)}, u32[]{:S(2)}) collective-permute-start(f32[384,128]{1,0:T(8,128)S(1)} %slice_add_fusion), channel_id=1, source_target_pairs={{0,2},{1,3},{2,0},{3,1},{4,6},{5,7},{6,4},{7,5},{8,10},{9,11},{10,... | collective-permute-start | bytes 589832 | tf_op jit(solution)/shard_map/ppermute | solution.py:461
